TPU v7x, 512 devices: a whole 4x8x8 slice. The times are simulated.
512 devices in a mesh: ev: 128 (over z, y, core), st: 4 (over x).
Axes of the slice: x: 4, y: 8, z: 8, core: 2. Of those that a mesh axis runs over, the one named last changes fastest.
Arguments:
- traces: float32 [12, 3, 1024, 1024], P('st', None, 'ev'), may hold values from -6 to 6
- ray_slowness: float32 [3, 12, 1024], P(None, 'st', 'ev'), may hold values from -5 to 5
- travel_time: float32 [12, 1024], P('st', 'ev'), may hold values from -6 to 6
- pair_first: int32 [16384], P('ev'), may hold values from 0 to 1023, as said below
- pair_second: int32 [16384], P('ev'), may hold values from 0 to 1023, as said below
- pair_lag: int32 [12, 16384], P('st', 'ev'), may hold values from -240 to 240
- pair_live: int32 [128], P('ev'), may hold values from 1 to 128, 8192 in all
Outputs:
- refined_shift: float32 [12, 16384], P('st', 'ev')
- location: float32 [4, 1024], P(None, 'ev')
Inputs may be any that keep to these rules, and one draw needn't show every extreme that they name: pair_first[p] is an event held by the same index of ev as pair slot p. pair_second[p] is an event held by the index of ev of pair slot p or by one of the two indices beside it. `pair_live`: slots at or past an index's count hold padding; some index of ev is full.
All inputs are finite; a program needn't handle non-finite values. No bound on the sum of `pair_live` on one device may be relied on, other than what follows from the above.
Results may differ from a plain program's by a relative error of at most 0.0003.
Values sent between devices are 32-bit elements; how exact they have to be, the bound alone decides.
No kernel may reach another device: no remote copies, remote signals or barrier semaphores. Data moves between devices by JAX's collectives and lax.ppermute only.
A program may use at most 192 MiB of HBM per device.

v0:
```python
import math

import jax
import jax.numpy as jnp
from jax import lax
from jax.sharding import PartitionSpec as P

LAGS = 32
PBLOCK = 128
ITERS = 2


eps_small = 1e-06
sample_step = 0.01
exact_mode = lax.Precision.HIGHEST


def passed_along(block, axis, distance):
    devices = range(lax.axis_size(axis))
    route = [(i - distance, i) for i in devices if i - distance in devices]
    return lax.ppermute(block, axis, route)


def dft_rows(length):
    half_len = length // 2
    row_ids = jnp.arange(length, dtype=jnp.int32)[:, None]
    freq_cos = jnp.arange(half_len + 1, dtype=jnp.int32)[None, :]
    freq_sin = jnp.arange(1, half_len, dtype=jnp.int32)[None, :]
    angle_cos = 2.0 * math.pi / length * (row_ids * freq_cos % length).astype(jnp.float32)
    angle_sin = 2.0 * math.pi / length * (row_ids * freq_sin % length).astype(jnp.float32)
    return jnp.concatenate([jnp.cos(angle_cos), jnp.sin(angle_sin)], axis=1)


def lag_rows(length, lag_count):
    half_len = length // 2
    shifts = jnp.arange(lag_count, dtype=jnp.int32)[None, :] - lag_count // 2
    freq_cos = jnp.arange(half_len + 1, dtype=jnp.int32)[:, None]
    freq_sin = jnp.arange(1, half_len, dtype=jnp.int32)[:, None]
    angle_cos = 2.0 * math.pi / length * (freq_cos * shifts % length).astype(jnp.float32)
    angle_sin = 2.0 * math.pi / length * (freq_sin * shifts % length).astype(jnp.float32)
    weight_cos = jnp.where((freq_cos == 0) | (freq_cos == half_len), 1.0 / length, 2.0 / length)
    return jnp.concatenate(
        [weight_cos * jnp.cos(angle_cos), -(2.0 / length) * jnp.sin(angle_sin)], axis=0
    )


def block_shifts(first_rows, second_rows, first_power, second_power, lag_block, lag_table):
    length = first_rows.shape[-1]
    half_len = length // 2
    cos_first = first_rows[..., : half_len + 1]
    sin_first = first_rows[..., half_len + 1 :]
    cos_second = second_rows[..., : half_len + 1]
    sin_second = second_rows[..., half_len + 1 :]
    zero_col = jnp.zeros(first_rows.shape[:-1] + (1,), jnp.float32)
    sin_first_pad = jnp.concatenate([zero_col, sin_first, zero_col], axis=-1)
    sin_second_pad = jnp.concatenate([zero_col, sin_second, zero_col], axis=-1)
    real_part = cos_first * cos_second + sin_first_pad * sin_second_pad
    imag_part = sin_first * cos_second[..., 1:half_len] - cos_first[..., 1:half_len] * sin_second
    frequencies = jnp.arange(half_len + 1, dtype=jnp.int32)
    phase_angle = (
        2.0
        * math.pi
        / length
        * (lag_block[:, None, :, None] * frequencies % length).astype(jnp.float32)
    )
    cos_lag = jnp.cos(phase_angle)
    sin_lag = jnp.sin(phase_angle)
    imag_pad = jnp.concatenate([zero_col, imag_part, zero_col], axis=-1)
    real_rot = real_part * cos_lag - imag_pad * sin_lag
    imag_rot = (
        real_part[..., 1:half_len] * sin_lag[..., 1:half_len] + imag_part * cos_lag[..., 1:half_len]
    )
    rotated = jnp.concatenate([real_rot, imag_rot], axis=-1)
    xcorr = jnp.einsum("gcbf,fk->gcbk", rotated, lag_table, precision=exact_mode)
    energy_scale = (first_power + eps_small) * (second_power + eps_small)
    energy = jnp.sum(xcorr * xcorr / energy_scale[..., None], axis=1)
    centred = (jnp.arange(lag_table.shape[1], dtype=jnp.int32) - lag_table.shape[1] // 2).astype(
        jnp.float32
    )
    return jnp.sum(energy * centred, axis=-1) / (jnp.sum(energy, axis=-1) + eps_small)


def slot_shifts(
    first_spec,
    first_power,
    second_spec,
    second_power,
    first_ids,
    second_ids,
    lags,
    weights,
    count,
    lag_table,
):
    groups, pair_dev = lags.shape

    def one_block(block_index, shift_out):
        first_rows = jnp.take(first_spec, first_ids, axis=2)
        second_rows = jnp.take(second_spec, second_ids, axis=2)
        first_block_power = jnp.take(first_power, first_ids, axis=2)
        second_block_power = jnp.take(second_power, second_ids, axis=2)
        shift_values = block_shifts(
            first_rows, second_rows, first_block_power, second_block_power, lags, lag_table
        )
        return shift_values * weights

    block_count = (count + PBLOCK - 1) // PBLOCK
    return lax.fori_loop(0, block_count, one_block, jnp.zeros((groups, pair_dev), jnp.float32))


def data_norm(values):
    return jnp.sqrt(lax.psum(jnp.sum(values * values), ("ev", "st")) + eps_small)


def body(traces, ray_slowness, travel_time, pair_first, pair_second, pair_lag, pair_live):
    groups, components, ev_dev, length = traces.shape
    pair_dev = pair_first.shape[0]
    quarter = length // 4
    first_event = lax.axis_index("ev") * ev_dev
    full_table = dft_rows(length)
    window_table = full_table[quarter : 3 * quarter]
    window = traces[..., quarter : 3 * quarter]
    first_spec = jnp.einsum("gcet,tf->gcef", window, window_table, precision=exact_mode)
    first_power = jnp.sum(window * window, axis=-1)
    first_local = pair_first - first_event
    second_local = pair_second - first_event + ev_dev
    live_count = pair_live[0]
    live_rows = (jnp.arange(pair_dev, dtype=jnp.int32) < live_count).astype(jnp.float32)
    lag_table = lag_rows(length, LAGS)
    pieces = []
    for stride in (1, -1):
        pieces.append(passed_along((traces, ray_slowness, travel_time), "ev", stride))
    near_traces = jnp.concatenate([pieces[0][0], traces, pieces[1][0]], axis=2)
    second_spec = jnp.einsum("gcet,tf->gcef", near_traces, full_table, precision=exact_mode)
    second_power = jnp.sum(near_traces * near_traces, axis=-1)
    near_slowness = jnp.concatenate([pieces[0][1], ray_slowness, pieces[1][1]], axis=2)
    near_time = jnp.concatenate([pieces[0][2], travel_time, pieces[1][2]], axis=1)
    refined_shift = slot_shifts(
        first_spec,
        first_power,
        second_spec,
        second_power,
        first_local,
        second_local,
        pair_lag,
        live_rows,
        live_count,
        lag_table,
    )
    first_hot = (first_local[:, None] == jnp.arange(ev_dev, dtype=jnp.int32)[None, :]).astype(
        jnp.float32
    )
    second_hot = (second_local[:, None] == jnp.arange(3 * ev_dev, dtype=jnp.int32)[None, :]).astype(
        jnp.float32
    )
    deriv_own = jnp.concatenate([ray_slowness, jnp.ones((1, groups, ev_dev), jnp.float32)], axis=0)
    deriv_near = jnp.concatenate(
        [near_slowness, jnp.ones((1, groups, 3 * ev_dev), jnp.float32)], axis=0
    )
    deriv_first = jnp.einsum("qge,pe->qgp", deriv_own, first_hot, precision=exact_mode)
    deriv_second = jnp.einsum("qge,pe->qgp", deriv_near, second_hot, precision=exact_mode)
    time_first = jnp.einsum("ge,pe->gp", travel_time, first_hot, precision=exact_mode)
    time_second = jnp.einsum("ge,pe->gp", near_time, second_hot, precision=exact_mode)
    rhs = live_rows * (
        sample_step * (pair_lag.astype(jnp.float32) + refined_shift) - time_first + time_second
    )

    def adjoint(data_vec):
        first_terms = jnp.sum(deriv_first * data_vec[None], axis=1)
        second_terms = jnp.sum(deriv_second * data_vec[None], axis=1)
        own_terms = jnp.einsum("qp,pe->qe", first_terms, first_hot, precision=exact_mode)
        near_terms = jnp.einsum("qp,pe->qe", second_terms, second_hot, precision=exact_mode)
        total_sum = own_terms - near_terms[:, ev_dev : 2 * ev_dev]
        for stride, lower in ((-1, 0), (1, 2 * ev_dev)):
            total_sum = total_sum - passed_along(
                near_terms[:, lower : lower + ev_dev], "ev", stride
            )
        return total_sum

    def project_back(resid_data):
        scale_norm = data_norm(resid_data)
        unit_data = resid_data / scale_norm
        return (adjoint(unit_data), unit_data, scale_norm)

    def model_update(partial_value, model_vec, beta_norm):
        whole = lax.psum(partial_value, "st")
        vector = whole - beta_norm * model_vec
        alpha_norm = jnp.sqrt(lax.psum(jnp.sum(vector * vector), "ev") + eps_small)
        return (vector / alpha_norm, alpha_norm)

    zero_model = jnp.zeros((4, ev_dev), jnp.float32)
    partial_value, unit_data, beta_norm = project_back(rhs)
    model_dir, alpha_norm = model_update(partial_value, zero_model, beta_norm)
    search_dir = model_dir
    location = zero_model
    phi_bar = beta_norm
    rho_bar = alpha_norm
    for turn in range(ITERS):
        near_parts = [model_dir, model_dir, model_dir]
        for forward_stride, place in ((1, 0), (-1, 2)):
            near_parts[place] = passed_along(model_dir, "ev", forward_stride)
        model_near = jnp.concatenate(near_parts, axis=1)
        at_first = jnp.einsum("qe,pe->qp", model_dir, first_hot, precision=exact_mode)
        at_second = jnp.einsum("qe,pe->qp", model_near, second_hot, precision=exact_mode)
        terms = deriv_first * at_first[:, None, :] - deriv_second * at_second[:, None, :]
        resid_data = live_rows * jnp.sum(terms, axis=0) - alpha_norm * unit_data
        final_turn = turn == ITERS - 1
        if final_turn:
            beta_norm = data_norm(resid_data)
        else:
            partial_value, unit_data, beta_norm = project_back(resid_data)
        rho_value = jnp.sqrt(rho_bar * rho_bar + beta_norm * beta_norm)
        cosine = rho_bar / rho_value
        sine_term = beta_norm / rho_value
        phi_value = cosine * phi_bar
        phi_bar = sine_term * phi_bar
        location = location + phi_value / rho_value * search_dir
        if not final_turn:
            next_dir, alpha_norm = model_update(partial_value, model_dir, beta_norm)
            theta_value = sine_term * alpha_norm
            rho_bar = -cosine * alpha_norm
            search_dir = next_dir - theta_value / rho_value * search_dir
            model_dir = next_dir
    return (refined_shift, location)


def solution(mesh):
    in_specs = (
        P("st", None, "ev", None),
        P(None, "st", "ev"),
        P("st", "ev"),
        P("ev"),
        P("ev"),
        P("st", "ev"),
        P("ev"),
    )
    out_specs = (P("st", "ev"), P(None, "ev"))
    return jax.shard_map(body, mesh=mesh, in_specs=in_specs, out_specs=out_specs, check_vma=False)
```

profile of v0, /device:TPU:1, one launch (start us, length us, event | category | flops | bytes accessed | tf_op | source)
XLA Modules:
  0.0 981.3 jit_solution(15623740784472262165)
XLA Ops:
  0.6 4.6 collective-permute-start
  5.2 6.2 collective-permute-start.1
  14.1 3.6 collective-permute-start.4
  21.4 9.4 fusion.19
  30.8 5.4 fusion.64
  39.0 7.6 fusion.28
  52.1 19.4 %gather_fusion = f32[128,3,3,1024]{3,2,1,0:T(4,128)} fusion(f32[3,3,8,1024]{3,1,2,0:T(4,128)S(1)} %copy.22, s32[1024]{0:T(1024)S(1)} %get-tuple-element.269), kind=kCustom, calls=%fused_computation | custom fusion | bytes 9437696 | tf_op jit(solution)/shard_map/while/body/jit(_take)/gather | solution.py:98
  71.6 5.1 sine_bitcast_fusion
  76.7 8.0 fusion.8
  84.7 3.8 collective-permute-start.2
  90.9 3.5 fusion.10
  97.3 6.6 gather_fusion.1
  103.9 5.9 fusion.7
  116.2 4.3 fusion.140
  124.8 103.9 %psum.49 = f32[]{:T(128)} all-reduce(f32[]{:T(128)} %get-tuple-element.265), channel_id=1, replica_groups=mesh['ev'=128,'st'=4] {'ev','st'}, use_global_device_ids=true, to_apply=%region_8.9 | all-reduce | flops 1 | bytes 8 | tf_op jit(solution)/shard_map/psum | solution.py:112
  236.7 6.7 psum.50
  244.0 247.2 %psum.51 = f32[]{:T(128)} all-reduce(f32[]{:T(128)} %multiply_reduce_fusion.10), channel_id=1, replica_groups=mesh['ev'=128,'st'=4] {'ev'}, use_global_device_ids=true, to_apply=%region_13.14 | all-reduce | flops 1 | bytes 8 | tf_op jit(solution)/shard_map/psum | solution.py:188
  491.9 3.0 collective-permute-start.9
  499.0 104.4 %psum.52 = f32[]{:T(128)} all-reduce(f32[]{:T(128)} %multiply_reduce_fusion.9), channel_id=1, replica_groups=mesh['ev'=128,'st'=4] {'ev','st'}, use_global_device_ids=true, to_apply=%region_16.17 | all-reduce | flops 1 | bytes 8 | tf_op jit(solution)/shard_map/psum | solution.py:112
  604.5 3.9 collective-permute-start.11
  610.4 3.0 collective-permute-done.10
  613.4 7.8 psum.53
  621.8 247.0 %psum.54 = f32[]{:T(128)} all-reduce(f32[]{:T(128)} %multiply_reduce_fusion.8), channel_id=1, replica_groups=mesh['ev'=128,'st'=4] {'ev'}, use_global_device_ids=true, to_apply=%region_21.22 | all-reduce | flops 1 | bytes 8 | tf_op jit(solution)/shard_map/psum | solution.py:188
  876.6 102.9 %psum.55 = f32[]{:T(128)} all-reduce(f32[]{:T(128)} %multiply_reduce_fusion.7), channel_id=1, replica_groups=mesh['ev'=128,'st'=4] {'ev','st'}, use_global_device_ids=true, to_apply=%region_24.25 | all-reduce | flops 1 | bytes 8 | tf_op jit(solution)/shard_map/psum | solution.py:112
  (121 shorter events, 53.4 us)
Async XLA Ops:
  0.6 30.2 %copy-start.9 = (s32[3,128]{1,0:T(4,128)S(1)}, s32[3,128]{1,0:T(4,128)}, u32[]{:S(2)}) copy-start(s32[3,128]{1,0:T(4,128)} %param.14) | copy-start | bytes 4612
  0.6 88.0 %collective-permute-start = (f32[3,3,8,1024]{3,2,1,0:T(8,128)}, f32[3,3,8,1024]{3,2,1,0:T(8,128)}, u32[]{:S(2)}, u32[]{:S(2)}) collective-permute-start(f32[3,3,8,1024]{3,2,1,0:T(8,128)} %param.9), channel_id=1, source_target_pairs={{0,4},{4,8},{8,12},{12,16},{16,20},{20,24},{24,28},{28,32},{32,36}... | collective-permute-start | bytes 884744 | tf_op jit(solution)/shard_map/ppermute | solution.py:21
  5.2 84.5 %collective-permute-start.1 = (f32[3,3,8,1024]{3,2,1,0:T(8,128)}, f32[3,3,8,1024]{3,2,1,0:T(8,128)}, u32[]{:S(2)}, u32[]{:S(2)}) collective-permute-start(f32[3,3,8,1024]{3,2,1,0:T(8,128)} %param.9), channel_id=1, source_target_pairs={{4,0},{8,4},{12,8},{16,12},{20,16},{24,20},{28,24},{32,28},{36,32}... | collective-permute-start | bytes 884744 | tf_op jit(solution)/shard_map/ppermute | solution.py:21
  12.1 72.5 %collective-permute-start.5 = (f32[3,3,8]{2,0,1:T(4,128)S(1)}, f32[3,3,8]{2,0,1:T(4,128)S(1)}, u32[]{:S(2)}, u32[]{:S(2)}) collective-permute-start(f32[3,3,8]{2,0,1:T(4,128)S(1)} %copy.29), channel_id=1, source_target_pairs={{4,0},{8,4},{12,8},{16,12},{20,16},{24,20},{28,24},{32,28},{36,32}... | collective-permute-start | bytes 872 | tf_op jit(solution)/shard_map/ppermute | solution.py:21
  14.1 74.4 %collective-permute-start.4 = (f32[3,3,8]{2,0,1:T(4,128)S(1)}, f32[3,3,8]{2,0,1:T(4,128)S(1)}, u32[]{:S(2)}, u32[]{:S(2)}) collective-permute-start(f32[3,3,8]{2,0,1:T(4,128)S(1)} %copy.29), channel_id=1, source_target_pairs={{0,4},{4,8},{8,12},{12,16},{16,20},{20,24},{24,28},{28,32},{32,36}... | collective-permute-start | bytes 872 | tf_op jit(solution)/shard_map/ppermute | solution.py:21
  17.7 105.5 %collective-permute-start.3 = (f32[3,8]{1,0:T(4,128)}, f32[3,8]{1,0:T(4,128)}, u32[]{:S(2)}, u32[]{:S(2)}) collective-permute-start(f32[3,8]{1,0:T(4,128)} %param.11), channel_id=1, source_target_pairs={{4,0},{8,4},{12,8},{16,12},{20,16},{24,20},{28,24},{32,28},{36,32}... | collective-permute-start | bytes 296 | tf_op jit(solution)/shard_map/ppermute | solution.py:21
  21.3 16.9 %copy-start.14 = (s32[128]{0:T(128)S(1)}, s32[128]{0:T(128)}, u32[]{:S(2)}) copy-start(s32[128]{0:T(128)} %param.13) | copy-start | bytes 1540
  21.4 17.5 %copy-start.15 = (s32[128]{0:T(128)S(1)}, s32[128]{0:T(128)}, u32[]{:S(2)}) copy-start(s32[128]{0:T(128)} %param.12) | copy-start | bytes 1540
  30.8 18.1 %copy-start.6 = (f32[3,3,8,1024]{3,2,1,0:T(8,128)S(1)}, f32[3,3,8,1024]{3,2,1,0:T(8,128)}, u32[]{:S(2)}) copy-start(f32[3,3,8,1024]{3,2,1,0:T(8,128)} %param.9) | copy-start | bytes 884740
  38.8 37.8 %copy-start.12 = (pred[128]{0:T(512)(128)(4,1)}, pred[128]{0:T(512)(128)(4,1)S(1)}, u32[]{:S(2)}) copy-start(pred[128]{0:T(512)(128)(4,1)S(1)} %get-tuple-element.250) | copy-start | bytes 388
  76.7 8.0 copy-start.10
  84.7 6.2 copy-start.1
  84.7 38.6 %collective-permute-start.2 = (f32[3,8]{1,0:T(4,128)S(1)}, f32[3,8]{1,0:T(4,128)}, u32[]{:S(2)}, u32[]{:S(2)}) collective-permute-start(f32[3,8]{1,0:T(4,128)S(1)} %copy-done.10), channel_id=1, source_target_pairs={{0,4},{4,8},{8,12},{12,16},{16,20},{20,24},{24,28},{28,32},{32,36}... | collective-permute-start | bytes 296 | tf_op jit(solution)/shard_map/ppermute | solution.py:21
  97.3 6.6 copy-start.11
  97.3 12.5 %slice-start = ((s8[4718592]{0:T(1024)(128)(4,1)}), s8[524288]{0:T(1024)(128)(4,1)S(1)}, s32[]{:S(2)}) async-start(s8[4718592]{0:T(1024)(128)(4,1)} %bitcast.54), calls=%async_computation | async-start | bytes 1048576
  103.9 5.9 slice-start.1
  229.7 4.4 collective-permute-start.7
  231.7 4.9 collective-permute-start.6
  491.9 5.7 collective-permute-start.9
  494.9 3.3 collective-permute-start.8
  604.5 5.9 collective-permute-start.11
  608.4 4.9 collective-permute-start.10
  869.5 5.8 collective-permute-start.13
  872.4 3.4 collective-permute-start.12
  (8 other events, 21.0 us)
where the time goes:
time: 991 us; the launch traced here: 981 us
  blocking collectives  820 us (83%)
  other arithmetic  54.3 us (5%)
  starting transfers between devices  43.3 us (4%)
  local copies, waits for them, and re-layouts  38.1 us (4%)
  matrix products  13.1 us (1%)
    psum x2, blocking collectives, model_update(): alpha_norm = jnp.sqrt(lax.psum(jnp.sum(vector * vector), 'ev') + eps_small)  494 us
    psum x3, blocking collectives, data_norm(): lax.psum(jnp.sum(values * values), ('ev', 'st')) + eps_small  311 us
    ppermute x14, starting transfers between devices, passed_along(): return lax.ppermute(block, axis, route)  43.3 us
  transfers between devices with their start and end apart: 14, of which 4 were waited for; matrix products, arithmetic and copies ran while one was open for 10% of the time, Pallas kernels for 0%

commit v1 on v0

v1 whole, which is shorter than its diff:
```python
import jax
import jax.numpy as jnp
from jax import lax
from jax.experimental import pallas as pl
from jax.experimental.pallas import tpu as pltpu
from jax.sharding import Mesh
from jax.sharding import PartitionSpec as P

LAGS = 32
LANES = 128
ROWS = 8
EV_DEV = 8
NEAR = 3 * EV_DEV
STATIONS_DEV = 3
TRACES_DEV = 9
LENGTH = 1024
CHUNKS = LENGTH // LANES
QUARTER = LENGTH // 4
WINDOW = LENGTH // 2
SPAN = WINDOW + LANES
SPAN_CHUNKS = SPAN // LANES
PAIR_DEV = 128
TRACE_ROWS = NEAR * CHUNKS
VMEM_BYTES = 48 * 1024 * 1024
DEAD = -1000.0

eps_small = 1e-06
sample_step = 0.01
exact_mode = lax.Precision.HIGHEST
NT = (((1,), (1,)), ((), ()))
NN = (((1,), (0,)), ((), ()))


def device_index():
    return lax.axis_index("g") * 2 + lax.axis_index("c")


def dot_exact(left, right, dims):
    return lax.dot_general(
        left, right, dims, precision=exact_mode, preferred_element_type=jnp.float32
    )


def dot_bf16(left, right, dims):
    return lax.dot_general(left, right, dims, preferred_element_type=jnp.float32)


def split_bf16(values):
    high = values.astype(jnp.bfloat16)
    low = (values - high.astype(jnp.float32)).astype(jnp.bfloat16)
    return high, low


def pack_kernel(live_ref, traces_ref, slowness_ref, time_ref, first_ref, second_ref, out_ref):
    base = device_index() * EV_DEV - EV_DEV
    out_ref[0:TRACES_DEV] = traces_ref[...]
    out_ref[TRACES_DEV] = jnp.zeros((ROWS, LENGTH), jnp.float32)
    slots = lax.broadcasted_iota(jnp.int32, (1, PAIR_DEV), 1)
    alive = slots < live_ref[0]
    for row, ids_ref in enumerate((first_ref, second_ref)):
        ids = (ids_ref[...] - base).astype(jnp.float32)
        out_ref[TRACES_DEV, row : row + 1, 0:LANES] = jnp.where(alive, ids, DEAD)
    out_ref[TRACES_DEV, 0:STATIONS_DEV, LANES : LANES + EV_DEV] = time_ref[...]
    for q in range(3):
        lane = (2 + q) * LANES
        out_ref[TRACES_DEV, 0:STATIONS_DEV, lane : lane + EV_DEV] = slowness_ref[q]


def incidence(aux, offset):
    events = lax.broadcasted_iota(jnp.int32, (NEAR, PAIR_DEV), 0).astype(jnp.float32)
    starts = aux[0:1, 0:LANES] + offset
    ends = aux[1:2, 0:LANES] + offset
    return (events == starts).astype(jnp.float32) - (events == ends).astype(jnp.float32)


def near_block(left, own, right, part):
    lane = part * LANES
    return jnp.concatenate(
        [aux[0:STATIONS_DEV, lane : lane + EV_DEV] for aux in (left, own, right)], axis=1
    )


def shift_kernel(
    second_ref,
    lag_ref,
    own_ref,
    left_ref,
    right_ref,
    lag_rows_ref,
    shift_ref,
    block_ref,
    near_ref,
    moved_ref,
    high_ref,
    low_ref,
):
    base = device_index() * EV_DEV - EV_DEV
    for part, ref in enumerate((left_ref, own_ref, right_ref)):
        for item in range(TRACES_DEV):
            values = ref[item]
            power = jnp.sum(values * values, axis=1, keepdims=True)
            values = values * lax.rsqrt(power + eps_small)
            for chunk in range(CHUNKS):
                start = item * TRACE_ROWS + part * EV_DEV * CHUNKS + chunk
                near_ref[pl.ds(start, EV_DEV, stride=CHUNKS), :] = values[
                    :, chunk * LANES : (chunk + 1) * LANES
                ]
    near_ref[pl.ds(TRACES_DEV * TRACE_ROWS, 2 * ROWS), :] = jnp.zeros((2 * ROWS, LANES), jnp.float32)

    lane_ids = lax.broadcasted_iota(jnp.int32, (ROWS, LANES), 1)

    def align(slot, carry):
        event = jnp.clip(second_ref[slot] - base, 0, NEAR - 1)
        for station in range(STATIONS_DEV):
            begin = lag_ref[station, slot] + (QUARTER - LAGS // 2)
            chunk = begin // LANES
            lane = begin % LANES
            keep = lane_ids >= lane
            for component in range(3):
                item = station * 3 + component
                row = item * TRACE_ROWS + event * CHUNKS + chunk
                here = near_ref[pl.ds(row, ROWS), :]
                after = near_ref[pl.ds(row + 1, ROWS), :]
                moved = pltpu.roll(jnp.where(keep, here, after), (LANES - lane) % LANES, 1)
                to = pl.multiple_of((item * PAIR_DEV + slot) * ROWS, ROWS)
                moved_ref[pl.ds(to, ROWS), :] = moved
        return carry

    lax.fori_loop(0, PAIR_DEV, align, 0, unroll=4)

    lag_in_row = lax.broadcasted_iota(jnp.int32, (16, EV_DEV * LAGS), 1)
    row_ids = lax.broadcasted_iota(jnp.int32, (16, EV_DEV * LAGS), 0)
    centred = (lag_in_row % LAGS - LAGS // 2).astype(jnp.float32)
    weights = jnp.where(row_ids < EV_DEV, centred, 1.0)
    pick = jnp.where(lag_in_row // LAGS == row_ids % EV_DEV, weights, 0.0)

    aux_left, aux_own, aux_right = left_ref[TRACES_DEV], own_ref[TRACES_DEV], right_ref[TRACES_DEV]
    signs = incidence(aux_own, 0.0)
    events = lax.broadcasted_iota(jnp.int32, (EV_DEV, PAIR_DEV), 0).astype(jnp.float32)
    first_hot = (events == aux_own[0:1, 0:LANES] - EV_DEV).astype(jnp.float32)
    station_shift = []
    for station in range(STATIONS_DEV):
        energy = jnp.zeros((PAIR_DEV, EV_DEV * LAGS), jnp.float32)
        for component in range(3):
            item = station * 3 + component
            window = own_ref[item, :, QUARTER : QUARTER + WINDOW]
            power = jnp.sum(window * window, axis=1, keepdims=True)
            window = window * lax.rsqrt(power + eps_small)
            padded = jnp.concatenate([window, jnp.zeros((EV_DEV, LANES), jnp.float32)], axis=1)
            for event in range(EV_DEV):
                wide = jnp.broadcast_to(padded[event : event + 1], (LAGS, SPAN))
                wide = pltpu.roll(wide, 0, 1, stride=1, stride_axis=0)
                high, low = split_bf16(wide)
                high_ref[pl.ds(event * LAGS, LAGS), :] = high
                low_ref[pl.ds(event * LAGS, LAGS), :] = low
            pieces = [
                moved_ref[pl.ds(item * PAIR_DEV * ROWS + chunk, PAIR_DEV, stride=ROWS), :]
                for chunk in range(SPAN_CHUNKS)
            ]
            high, low = split_bf16(jnp.concatenate(pieces, axis=1))
            xcorr = dot_bf16(high, high_ref[...], NT)
            xcorr = xcorr + dot_bf16(low, high_ref[...], NT)
            xcorr = xcorr + dot_bf16(high, low_ref[...], NT)
            energy = energy + xcorr * xcorr
        sums = dot_exact(pick, energy, NT)
        above = jnp.sum(sums[0:EV_DEV] * first_hot, axis=0, keepdims=True)
        below = jnp.sum(sums[EV_DEV:] * first_hot, axis=0, keepdims=True)
        station_shift.append(above / (below + eps_small))
    slots_alive = (aux_own[0:1, 0:LANES] >= 0.0).astype(jnp.float32)
    shift = jnp.concatenate(station_shift, axis=0) * slots_alive
    shift_ref[...] = shift

    times = near_block(aux_left, aux_own, aux_right, 1)
    rhs = slots_alive * (
        sample_step * (lag_rows_ref[...].astype(jnp.float32) + shift)
    ) - dot_exact(times, signs, NN)
    per_event = dot_exact(rhs, signs, NT)
    station_group = lax.axis_index("x")
    own_signs = signs[EV_DEV : 2 * EV_DEV]
    counts = dot_exact(own_signs, signs, NT)
    for aux, offset in ((aux_left, -float(EV_DEV)), (aux_right, float(EV_DEV))):
        other = incidence(aux, offset)
        counts = counts + dot_exact(other[EV_DEV : 2 * EV_DEV], other, NT)
    block_ref[...] = jnp.zeros((ROWS, LANES), jnp.float32)
    for q in range(3):
        slowness = near_block(aux_left, aux_own, aux_right, 2 + q)
        block_ref[q : q + 1, 0:NEAR] = jnp.sum(slowness * per_event, axis=0, keepdims=True)
    block_ref[3:4, 0:NEAR] = jnp.sum(per_event, axis=0, keepdims=True)
    total = jnp.sum(jnp.sum(rhs * rhs, axis=1, keepdims=True), axis=0, keepdims=True)
    block_ref[0:1, NEAR : NEAR + 1] = total
    block_ref[:, 32 : 32 + NEAR] = jnp.where(station_group == 0, counts, 0.0)
    for group in range(4):
        row = 4 * (group // 2)
        lane = 64 + 32 * (group % 2)
        for q in range(3):
            own = aux_own[0:STATIONS_DEV, (2 + q) * LANES : (2 + q) * LANES + EV_DEV]
            at = lane + q * EV_DEV
            block_ref[row : row + STATIONS_DEV, at : at + EV_DEV] = jnp.where(
                station_group == group, own, 0.0
            )


def solve_kernel(gathered_ref, out_ref, rows_ref):
    half = LANES // 2
    tables = []
    for row in range(ROWS):
        for core in range(2):
            values = gathered_ref[pl.ds(core * half * ROWS + row, half, stride=ROWS), :]
            rows_ref[pl.ds(row * LANES + core, half, stride=2), :] = values
        tables.append(jnp.transpose(rows_ref[pl.ds(row * LANES, LANES), :]))

    def along(lower, own, upper):
        return own + pltpu.roll(upper, 1, 1) + pltpu.roll(lower, LANES - 1, 1)

    back = [along(tables[q][0:8], tables[q][8:16], tables[q][16:24]) for q in range(4)]
    counts = [
        [tables[a][32 + 8 * side : 40 + 8 * side] for side in range(3)] for a in range(EV_DEV)
    ]
    deriv = []
    for group in range(4):
        for station in range(STATIONS_DEV):
            table = tables[4 * (group // 2) + station]
            lane = 64 + 32 * (group % 2)
            deriv.append([table[lane + 8 * q : lane + 8 * q + 8] for q in range(3)])

    def total(values):
        return jnp.sum(jnp.sum(values, axis=1, keepdims=True), axis=0, keepdims=True)

    def inner(left, right):
        terms = left[0] * right[0]
        for q in range(1, 4):
            terms = terms + left[q] * right[q]
        return total(terms)

    def normal(model):
        result = [jnp.zeros((EV_DEV, LANES), jnp.float32) for _ in range(4)]
        for rates in deriv:
            data = model[3]
            for q in range(3):
                data = data + rates[q] * model[q]
            sides = [None, None, None]
            for a in range(EV_DEV):
                row = jnp.broadcast_to(data[a : a + 1], (EV_DEV, LANES))
                for side in range(3):
                    term = counts[a][side] * row
                    sides[side] = term if a == 0 else sides[side] + term
            mixed = along(*sides)
            for q in range(3):
                result[q] = result[q] + rates[q] * mixed
            result[3] = result[3] + mixed
        return result

    rhs_square = total(tables[0][NEAR : NEAR + 1])
    beta = jnp.sqrt(rhs_square + eps_small)
    unit_square = rhs_square / (beta * beta)
    adjoint = [value / beta for value in back]
    alpha = jnp.sqrt(inner(adjoint, adjoint) + eps_small)
    model = [value / alpha for value in adjoint]
    search = model
    location = [jnp.zeros((EV_DEV, LANES), jnp.float32) for _ in range(4)]
    phi_bar = beta
    rho_bar = alpha
    for turn in range(2):
        normal_model = normal(model)
        square = inner(model, normal_model) - 2.0 * alpha * inner(model, adjoint)
        square = jnp.maximum(square + alpha * alpha * unit_square, 0.0)
        beta = jnp.sqrt(square + eps_small)
        rho = jnp.sqrt(rho_bar * rho_bar + beta * beta)
        cosine = rho_bar / rho
        sine = beta / rho
        phi = cosine * phi_bar
        phi_bar = sine * phi_bar
        step = phi / rho
        location = [location[q] + step * search[q] for q in range(4)]
        if turn == 0:
            unit_square = square / (beta * beta)
            adjoint = [(normal_model[q] - alpha * adjoint[q]) / beta for q in range(4)]
            vector = [adjoint[q] - beta * model[q] for q in range(4)]
            alpha = jnp.sqrt(inner(vector, vector) + eps_small)
            model = [value / alpha for value in vector]
            theta = sine * alpha
            rho_bar = -cosine * alpha
            search = [model[q] - theta / rho * search[q] for q in range(4)]

    lanes = lax.broadcasted_iota(jnp.int32, (ROWS, LANES), 1)
    mine = (lanes == device_index()).astype(jnp.float32)
    own = dot_exact(mine, jnp.concatenate(location, axis=0), NT)
    for q in range(4):
        out_ref[q : q + 1, :] = own[0:1, q * EV_DEV : (q + 1) * EV_DEV]


def passed_along(block, distance):
    count = lax.axis_size("g") * lax.axis_size("c")
    route = [(i - distance, i) for i in range(count) if 0 <= i - distance < count]
    return lax.ppermute(block, ("g", "c"), route)


def body(traces, ray_slowness, travel_time, pair_first, pair_second, pair_lag, pair_live):
    vmem = pl.BlockSpec(memory_space=pltpu.VMEM)
    smem = pl.BlockSpec(memory_space=pltpu.SMEM)
    params = pltpu.CompilerParams(vmem_limit_bytes=VMEM_BYTES)
    message = pl.pallas_call(
        pack_kernel,
        out_shape=jax.ShapeDtypeStruct((TRACES_DEV + 1, ROWS, LENGTH), jnp.float32),
        in_specs=[smem] + [vmem] * 5,
        out_specs=vmem,
        compiler_params=params,
        name="pack",
    )(
        pair_live,
        traces.reshape(TRACES_DEV, EV_DEV, LENGTH),
        ray_slowness,
        travel_time,
        pair_first.reshape(1, PAIR_DEV),
        pair_second.reshape(1, PAIR_DEV),
    )
    from_left = passed_along(message, 1)
    from_right = passed_along(message, -1)
    refined_shift, block = pl.pallas_call(
        shift_kernel,
        out_shape=(
            jax.ShapeDtypeStruct((STATIONS_DEV, PAIR_DEV), jnp.float32),
            jax.ShapeDtypeStruct((ROWS, LANES), jnp.float32),
        ),
        in_specs=[smem, smem] + [vmem] * 4,
        out_specs=(vmem, vmem),
        scratch_shapes=[
            pltpu.VMEM((TRACES_DEV * TRACE_ROWS + 2 * ROWS, LANES), jnp.float32),
            pltpu.VMEM((TRACES_DEV * PAIR_DEV * ROWS, LANES), jnp.float32),
            pltpu.VMEM((EV_DEV * LAGS, SPAN), jnp.bfloat16),
            pltpu.VMEM((EV_DEV * LAGS, SPAN), jnp.bfloat16),
        ],
        compiler_params=params,
        name="shifts",
    )(pair_second, pair_lag, message, from_left, from_right, pair_lag)
    block = lax.psum(block, "x")
    chips = lax.axis_size("g")
    copies = jnp.broadcast_to(block[None], (chips, ROWS, LANES))
    gathered = lax.all_to_all(copies, "g", 0, 0, tiled=True)
    gathered = lax.all_gather(gathered, "c", axis=0)
    location = pl.pallas_call(
        solve_kernel,
        out_shape=jax.ShapeDtypeStruct((4, EV_DEV), jnp.float32),
        in_specs=[vmem],
        out_specs=vmem,
        scratch_shapes=[pltpu.VMEM((ROWS * LANES, LANES), jnp.float32)],
        compiler_params=params,
        name="solve",
    )(gathered.reshape(2 * chips * ROWS, LANES))
    return refined_shift, location


def solution(mesh):
    ev, st = mesh.devices.shape
    fine = Mesh(mesh.devices.reshape(ev // 2, 2, st), ("g", "c", "x"))
    event_axes = ("g", "c")
    in_specs = (
        P("x", None, event_axes, None),
        P(None, "x", event_axes),
        P("x", event_axes),
        P(event_axes),
        P(event_axes),
        P("x", event_axes),
        P(event_axes),
    )
    out_specs = (P("x", event_axes), P(None, event_axes))
    return jax.shard_map(body, mesh=fine, in_specs=in_specs, out_specs=out_specs, check_vma=False)
```

time: 991 us -> 72.7 us (0.07)
  blocking collectives: 820 us -> 40.6 us
  other arithmetic: 54.3 us -> 0 us
  local copies, waits for them, and re-layouts: 38.1 us -> 2.32 us
  starting transfers between devices: 43.3 us -> 10.7 us
  Pallas kernels: 0 us -> 13.5 us
  matrix products: 13.1 us -> 0 us
    psum x7 -> x1, blocking collectives: 820 us -> 5.97 us  [body(): block = lax.psum(block, 'x')]
    ppermute x14 -> x2, starting transfers between devices: 43.3 us -> 10.7 us  [passed_along(): return lax.ppermute(block, ('g', 'c'), route)]
    gather x4 -> x0, local copies, waits for them, and re-layouts: 28.2 us -> none  [the longest x1 19.4 us: one_block(): first_rows = jnp.take(first_spec, first_ids, axis=2)]
    all_to_all x0 -> x1, blocking collectives: none -> 27 us  [body(): gathered = lax.all_to_all(copies, 'g', 0, 0, tiled=True)]
    cos x2 -> x0, other arithmetic: 14.9 us -> none  [the longest x1 9.44 us: dft_rows(): return jnp.concatenate([jnp.cos(angle_cos), jnp.sin(angle_sin)], axis=1)]
    select_n x4 -> x0, other arithmetic: 13.8 us -> none  [the longest x2 7.96 us: one_block(): first_rows = jnp.take(first_spec, first_ids, axis=2)]
    pallas_call x0 -> x3, Pallas kernels: none -> 13.5 us  [the longest x1 11.8 us: body(): pl.pallas_call(shift_kernel, out_shape=(jax.ShapeDtypeStruct((STATIONS_DE...]
    dot_general x15 -> x0, matrix products: 13.1 us -> none  [the longest x1 4.3 us: block_shifts(): jnp.einsum('gcbf,fk->gcbk', rotated, lag_table, precision=exact_mode)]
  transfers between devices with their start and end apart: 14 -> 2, of which waited for: 4 -> 1; matrix products, arithmetic and copies ran while one was open for 10% -> 0% of each run, Pallas kernels for 0% -> 0%
where the time goes in v1:
time: 72.7 us; the launch traced here: 72.4 us
  blocking collectives  40.6 us (56%)
  Pallas kernels  13.5 us (19%)
  starting transfers between devices  10.7 us (15%)
  waiting for transfers between devices  3.99 us (5%)
  local copies, waits for them, and re-layouts  2.32 us (3%)
  between operations  1.36 us (2%)
    all_to_all x1, blocking collectives, body(): gathered = lax.all_to_all(copies, 'g', 0, 0, tiled=True)  27 us
    pallas_call x1, Pallas kernels, body(): pl.pallas_call(shift_kernel, out_shape=(jax.ShapeDtypeStruct((STATIONS_DE...  11.8 us
    ppermute x2, starting transfers between devices, passed_along(): return lax.ppermute(block, ('g', 'c'), route)  10.7 us
    all_gather x1, blocking collectives, body(): gathered = lax.all_gather(gathered, 'c', axis=0)  7.55 us
    psum x1, blocking collectives, body(): block = lax.psum(block, 'x')  5.97 us
    ppermute x2, waiting for transfers between devices, passed_along(): return lax.ppermute(block, ('g', 'c'), route)  3.99 us
    unnamed x12, local copies, waits for them, and re-layouts  2.3 us
    pallas_call x1, Pallas kernels, body(): pl.pallas_call(solve_kernel, out_shape=jax.ShapeDtypeStruct((4, EV_DEV),...  1.71 us
  transfers between devices with their start and end apart: 2, of which 1 were waited for; matrix products, arithmetic and copies ran while one was open for 0% of the time, Pallas kernels for 0%

profile of v1, /device:TPU:1, one launch (start us, length us, event | category | flops | bytes accessed | tf_op | source)
XLA Modules:
  0.0 72.4 jit_solution(5224307657881418685)
XLA Ops:
  0.6 0.0 copy-start.2
  1.3 0.0 copy-start.3
  1.3 0.0 copy-start.5
  1.3 0.0 copy-done.2
  1.3 0.6 copy-done.3
  2.0 0.0 copy-done.5
  2.0 0.0 copy-start
  2.0 1.0 %copy-done = f32[3,3,8,1024]{3,2,1,0:T(8,128)S(1)} copy-done((f32[3,3,8,1024]{3,2,1,0:T(8,128)S(1)}, f32[3,3,8,1024]{3,2,1,0:T(8,128)}, u32[]{:S(2)}) %copy-start) | copy-done | bytes 294936
  2.9 0.0 copy-start.4
  2.9 0.7 copy-done.4
  3.6 0.0 copy-start.1
  3.6 8.8 %collective-permute-start.1 = (f32[10,8,1024]{2,1,0:T(8,128)S(1)}, f32[10,8,1024]{2,1,0:T(8,128)S(1)}, u32[]{:S(2)}, u32[]{:S(2)}) collective-permute-start(f32[10,8,1024]{2,1,0:T(8,128)S(1)} %pack.1.own_ref), channel_id=1, source_target_pairs={{4,0},{8,4},{12,8},{16,12},{20,16},{24,20},{28,24},{32,28},{36,32}... | collective-permute-start | bytes 983048 | tf_op jit(solution)/shard_map/ppermute | solution.py:295
  12.4 1.9 %collective-permute-start = (f32[10,8,1024]{2,1,0:T(8,128)S(1)}, f32[10,8,1024]{2,1,0:T(8,128)S(1)}, u32[]{:S(2)}, u32[]{:S(2)}) collective-permute-start(f32[10,8,1024]{2,1,0:T(8,128)S(1)} %pack.1.own_ref), channel_id=1, source_target_pairs={{0,4},{4,8},{8,12},{12,16},{16,20},{20,24},{24,28},{28,32},{32,36}... | collective-permute-start | bytes 983048 | tf_op jit(solution)/shard_map/ppermute | solution.py:295
  14.4 0.0 collective-permute-done.1.right_ref
  14.4 4.0 %collective-permute-done.left_ref = f32[10,8,1024]{2,1,0:T(8,128)S(1)} collective-permute-done((f32[10,8,1024]{2,1,0:T(8,128)S(1)}, f32[10,8,1024]{2,1,0:T(8,128)S(1)}, u32[]{:S(2)}, u32[]{:S(2)}) %collective-permute-start) | collective-permute-done | bytes 327712 | tf_op jit(solution)/shard_map/ppermute | solution.py:295
  18.4 0.0 copy-done.1
  18.4 11.8 %shifts.1 = (f32[3,128]{1,0:T(4,128)}, f32[8,128]{1,0:T(8,128)S(1)}) custom-call(s32[128]{0:T(128)S(1)} %copy-done.3, s32[3,128]{1,0:T(4,128)S(1)} %copy-done.1, f32[10,8,1024]{2,1,0:T(8,128)S(1)} %pack.1.own_ref, f32[10,8,1024]{2,1,0:T(8,128)S(1)} %collective-permute-done.left_ref, f32[10,8,1024]{2,1,0:T(8,128)S(1)} %collective-permute-done.1.right_ref, ...), custom_call_target="tpu_custom_call" | custom-call | tf_op jit(solution)/shard_map/shifts/pallas_call | solution.py:319
  30.1 6.0 %psum.7 = f32[8,128]{1,0:T(8,128)S(1)} all-reduce(f32[8,128]{1,0:T(8,128)S(1)} %get-tuple-element.5), channel_id=1, replica_groups=mesh['g'=64,'c'=2,'x'=4] {'x'}, use_global_device_ids=true, to_apply=%region_0.0 | all-reduce | flops 1024 | bytes 8192 | tf_op jit(solution)/shard_map/psum | solution.py:336
  36.1 27.0 %all_to_all.5 = f32[64,8,128]{2,1,0:T(8,128)S(1)} all-to-all(f32[64,8,128]{2,1,0:T(8,128)S(1)} %broadcast_in_dim.2), channel_id=1, replica_groups=mesh['g'=64,'c'=2,'x'=4] {'g'}, dimensions={0} | all-to-all | bytes 524288 | tf_op jit(solution)/shard_map/all_to_all | solution.py:339
  63.1 7.6 %all-gather = f32[128,8,128]{2,1,0:T(8,128)S(1)} all-gather(f32[64,8,128]{2,1,0:T(8,128)S(1)} %all_to_all.5), channel_id=2, replica_groups=mesh['g'=64,'c'=2,'x'=4] {'c'}, dimensions={0}, use_global_device_ids=true | all-gather | bytes 786432 | tf_op jit(solution)/shard_map/all_gather | solution.py:340
  70.7 1.7 %solve.1 = f32[4,8]{1,0:T(4,128)} custom-call(f32[1024,128]{1,0:T(8,128)S(1)} %bitcast.4), custom_call_target="tpu_custom_call" | custom-call | tf_op jit(solution)/shard_map/solve/pallas_call | solution.py:341
  (2 shorter events, 0.0 us)
Async XLA Ops:
  0.6 0.7 copy-start.2
  1.3 0.7 copy-start.3
  1.3 0.7 copy-start.5
  2.0 1.0 %copy-start = (f32[3,3,8,1024]{3,2,1,0:T(8,128)S(1)}, f32[3,3,8,1024]{3,2,1,0:T(8,128)}, u32[]{:S(2)}) copy-start(f32[3,3,8,1024]{3,2,1,0:T(8,128)} %param.7) | copy-start | bytes 884740
  2.9 0.7 copy-start.4
  3.6 14.8 %copy-start.1 = (s32[3,128]{1,0:T(4,128)S(1)}, s32[3,128]{1,0:T(4,128)}, u32[]{:S(2)}) copy-start(s32[3,128]{1,0:T(4,128)} %lag_rows_ref.1) | copy-start | bytes 4612
  3.6 10.7 %collective-permute-start.1 = (f32[10,8,1024]{2,1,0:T(8,128)S(1)}, f32[10,8,1024]{2,1,0:T(8,128)S(1)}, u32[]{:S(2)}, u32[]{:S(2)}) collective-permute-start(f32[10,8,1024]{2,1,0:T(8,128)S(1)} %pack.1.own_ref), channel_id=1, source_target_pairs={{4,0},{8,4},{12,8},{16,12},{20,16},{24,20},{28,24},{32,28},{36,32}... | collective-permute-start | bytes 983048 | tf_op jit(solution)/shard_map/ppermute | solution.py:295
  12.4 5.9 %collective-permute-start = (f32[10,8,1024]{2,1,0:T(8,128)S(1)}, f32[10,8,1024]{2,1,0:T(8,128)S(1)}, u32[]{:S(2)}, u32[]{:S(2)}) collective-permute-start(f32[10,8,1024]{2,1,0:T(8,128)S(1)} %pack.1.own_ref), channel_id=1, source_target_pairs={{0,4},{4,8},{8,12},{12,16},{16,20},{20,24},{24,28},{28,32},{32,36}... | collective-permute-start | bytes 983048 | tf_op jit(solution)/shard_map/ppermute | solution.py:295

commit v2 on v1

--- a/solution.py
+++ b/solution.py
@@ -51,19 +51,88 @@
     return high, low
 
 
-def pack_kernel(live_ref, traces_ref, slowness_ref, time_ref, first_ref, second_ref, out_ref):
-    base = device_index() * EV_DEV - EV_DEV
-    out_ref[0:TRACES_DEV] = traces_ref[...]
+def pack_kernel(
+    live_ref,
+    traces_ref,
+    slowness_ref,
+    time_ref,
+    first_ref,
+    second_ref,
+    lag_ref,
+    out_ref,
+    rows_ref,
+    lanes_ref,
+    live,
+    slowness,
+    time,
+    first,
+    second,
+    lag,
+    sems,
+):
+    copies = [
+        pltpu.make_async_copy(source, target, sems.at[at])
+        for at, (source, target) in enumerate(
+            (
+                (traces_ref, out_ref.at[pl.ds(0, TRACES_DEV)]),
+                (live_ref, live),
+                (slowness_ref, slowness),
+                (time_ref, time),
+                (first_ref, first),
+                (second_ref, second),
+                (lag_ref, lag),
+            )
+        )
+    ]
+    for copy in copies:
+        copy.start()
     out_ref[TRACES_DEV] = jnp.zeros((ROWS, LENGTH), jnp.float32)
+    for copy in copies[1:]:
+        copy.wait()
+    me = device_index()
+    base = me * EV_DEV - EV_DEV
     slots = lax.broadcasted_iota(jnp.int32, (1, PAIR_DEV), 1)
-    alive = slots < live_ref[0]
-    for row, ids_ref in enumerate((first_ref, second_ref)):
-        ids = (ids_ref[...] - base).astype(jnp.float32)
-        out_ref[TRACES_DEV, row : row + 1, 0:LANES] = jnp.where(alive, ids, DEAD)
-    out_ref[TRACES_DEV, 0:STATIONS_DEV, LANES : LANES + EV_DEV] = time_ref[...]
+    alive = slots < live[0]
+    for row, ids in enumerate((first, second)):
+        near = (ids[...] - base).astype(jnp.float32)
+        out_ref[TRACES_DEV, row : row + 1, 0:LANES] = jnp.where(alive, near, DEAD)
+    out_ref[TRACES_DEV, 0:STATIONS_DEV, LANES : LANES + EV_DEV] = time[...]
     for q in range(3):
         lane = (2 + q) * LANES
-        out_ref[TRACES_DEV, 0:STATIONS_DEV, lane : lane + EV_DEV] = slowness_ref[q]
+        out_ref[TRACES_DEV, 0:STATIONS_DEV, lane : lane + EV_DEV] = slowness[q]
+    begin = lag[...] + (QUARTER - LAGS // 2)
+    holder = lax.shift_right_arithmetic(second[...], 3)
+    part = jnp.where(holder == me, 0, jnp.where(holder == jnp.bitwise_xor(me, 1), 1, 2))
+    event = part * EV_DEV + jnp.bitwise_and(second[...], EV_DEV - 1)
+    rows_ref[...] = event * CHUNKS + lax.shift_right_arithmetic(begin, 7)
+    lanes_ref[...] = jnp.bitwise_and(begin, LANES - 1)
+    copies[0].wait()
+
+
+def fill_table(ref, table_ref, part):
+    for item in range(TRACES_DEV):
+        values = ref[item]
+        power = jnp.sum(values * values, axis=1, keepdims=True)
+        values = values * lax.rsqrt(power + eps_small)
+        for chunk in range(CHUNKS):
+            start = item * TRACE_ROWS + part * EV_DEV * CHUNKS + chunk
+            table_ref[pl.ds(start, EV_DEV, stride=CHUNKS), :] = values[
+                :, chunk * LANES : (chunk + 1) * LANES
+            ]
+
+
+def first_kernel(own_ref, high_ref, low_ref):
+    for item in range(TRACES_DEV):
+        window = own_ref[item, :, QUARTER : QUARTER + WINDOW]
+        power = jnp.sum(window * window, axis=1, keepdims=True)
+        window = window * lax.rsqrt(power + eps_small)
+        padded = jnp.concatenate([window, jnp.zeros((EV_DEV, LANES), jnp.float32)], axis=1)
+        for event in range(EV_DEV):
+            wide = jnp.broadcast_to(padded[event : event + 1], (LAGS, SPAN))
+            wide = pltpu.roll(wide, 0, 1, stride=1, stride_axis=0)
+            high, low = split_bf16(wide)
+            high_ref[item, pl.ds(event * LAGS, LAGS), :] = high
+            low_ref[item, pl.ds(event * LAGS, LAGS), :] = low
 
 
 def incidence(aux, offset):
@@ -81,106 +150,94 @@
 
 
 def shift_kernel(
-    second_ref,
+    rows_ref,
+    lanes_ref,
+    own_ref,
+    mate_ref,
+    cross_ref,
     lag_ref,
-    own_ref,
-    left_ref,
-    right_ref,
-    lag_rows_ref,
+    high_ref,
+    low_ref,
     shift_ref,
     block_ref,
-    near_ref,
+    table_ref,
     moved_ref,
-    high_ref,
-    low_ref,
 ):
-    base = device_index() * EV_DEV - EV_DEV
-    for part, ref in enumerate((left_ref, own_ref, right_ref)):
-        for item in range(TRACES_DEV):
-            values = ref[item]
-            power = jnp.sum(values * values, axis=1, keepdims=True)
-            values = values * lax.rsqrt(power + eps_small)
-            for chunk in range(CHUNKS):
-                start = item * TRACE_ROWS + part * EV_DEV * CHUNKS + chunk
-                near_ref[pl.ds(start, EV_DEV, stride=CHUNKS), :] = values[
-                    :, chunk * LANES : (chunk + 1) * LANES
-                ]
-    near_ref[pl.ds(TRACES_DEV * TRACE_ROWS, 2 * ROWS), :] = jnp.zeros((2 * ROWS, LANES), jnp.float32)
+    for part, ref in enumerate((own_ref, mate_ref, cross_ref)):
+        fill_table(ref, table_ref, part)
+    table_ref[pl.ds(TRACES_DEV * TRACE_ROWS, 2 * ROWS), :] = jnp.zeros(
+        (2 * ROWS, LANES), jnp.float32
+    )
 
     lane_ids = lax.broadcasted_iota(jnp.int32, (ROWS, LANES), 1)
 
     def align(slot, carry):
-        event = jnp.clip(second_ref[slot] - base, 0, NEAR - 1)
         for station in range(STATIONS_DEV):
-            begin = lag_ref[station, slot] + (QUARTER - LAGS // 2)
-            chunk = begin // LANES
-            lane = begin % LANES
+            row = rows_ref[station, slot]
+            lane = lanes_ref[station, slot]
+            turn = jnp.bitwise_and(-lane, LANES - 1)
             keep = lane_ids >= lane
             for component in range(3):
                 item = station * 3 + component
-                row = item * TRACE_ROWS + event * CHUNKS + chunk
-                here = near_ref[pl.ds(row, ROWS), :]
-                after = near_ref[pl.ds(row + 1, ROWS), :]
-                moved = pltpu.roll(jnp.where(keep, here, after), (LANES - lane) % LANES, 1)
+                here = table_ref[pl.ds(row + item * TRACE_ROWS, ROWS), :]
+                after = table_ref[pl.ds(row + (item * TRACE_ROWS + 1), ROWS), :]
+                moved = pltpu.roll(jnp.where(keep, here, after), turn, 1)
                 to = pl.multiple_of((item * PAIR_DEV + slot) * ROWS, ROWS)
                 moved_ref[pl.ds(to, ROWS), :] = moved
         return carry
 
-    lax.fori_loop(0, PAIR_DEV, align, 0, unroll=4)
-
-    lag_in_row = lax.broadcasted_iota(jnp.int32, (16, EV_DEV * LAGS), 1)
-    row_ids = lax.broadcasted_iota(jnp.int32, (16, EV_DEV * LAGS), 0)
-    centred = (lag_in_row % LAGS - LAGS // 2).astype(jnp.float32)
-    weights = jnp.where(row_ids < EV_DEV, centred, 1.0)
-    pick = jnp.where(lag_in_row // LAGS == row_ids % EV_DEV, weights, 0.0)
-
-    aux_left, aux_own, aux_right = left_ref[TRACES_DEV], own_ref[TRACES_DEV], right_ref[TRACES_DEV]
-    signs = incidence(aux_own, 0.0)
-    events = lax.broadcasted_iota(jnp.int32, (EV_DEV, PAIR_DEV), 0).astype(jnp.float32)
-    first_hot = (events == aux_own[0:1, 0:LANES] - EV_DEV).astype(jnp.float32)
-    station_shift = []
+    lax.fori_loop(0, PAIR_DEV, align, 0, unroll=8)
+
+    aux_own = own_ref[TRACES_DEV]
+    even = lax.axis_index("c") == 0
+    aux_left = jnp.where(even, cross_ref[TRACES_DEV], mate_ref[TRACES_DEV])
+    aux_right = jnp.where(even, mate_ref[TRACES_DEV], cross_ref[TRACES_DEV])
+
+    energies = []
     for station in range(STATIONS_DEV):
         energy = jnp.zeros((PAIR_DEV, EV_DEV * LAGS), jnp.float32)
         for component in range(3):
             item = station * 3 + component
-            window = own_ref[item, :, QUARTER : QUARTER + WINDOW]
-            power = jnp.sum(window * window, axis=1, keepdims=True)
-            window = window * lax.rsqrt(power + eps_small)
-            padded = jnp.concatenate([window, jnp.zeros((EV_DEV, LANES), jnp.float32)], axis=1)
-            for event in range(EV_DEV):
-                wide = jnp.broadcast_to(padded[event : event + 1], (LAGS, SPAN))
-                wide = pltpu.roll(wide, 0, 1, stride=1, stride_axis=0)
-                high, low = split_bf16(wide)
-                high_ref[pl.ds(event * LAGS, LAGS), :] = high
-                low_ref[pl.ds(event * LAGS, LAGS), :] = low
             pieces = [
                 moved_ref[pl.ds(item * PAIR_DEV * ROWS + chunk, PAIR_DEV, stride=ROWS), :]
                 for chunk in range(SPAN_CHUNKS)
             ]
             high, low = split_bf16(jnp.concatenate(pieces, axis=1))
-            xcorr = dot_bf16(high, high_ref[...], NT)
-            xcorr = xcorr + dot_bf16(low, high_ref[...], NT)
-            xcorr = xcorr + dot_bf16(high, low_ref[...], NT)
+            both = dot_bf16(jnp.concatenate([high, low], axis=0), high_ref[item], NT)
+            xcorr = both[0:PAIR_DEV] + both[PAIR_DEV:] + dot_bf16(high, low_ref[item], NT)
             energy = energy + xcorr * xcorr
-        sums = dot_exact(pick, energy, NT)
-        above = jnp.sum(sums[0:EV_DEV] * first_hot, axis=0, keepdims=True)
-        below = jnp.sum(sums[EV_DEV:] * first_hot, axis=0, keepdims=True)
+        energies.append(energy)
+    lag_in_row = lax.broadcasted_iota(jnp.int32, (16, EV_DEV * LAGS), 1)
+    row_ids = lax.broadcasted_iota(jnp.int32, (16, EV_DEV * LAGS), 0)
+    centred = (lag_in_row % LAGS - LAGS // 2).astype(jnp.float32)
+    weights = jnp.where(row_ids < EV_DEV, centred, 1.0)
+    pick = jnp.where(lag_in_row // LAGS == row_ids % EV_DEV, weights, 0.0).astype(jnp.bfloat16)
+    high, low = split_bf16(jnp.concatenate(energies, axis=0))
+    sums = dot_bf16(pick, high, NT) + dot_bf16(pick, low, NT)
+    events = lax.broadcasted_iota(jnp.int32, (EV_DEV, PAIR_DEV), 0).astype(jnp.float32)
+    first_hot = (events == aux_own[0:1, 0:LANES] - EV_DEV).astype(jnp.float32)
+    station_shift = []
+    for station in range(STATIONS_DEV):
+        lane = station * PAIR_DEV
+        above = jnp.sum(sums[0:EV_DEV, lane : lane + PAIR_DEV] * first_hot, axis=0, keepdims=True)
+        below = jnp.sum(sums[EV_DEV:, lane : lane + PAIR_DEV] * first_hot, axis=0, keepdims=True)
         station_shift.append(above / (below + eps_small))
     slots_alive = (aux_own[0:1, 0:LANES] >= 0.0).astype(jnp.float32)
     shift = jnp.concatenate(station_shift, axis=0) * slots_alive
     shift_ref[...] = shift
 
+    signs = incidence(aux_own, 0.0)
     times = near_block(aux_left, aux_own, aux_right, 1)
     rhs = slots_alive * (
-        sample_step * (lag_rows_ref[...].astype(jnp.float32) + shift)
+        sample_step * (lag_ref[...].astype(jnp.float32) + shift)
     ) - dot_exact(times, signs, NN)
     per_event = dot_exact(rhs, signs, NT)
     station_group = lax.axis_index("x")
-    own_signs = signs[EV_DEV : 2 * EV_DEV]
-    counts = dot_exact(own_signs, signs, NT)
+    own_signs = signs[EV_DEV : 2 * EV_DEV].astype(jnp.bfloat16)
+    counts = dot_bf16(own_signs, signs.astype(jnp.bfloat16), NT)
     for aux, offset in ((aux_left, -float(EV_DEV)), (aux_right, float(EV_DEV))):
-        other = incidence(aux, offset)
-        counts = counts + dot_exact(other[EV_DEV : 2 * EV_DEV], other, NT)
+        other = incidence(aux, offset).astype(jnp.bfloat16)
+        counts = counts + dot_bf16(other[EV_DEV : 2 * EV_DEV], other, NT)
     block_ref[...] = jnp.zeros((ROWS, LANES), jnp.float32)
     for q in range(3):
         slowness = near_block(aux_left, aux_own, aux_right, 2 + q)
@@ -289,22 +346,46 @@
         out_ref[q : q + 1, :] = own[0:1, q * EV_DEV : (q + 1) * EV_DEV]
 
 
-def passed_along(block, distance):
+def swapped(block, partner):
     count = lax.axis_size("g") * lax.axis_size("c")
-    route = [(i - distance, i) for i in range(count) if 0 <= i - distance < count]
+    route = [(i, partner(i)) for i in range(count) if 0 <= partner(i) < count]
     return lax.ppermute(block, ("g", "c"), route)
 
 
-def body(traces, ray_slowness, travel_time, pair_first, pair_second, pair_lag, pair_live):
-    vmem = pl.BlockSpec(memory_space=pltpu.VMEM)
-    smem = pl.BlockSpec(memory_space=pltpu.SMEM)
-    params = pltpu.CompilerParams(vmem_limit_bytes=VMEM_BYTES)
-    message = pl.pallas_call(
+def in_other_core(index):
+    return index + 1 - 2 * (index % 2)
+
+
+def in_other_chip(index):
+    return index - 1 + 2 * (index % 2)
+
+
+VMEM = pl.BlockSpec(memory_space=pltpu.VMEM)
+SMEM = pl.BlockSpec(memory_space=pltpu.SMEM)
+HBM = pl.BlockSpec(memory_space=pltpu.HBM)
+PARAMS = pltpu.CompilerParams(vmem_limit_bytes=VMEM_BYTES)
+
+
+def pack(traces, ray_slowness, travel_time, pair_first, pair_second, pair_lag, pair_live):
+    return pl.pallas_call(
         pack_kernel,
-        out_shape=jax.ShapeDtypeStruct((TRACES_DEV + 1, ROWS, LENGTH), jnp.float32),
-        in_specs=[smem] + [vmem] * 5,
-        out_specs=vmem,
-        compiler_params=params,
+        out_shape=(
+            jax.ShapeDtypeStruct((TRACES_DEV + 1, ROWS, LENGTH), jnp.float32),
+            jax.ShapeDtypeStruct((STATIONS_DEV, PAIR_DEV), jnp.int32),
+            jax.ShapeDtypeStruct((STATIONS_DEV, PAIR_DEV), jnp.int32),
+        ),
+        in_specs=[HBM] * 7,
+        out_specs=(VMEM, VMEM, VMEM),
+        scratch_shapes=[
+            pltpu.SMEM((1,), jnp.int32),
+            pltpu.VMEM((3, STATIONS_DEV, EV_DEV), jnp.float32),
+            pltpu.VMEM((STATIONS_DEV, EV_DEV), jnp.float32),
+            pltpu.VMEM((1, PAIR_DEV), jnp.int32),
+            pltpu.VMEM((1, PAIR_DEV), jnp.int32),
+            pltpu.VMEM((STATIONS_DEV, PAIR_DEV), jnp.int32),
+            pltpu.SemaphoreType.DMA((7,)),
+        ],
+        compiler_params=PARAMS,
         name="pack",
     )(
         pair_live,
@@ -313,40 +394,68 @@
         travel_time,
         pair_first.reshape(1, PAIR_DEV),
         pair_second.reshape(1, PAIR_DEV),
-    )
-    from_left = passed_along(message, 1)
-    from_right = passed_along(message, -1)
-    refined_shift, block = pl.pallas_call(
+        pair_lag,
+    )
+
+
+def firsts(message):
+    toeplitz = jax.ShapeDtypeStruct((TRACES_DEV, EV_DEV * LAGS, SPAN), jnp.bfloat16)
+    return pl.pallas_call(
+        first_kernel,
+        out_shape=(toeplitz, toeplitz),
+        in_specs=[VMEM],
+        out_specs=(VMEM, VMEM),
+        compiler_params=PARAMS,
+        name="firsts",
+    )(message)
+
+
+def shifts(rows, lanes, message, from_mate, from_cross, pair_lag, high, low):
+    return pl.pallas_call(
         shift_kernel,
         out_shape=(
             jax.ShapeDtypeStruct((STATIONS_DEV, PAIR_DEV), jnp.float32),
             jax.ShapeDtypeStruct((ROWS, LANES), jnp.float32),
         ),
-        in_specs=[smem, smem] + [vmem] * 4,
-        out_specs=(vmem, vmem),
+        in_specs=[SMEM, SMEM] + [VMEM] * 6,
+        out_specs=(VMEM, VMEM),
         scratch_shapes=[
             pltpu.VMEM((TRACES_DEV * TRACE_ROWS + 2 * ROWS, LANES), jnp.float32),
             pltpu.VMEM((TRACES_DEV * PAIR_DEV * ROWS, LANES), jnp.float32),
-            pltpu.VMEM((EV_DEV * LAGS, SPAN), jnp.bfloat16),
-            pltpu.VMEM((EV_DEV * LAGS, SPAN), jnp.bfloat16),
         ],
-        compiler_params=params,
+        compiler_params=PARAMS,
         name="shifts",
-    )(pair_second, pair_lag, message, from_left, from_right, pair_lag)
+    )(rows, lanes, message, from_mate, from_cross, pair_lag, high, low)
+
+
+def solve(gathered):
+    return pl.pallas_call(
+        solve_kernel,
+        out_shape=jax.ShapeDtypeStruct((4, EV_DEV), jnp.float32),
+        in_specs=[VMEM],
+        out_specs=VMEM,
+        scratch_shapes=[pltpu.VMEM((ROWS * LANES, LANES), jnp.float32)],
+        compiler_params=PARAMS,
+        name="solve",
+    )(gathered)
+
+
+def body(traces, ray_slowness, travel_time, pair_first, pair_second, pair_lag, pair_live):
+    message, rows, lanes = pack(
+        traces, ray_slowness, travel_time, pair_first, pair_second, pair_lag, pair_live
+    )
+    from_cross = swapped(message, in_other_chip)
+    from_mate = swapped(message, in_other_core)
+    high, low = firsts(message)
+    refined_shift, block = shifts(
+        rows, lanes, message, from_mate, from_cross, pair_lag, high, low
+    )
     block = lax.psum(block, "x")
     chips = lax.axis_size("g")
     copies = jnp.broadcast_to(block[None], (chips, ROWS, LANES))
     gathered = lax.all_to_all(copies, "g", 0, 0, tiled=True)
     gathered = lax.all_gather(gathered, "c", axis=0)
-    location = pl.pallas_call(
-        solve_kernel,
-        out_shape=jax.ShapeDtypeStruct((4, EV_DEV), jnp.float32),
-        in_specs=[vmem],
-        out_specs=vmem,
-        scratch_shapes=[pltpu.VMEM((ROWS * LANES, LANES), jnp.float32)],
-        compiler_params=params,
-        name="solve",
-    )(gathered.reshape(2 * chips * ROWS, LANES))
+    location = solve(gathered.reshape(2 * chips * ROWS, LANES))
     return refined_shift, location
 
 

time: 72.7 us -> 69 us (0.949)
  waiting for transfers between devices: 3.99 us -> 0.01 us
  local copies, waits for them, and re-layouts: 2.32 us -> 5.95 us
  Pallas kernels: 13.5 us -> 11.9 us
  starting transfers between devices: 10.7 us -> 9.47 us
    ppermute x2, waiting for transfers between devices: 3.99 us -> 0.01 us  [swapped(): return lax.ppermute(block, ('g', 'c'), route)]
    unnamed x12 -> x14, local copies, waits for them, and re-layouts: 2.3 us -> 5.93 us
    pallas_call x3 -> x4, Pallas kernels: 13.5 us -> 11.9 us  [the longest x1 7.28 us: shifts(): pl.pallas_call(shift_kernel, out_shape=(jax.ShapeDtypeStruct((STATIONS_DE...]
    ppermute x2, starting transfers between devices: 10.7 us -> 9.47 us  [swapped(): return lax.ppermute(block, ('g', 'c'), route)]
    all_gather x1, blocking collectives: 7.55 us -> 6.77 us  [body(): gathered = lax.all_gather(gathered, 'c', axis=0)]
  transfers between devices with their start and end apart: 2 -> 2, of which waited for: 1 -> 0; matrix products, arithmetic and copies ran while one was open for 0% -> 0% of each run, Pallas kernels for 0% -> 3%
where the time goes in v2:
time: 69 us; the launch traced here: 68.7 us
  blocking collectives  40 us (58%)
  Pallas kernels  11.9 us (17%)
  starting transfers between devices  9.47 us (14%)
  local copies, waits for them, and re-layouts  5.95 us (9%)
  between operations  1.34 us (2%)
    all_to_all x1, blocking collectives, body(): gathered = lax.all_to_all(copies, 'g', 0, 0, tiled=True)  27.2 us
    ppermute x2, starting transfers between devices, swapped(): return lax.ppermute(block, ('g', 'c'), route)  9.47 us
    pallas_call x1, Pallas kernels, shifts(): pl.pallas_call(shift_kernel, out_shape=(jax.ShapeDtypeStruct((STATIONS_DE...  7.28 us
    all_gather x1, blocking collectives, body(): gathered = lax.all_gather(gathered, 'c', axis=0)  6.77 us
    psum x1, blocking collectives, body(): block = lax.psum(block, 'x')  5.97 us
    unnamed x14, local copies, waits for them, and re-layouts  5.93 us
    pallas_call x1, Pallas kernels, firsts(): pl.pallas_call(first_kernel, out_shape=(toeplitz, toeplitz), in_specs=[VM...  2.25 us
    pallas_call x1, Pallas kernels, solve(): pl.pallas_call(solve_kernel, out_shape=jax.ShapeDtypeStruct((4, EV_DEV),...  1.71 us
  transfers between devices with their start and end apart: 2, of which 0 were waited for; matrix products, arithmetic and copies ran while one was open for 0% of the time, Pallas kernels for 3%

profile of v2, /device:TPU:1, one launch (start us, length us, event | category | flops | bytes accessed | tf_op | source)
XLA Modules:
  0.0 68.7 jit_solution(8473452877974206505)
XLA Ops:
  1.3 0.0 copy-start.1
  1.3 1.0 %copy-done.1 = f32[3,3,8,1024]{3,2,1,0:T(8,128)S(1)} copy-done((f32[3,3,8,1024]{3,2,1,0:T(8,128)S(1)}, f32[3,3,8,1024]{3,2,1,0:T(8,128)}, u32[]{:S(2)}) %copy-start.1) | copy-done | bytes 294936
  2.2 0.0 copy-start.2
  2.2 0.7 copy-done.2
  2.9 0.0 copy-start.3
  2.9 0.7 %copy-done.3 = f32[3,3,8]{2,1,0:T(4,128)S(1)} copy-done((f32[3,3,8]{2,1,0:T(4,128)S(1)}, f32[3,3,8]{2,1,0:T(4,128)}, u32[]{:S(2)}) %copy-start.3) | copy-done | bytes 312
  3.6 0.0 copy-start.4
  3.6 0.7 copy-done.4
  4.3 0.0 copy-start.5
  4.3 0.7 copy-done.5
  5.0 0.7 copy-done.6
  5.6 0.7 pack.1
  6.3 4.6 %collective-permute-start.1 = (f32[10,8,1024]{2,1,0:T(8,128)S(1)}, f32[10,8,1024]{2,1,0:T(8,128)S(1)}, u32[]{:S(2)}, u32[]{:S(2)}) collective-permute-start(f32[10,8,1024]{2,1,0:T(8,128)S(1)} %get-tuple-element.11.own_ref), channel_id=1, source_target_pairs={{4,8},{8,4},{12,16},{16,12},{20,24},{24,20},{28,32},{32,28},{36,40... | collective-permute-start | bytes 983048 | tf_op jit(solution)/shard_map/ppermute | solution.py:352
  10.9 4.9 %collective-permute-start = (f32[10,8,1024]{2,1,0:T(8,128)S(1)}, f32[10,8,1024]{2,1,0:T(8,128)S(1)}, u32[]{:S(2)}, u32[]{:S(2)}) collective-permute-start(f32[10,8,1024]{2,1,0:T(8,128)S(1)} %get-tuple-element.11.own_ref), channel_id=1, source_target_pairs={{0,4},{4,0},{8,12},{12,8},{16,20},{20,16},{24,28},{28,24},{32,36},... | collective-permute-start | bytes 983048 | tf_op jit(solution)/shard_map/ppermute | solution.py:352
  15.8 2.2 %firsts.1 = (bf16[9,256,640]{2,1,0:T(8,128)(2,1)S(1)}, bf16[9,256,640]{2,1,0:T(8,128)(2,1)S(1)}) custom-call(f32[10,8,1024]{2,1,0:T(8,128)S(1)} %get-tuple-element.11.own_ref), custom_call_target="tpu_custom_call" | custom-call | tf_op jit(solution)/shard_map/firsts/pallas_call | solution.py:403
  18.0 0.0 copy-start
  18.0 1.6 %copy-done = bf16[9,256,640]{2,1,0:T(8,128)(2,1)} copy-done((bf16[9,256,640]{2,1,0:T(8,128)(2,1)}, bf16[9,256,640]{2,1,0:T(8,128)(2,1)S(1)}, u32[]{:S(2)}) %copy-start) | copy-done | bytes 2949144
  19.7 0.0 collective-permute-done.1.cross_ref
  19.7 0.0 collective-permute-done.mate_ref
  19.7 7.3 %shifts.1 = (f32[3,128]{1,0:T(4,128)}, f32[8,128]{1,0:T(8,128)S(1)}) custom-call(s32[3,128]{1,0:T(4,128)S(1)} %get-tuple-element.9.rows_ref, s32[3,128]{1,0:T(4,128)S(1)} %get-tuple-element.10.lanes_ref, f32[10,8,1024]{2,1,0:T(8,128)S(1)} %get-tuple-element.11.own_ref, f32[10,8,1024]{2,1,0:T(8,128)S(1)} %collective-permute-done.mate_ref, ...), custom_call_target="tpu_custom_call" | custom-call | tf_op jit(solution)/shard_map/shifts/pallas_call | solution.py:414
  26.9 6.0 %psum.7 = f32[8,128]{1,0:T(8,128)S(1)} all-reduce(f32[8,128]{1,0:T(8,128)S(1)} %get-tuple-element.15), channel_id=1, replica_groups=mesh['g'=64,'c'=2,'x'=4] {'x'}, use_global_device_ids=true, to_apply=%region_0.0 | all-reduce | flops 1024 | bytes 8192 | tf_op jit(solution)/shard_map/psum | solution.py:453
  32.9 27.2 %all_to_all.5 = f32[64,8,128]{2,1,0:T(8,128)S(1)} all-to-all(f32[64,8,128]{2,1,0:T(8,128)S(1)} %broadcast_in_dim.2), channel_id=1, replica_groups=mesh['g'=64,'c'=2,'x'=4] {'g'}, dimensions={0} | all-to-all | bytes 524288 | tf_op jit(solution)/shard_map/all_to_all | solution.py:456
  60.2 6.8 %all-gather = f32[128,8,128]{2,1,0:T(8,128)S(1)} all-gather(f32[64,8,128]{2,1,0:T(8,128)S(1)} %all_to_all.5), channel_id=2, replica_groups=mesh['g'=64,'c'=2,'x'=4] {'c'}, dimensions={0}, use_global_device_ids=true | all-gather | bytes 786432 | tf_op jit(solution)/shard_map/all_gather | solution.py:457
  67.0 1.7 %solve.1 = f32[4,8]{1,0:T(4,128)} custom-call(f32[1024,128]{1,0:T(8,128)S(1)} %bitcast.4), custom_call_target="tpu_custom_call" | custom-call | tf_op jit(solution)/shard_map/solve/pallas_call | solution.py:432
  (2 shorter events, 0.0 us)
Async XLA Ops:
  1.3 1.0 %copy-start.1 = (f32[3,3,8,1024]{3,2,1,0:T(8,128)S(1)}, f32[3,3,8,1024]{3,2,1,0:T(8,128)}, u32[]{:S(2)}) copy-start(f32[3,3,8,1024]{3,2,1,0:T(8,128)} %param.7) | copy-start | bytes 884740
  2.2 0.7 copy-start.2
  2.9 0.7 %copy-start.3 = (f32[3,3,8]{2,1,0:T(4,128)S(1)}, f32[3,3,8]{2,1,0:T(4,128)}, u32[]{:S(2)}) copy-start(f32[3,3,8]{2,1,0:T(4,128)} %slowness_ref.1) | copy-start | bytes 868
  3.6 0.7 copy-start.4
  4.3 0.7 copy-start.5
  5.0 0.7 copy-start.6
  6.3 13.4 %collective-permute-start.1 = (f32[10,8,1024]{2,1,0:T(8,128)S(1)}, f32[10,8,1024]{2,1,0:T(8,128)S(1)}, u32[]{:S(2)}, u32[]{:S(2)}) collective-permute-start(f32[10,8,1024]{2,1,0:T(8,128)S(1)} %get-tuple-element.11.own_ref), channel_id=1, source_target_pairs={{4,8},{8,4},{12,16},{16,12},{20,24},{24,20},{28,32},{32,28},{36,40... | collective-permute-start | bytes 983048 | tf_op jit(solution)/shard_map/ppermute | solution.py:352
  10.9 8.8 %collective-permute-start = (f32[10,8,1024]{2,1,0:T(8,128)S(1)}, f32[10,8,1024]{2,1,0:T(8,128)S(1)}, u32[]{:S(2)}, u32[]{:S(2)}) collective-permute-start(f32[10,8,1024]{2,1,0:T(8,128)S(1)} %get-tuple-element.11.own_ref), channel_id=1, source_target_pairs={{0,4},{4,0},{8,12},{12,8},{16,20},{20,16},{24,28},{28,24},{32,36},... | collective-permute-start | bytes 983048 | tf_op jit(solution)/shard_map/ppermute | solution.py:352
  18.0 1.6 %copy-start = (bf16[9,256,640]{2,1,0:T(8,128)(2,1)}, bf16[9,256,640]{2,1,0:T(8,128)(2,1)S(1)}, u32[]{:S(2)}) copy-start(bf16[9,256,640]{2,1,0:T(8,128)(2,1)S(1)} %get-tuple-element.13.low_ref) | copy-start | bytes 8847364

commit v3 on v2

v3 whole, which is shorter than its diff:
```python
import jax
import jax.numpy as jnp
from jax import lax
from jax.experimental import pallas as pl
from jax.experimental.pallas import tpu as pltpu
from jax.sharding import Mesh
from jax.sharding import PartitionSpec as P

LAGS = 32
LANES = 128
ROWS = 8
EV_DEV = 8
NEAR = 3 * EV_DEV
STATIONS_DEV = 3
TRACES_DEV = 9
LENGTH = 1024
CHUNKS = LENGTH // LANES
QUARTER = LENGTH // 4
WINDOW = LENGTH // 2
SPAN = WINDOW + LANES
SPAN_CHUNKS = SPAN // LANES
PAIR_DEV = 128
PART_ROWS = TRACES_DEV * EV_DEV * CHUNKS
VMEM_BYTES = 24 * 1024 * 1024
WHOLE_BYTES = 60 * 1024 * 1024
DEAD = -1000.0
PAYLOAD = 5 * LANES
SQUARE_AT = 4 * NEAR

eps_small = 1e-06
sample_step = 0.01
exact_mode = lax.Precision.HIGHEST
NT = (((1,), (1,)), ((), ()))
NN = (((1,), (0,)), ((), ()))


def device_index():
    return lax.axis_index("g") * 2 + lax.axis_index("c")


def dot_exact(left, right, dims):
    return lax.dot_general(
        left, right, dims, precision=exact_mode, preferred_element_type=jnp.float32
    )


def dot_bf16(left, right, dims):
    return lax.dot_general(left, right, dims, preferred_element_type=jnp.float32)


def count_place(event):
    return LANES + NEAR * event if event < 5 else 2 * LANES + NEAR * (event - 5)


def rate_place(group, station, q):
    index = (group * STATIONS_DEV + station) * 3 + q
    return 3 * LANES + 8 * index if index < 32 else 2 * LANES + 96 + 8 * (index - 32)


def dot_signs(left, signs, dims):
    high = left.astype(jnp.bfloat16)
    rest = left - high.astype(jnp.float32)
    middle = rest.astype(jnp.bfloat16)
    low = (rest - middle.astype(jnp.float32)).astype(jnp.bfloat16)
    rows = left.shape[0]
    parts = dot_bf16(jnp.concatenate([high, middle, low], axis=0), signs, dims)
    return parts[0:rows] + parts[rows : 2 * rows] + parts[2 * rows :]


def split_bf16(values):
    high = values.astype(jnp.bfloat16)
    low = (values - high.astype(jnp.float32)).astype(jnp.bfloat16)
    return high, low


def pack_kernel(
    live_ref,
    traces_ref,
    slowness_ref,
    time_ref,
    first_ref,
    second_ref,
    lag_ref,
    out_ref,
    traces,
    live,
    slowness,
    time,
    first,
    second,
    lag,
    aux,
    sems,
):
    pairs = [(traces_ref.at[pl.ds(3 * part, 3)], traces.at[pl.ds(3 * part, 3)]) for part in range(3)]
    pairs += [
        (live_ref, live),
        (slowness_ref, slowness),
        (time_ref, time),
        (first_ref, first),
        (second_ref, second),
        (lag_ref, lag),
    ]
    copies = [
        pltpu.make_async_copy(source, target, sems.at[at])
        for at, (source, target) in enumerate(pairs)
    ]
    moves = [
        pltpu.make_async_copy(traces.at[part], out_ref.at[part], sems.at[len(copies) + at])
        for at, part in enumerate([pl.ds(3 * third, 3) for third in range(3)])
    ]
    for copy in copies:
        copy.start()
    aux[...] = jnp.zeros((ROWS, LENGTH), jnp.float32)
    for copy in copies[3:]:
        copy.wait()
    base = device_index() * EV_DEV - EV_DEV
    slots = lax.broadcasted_iota(jnp.int32, (1, PAIR_DEV), 1)
    alive = slots < live[0]
    for row, ids in enumerate((first, second)):
        near = (ids[...] - base).astype(jnp.float32)
        aux[row : row + 1, 0:LANES] = jnp.where(alive, near, DEAD)
        aux[row : row + 1, 6 * LANES : 7 * LANES] = near
    aux[0:STATIONS_DEV, LANES : LANES + EV_DEV] = time[...]
    for q in range(3):
        lane = (2 + q) * LANES
        aux[0:STATIONS_DEV, lane : lane + EV_DEV] = slowness[q]
    aux[0:STATIONS_DEV, 5 * LANES : 6 * LANES] = lag[...].astype(jnp.float32)
    moves.append(pltpu.make_async_copy(aux, out_ref.at[TRACES_DEV], sems.at[len(copies) + 3]))
    moves[3].start()
    for third in range(3):
        copies[third].wait()
        moves[third].start()
    for move in moves:
        move.wait()


def first_kernel(own_ref, high_ref, low_ref, places_ref, pick_ref, rates_ref):
    for item in range(TRACES_DEV):
        window = own_ref[item, :, QUARTER : QUARTER + WINDOW]
        power = jnp.sum(window * window, axis=1, keepdims=True)
        window = window * lax.rsqrt(power + eps_small)
        padded = jnp.concatenate([window, jnp.zeros((EV_DEV, LANES), jnp.float32)], axis=1)
        for event in range(EV_DEV):
            wide = jnp.broadcast_to(padded[event : event + 1], (LAGS, SPAN))
            wide = pltpu.roll(wide, 0, 1, stride=1, stride_axis=0)
            high, low = split_bf16(wide)
            high_ref[item, pl.ds(event * LAGS, LAGS), :] = high
            low_ref[item, pl.ds(event * LAGS, LAGS), :] = low
    aux = own_ref[TRACES_DEV]
    first = aux[0:1, 6 * LANES : 7 * LANES].astype(jnp.int32)
    second = aux[1:2, 6 * LANES : 7 * LANES].astype(jnp.int32)
    begin = aux[0:STATIONS_DEV, 5 * LANES : 6 * LANES].astype(jnp.int32) + (QUARTER - LAGS // 2)
    side = lax.shift_right_arithmetic(second, 3)
    mate_side = 2 - 2 * lax.axis_index("c")
    far = jnp.logical_and(side != 1, side != mate_side)
    part = jnp.where(side == 1, 0, jnp.where(far, 2, 1))
    event = jnp.bitwise_and(second, EV_DEV - 1)
    rows = part * PART_ROWS + event * CHUNKS + lax.shift_right_arithmetic(begin, 7)
    upper = lax.broadcasted_iota(jnp.int32, (PAIR_DEV, PAIR_DEV), 0)
    lower = lax.broadcasted_iota(jnp.int32, (PAIR_DEV, PAIR_DEV), 1)
    ahead = (upper <= lower).astype(jnp.bfloat16)
    marked = jnp.broadcast_to(far.astype(jnp.float32), (ROWS, PAIR_DEV)).astype(jnp.bfloat16)
    place = dot_bf16(marked, ahead, NN)[0:1]
    place = jnp.where(far, place - 1.0, -1.0)
    hot = (upper.astype(jnp.float32) == place).astype(jnp.bfloat16)
    slots = lax.broadcasted_iota(jnp.int32, (ROWS, PAIR_DEV), 1).astype(jnp.bfloat16)
    listed = dot_bf16(slots, hot, NT)[0:1].astype(jnp.int32)
    count = jnp.sum(far.astype(jnp.float32), axis=1, keepdims=True).astype(jnp.int32)
    spare = lax.broadcasted_iota(jnp.int32, (1, PAIR_DEV), 1) >= count
    listed = jnp.where(spare, listed[:, 0:1], listed)
    places_ref[0:3, :] = rows
    places_ref[3:6, :] = jnp.bitwise_and(begin, LANES - 1)
    places_ref[6:7, :] = listed
    places_ref[7:8, :] = jnp.broadcast_to(count, (1, PAIR_DEV))
    ends = jnp.bitwise_and(first, EV_DEV - 1).astype(jnp.float32)
    column = jnp.transpose(jnp.broadcast_to(ends, (LANES, PAIR_DEV)))
    groups = lax.broadcasted_iota(jnp.int32, (PAIR_DEV, LANES), 1) // LAGS
    for half in range(2):
        mine = column == (groups + half * (LANES // LAGS)).astype(jnp.float32)
        pick_ref[:, half * LANES : (half + 1) * LANES] = mine.astype(jnp.float32)
    rates_ref[...] = jnp.zeros((1, PAYLOAD), jnp.float32)
    for station in range(STATIONS_DEV):
        for q in range(3):
            lane = (2 + q) * LANES
            own = aux[station : station + 1, lane : lane + EV_DEV]
            for group in range(4):
                at = rate_place(group, station, q)
                rates_ref[:, at : at + EV_DEV] = jnp.where(
                    lax.axis_index("x") == group, own, 0.0
                )


def fill_table(ref, table_ref, part):
    for item in range(TRACES_DEV):
        values = ref[item]
        power = jnp.sum(values * values, axis=1, keepdims=True)
        values = values * lax.rsqrt(power + eps_small)
        for chunk in range(CHUNKS):
            start = part * PART_ROWS + item * EV_DEV * CHUNKS + chunk
            table_ref[pl.ds(start, EV_DEV, stride=CHUNKS), :] = values[
                :, chunk * LANES : (chunk + 1) * LANES
            ]


def align(places_ref, table_ref, moved_ref, slot, offset):
    lane_ids = lax.broadcasted_iota(jnp.int32, (ROWS, LANES), 1)
    for station in range(STATIONS_DEV):
        row = places_ref[station, slot] - offset
        lane = places_ref[3 + station, slot]
        turn = jnp.bitwise_and(-lane, LANES - 1)
        keep = lane_ids >= lane
        for component in range(3):
            item = station * 3 + component
            at = item * EV_DEV * CHUNKS
            here = table_ref[pl.ds(row + at, ROWS), :]
            after = table_ref[pl.ds(row + (at + 1), ROWS), :]
            moved = pltpu.roll(jnp.where(keep, here, after), turn, 1)
            to = pl.multiple_of((item * PAIR_DEV + slot) * ROWS, ROWS)
            moved_ref[pl.ds(to, ROWS), :] = moved


def early_kernel(places_ref, own_ref, mate_ref, moved_ref, table_ref):
    table_ref[pl.ds(2 * PART_ROWS, PART_ROWS + 2 * ROWS), :] = jnp.zeros(
        (PART_ROWS + 2 * ROWS, LANES), jnp.float32
    )
    fill_table(own_ref, table_ref, 0)
    fill_table(mate_ref, table_ref, 1)

    def step(slot, carry):
        align(places_ref, table_ref, moved_ref, slot, 0)
        return carry

    lax.fori_loop(0, PAIR_DEV, step, 0, unroll=32)


def incidence(aux, offset):
    events = lax.broadcasted_iota(jnp.int32, (NEAR, PAIR_DEV), 0).astype(jnp.float32)
    starts = aux[0:1, 0:LANES] + offset
    ends = aux[1:2, 0:LANES] + offset
    return (events == starts).astype(jnp.float32) - (events == ends).astype(jnp.float32)


def near_block(left, own, right, part):
    lane = part * LANES
    return jnp.concatenate(
        [aux[0:STATIONS_DEV, lane : lane + EV_DEV] for aux in (left, own, right)], axis=1
    )


def late_kernel(
    places_in_ref,
    moved_in_ref,
    own_ref,
    mate_ref,
    cross_ref,
    high_ref,
    low_ref,
    pick_ref,
    rates_ref,
    shift_ref,
    block_ref,
    moved_ref,
    table_ref,
    places_ref,
    sem,
):
    del moved_in_ref
    fetch = pltpu.make_async_copy(places_in_ref, places_ref, sem)
    fetch.start()
    table_ref[pl.ds(PART_ROWS, 2 * ROWS), :] = jnp.zeros((2 * ROWS, LANES), jnp.float32)
    fill_table(cross_ref, table_ref, 0)
    fetch.wait()

    def step(index, carry):
        for turn in range(8):
            slot = places_ref[6, index * 8 + turn]
            align(places_ref, table_ref, moved_ref, slot, 2 * PART_ROWS)
        return carry

    lax.fori_loop(0, lax.shift_right_arithmetic(places_ref[7, 0] + 7, 3), step, 0)

    aux_own = own_ref[TRACES_DEV]
    even = lax.axis_index("c") == 0
    aux_left = jnp.where(even, cross_ref[TRACES_DEV], mate_ref[TRACES_DEV])
    aux_right = jnp.where(even, mate_ref[TRACES_DEV], cross_ref[TRACES_DEV])

    lane_ids = lax.broadcasted_iota(jnp.int32, (1, LANES), 1)
    centred = (lane_ids - LAGS // 2).astype(jnp.float32)
    weights = jnp.where(lane_ids < LAGS, centred, jnp.where(lane_ids < 2 * LAGS, 1.0, 0.0))
    folded = []
    for station in range(STATIONS_DEV):
        energy = jnp.zeros((PAIR_DEV, EV_DEV * LAGS), jnp.float32)
        for component in range(3):
            item = station * 3 + component
            pieces = [
                moved_ref[pl.ds(item * PAIR_DEV * ROWS + chunk, PAIR_DEV, stride=ROWS), :]
                for chunk in range(SPAN_CHUNKS)
            ]
            high, low = split_bf16(jnp.concatenate(pieces, axis=1))
            both = dot_bf16(jnp.concatenate([high, low], axis=0), high_ref[item], NT)
            xcorr = both[0:PAIR_DEV] + both[PAIR_DEV:] + dot_bf16(high, low_ref[item], NT)
            energy = energy + xcorr * xcorr
        energy = energy * pick_ref[...]
        energy = energy[:, 0:LANES] + energy[:, LANES:]
        energy = energy + pltpu.roll(energy, LANES // 2, 1)
        energy = energy + pltpu.roll(energy, LANES // 4, 1)
        folded.append(energy)
    pair = folded[0] * weights + folded[1] * pltpu.roll(weights, LANES // 2, 1)
    tables = [jnp.transpose(pair), jnp.transpose(folded[2] * weights)]
    station_shift = []
    for station in range(STATIONS_DEV):
        rows = tables[station // 2][(station % 2) * 2 * LAGS : (station % 2 + 1) * 2 * LAGS]
        above = jnp.sum(rows[0:LAGS], axis=0, keepdims=True)
        below = jnp.sum(rows[LAGS:], axis=0, keepdims=True)
        station_shift.append(above / (below + eps_small))
    slots_alive = (aux_own[0:1, 0:LANES] >= 0.0).astype(jnp.float32)
    shift = jnp.concatenate(station_shift, axis=0) * slots_alive
    shift_ref[...] = shift

    signs = incidence(aux_own, 0.0).astype(jnp.bfloat16)
    times = dot_signs(near_block(aux_left, aux_own, aux_right, 1), signs, NN)
    lags = aux_own[0:STATIONS_DEV, 5 * LANES : 6 * LANES]
    rhs = slots_alive * (sample_step * (lags + shift)) - times
    per_event = dot_signs(rhs, signs, NT)
    counts = dot_bf16(signs[EV_DEV : 2 * EV_DEV], signs, NT)
    for aux, offset in ((aux_left, -float(EV_DEV)), (aux_right, float(EV_DEV))):
        other = incidence(aux, offset).astype(jnp.bfloat16)
        counts = counts + dot_bf16(other[EV_DEV : 2 * EV_DEV], other, NT)
    counts = jnp.where(lax.axis_index("x") == 0, counts, 0.0)
    block_ref[...] = rates_ref[...]
    for event in range(EV_DEV):
        at = count_place(event)
        block_ref[:, at : at + NEAR] = counts[event : event + 1]
    for q in range(4):
        terms = per_event
        if q < 3:
            terms = terms * near_block(aux_left, aux_own, aux_right, 2 + q)
        block_ref[:, q * NEAR : (q + 1) * NEAR] = jnp.sum(terms, axis=0, keepdims=True)
    total = jnp.sum(jnp.sum(rhs * rhs, axis=1, keepdims=True), axis=0, keepdims=True)
    block_ref[:, SQUARE_AT : SQUARE_AT + 1] = total


def solve_kernel(gathered_ref, shift_ref, out_ref, shift_out_ref, rows_ref):
    shift_out_ref[...] = shift_ref[...]
    half = LANES // 2
    tables = []
    for row in range(PAYLOAD // LANES):
        for core in range(2):
            values = gathered_ref[pl.ds(core * half, half), row * LANES : (row + 1) * LANES]
            rows_ref[pl.ds(row * LANES + core, half, stride=2), :] = values
        tables.append(jnp.transpose(rows_ref[pl.ds(row * LANES, LANES), :]))

    def read(at):
        return tables[at // LANES][at % LANES : at % LANES + 8]

    def along(lower, own, upper):
        return own + pltpu.roll(upper, 1, 1) + pltpu.roll(lower, LANES - 1, 1)

    back = [along(*[read(q * NEAR + 8 * side) for side in range(3)]) for q in range(4)]
    counts = [[read(count_place(a) + 8 * side) for side in range(3)] for a in range(EV_DEV)]
    deriv = [
        [read(rate_place(group, station, q)) for q in range(3)]
        for group in range(4)
        for station in range(STATIONS_DEV)
    ]

    def total(values):
        return jnp.sum(jnp.sum(values, axis=1, keepdims=True), axis=0, keepdims=True)

    def inner(left, right):
        terms = left[0] * right[0]
        for q in range(1, 4):
            terms = terms + left[q] * right[q]
        return total(terms)

    def normal(model):
        result = [jnp.zeros((EV_DEV, LANES), jnp.float32) for _ in range(4)]
        for rates in deriv:
            data = model[3]
            for q in range(3):
                data = data + rates[q] * model[q]
            sides = [None, None, None]
            for a in range(EV_DEV):
                row = jnp.broadcast_to(data[a : a + 1], (EV_DEV, LANES))
                for side in range(3):
                    term = counts[a][side] * row
                    sides[side] = term if a == 0 else sides[side] + term
            mixed = along(*sides)
            for q in range(3):
                result[q] = result[q] + rates[q] * mixed
            result[3] = result[3] + mixed
        return result

    rhs_square = total(tables[0][SQUARE_AT : SQUARE_AT + 1])
    beta = jnp.sqrt(rhs_square + eps_small)
    unit_square = rhs_square / (beta * beta)
    adjoint = [value / beta for value in back]
    alpha = jnp.sqrt(inner(adjoint, adjoint) + eps_small)
    model = [value / alpha for value in adjoint]
    search = model
    location = [jnp.zeros((EV_DEV, LANES), jnp.float32) for _ in range(4)]
    phi_bar = beta
    rho_bar = alpha
    for turn in range(2):
        normal_model = normal(model)
        square = inner(model, normal_model) - 2.0 * alpha * inner(model, adjoint)
        square = jnp.maximum(square + alpha * alpha * unit_square, 0.0)
        beta = jnp.sqrt(square + eps_small)
        rho = jnp.sqrt(rho_bar * rho_bar + beta * beta)
        cosine = rho_bar / rho
        sine = beta / rho
        phi = cosine * phi_bar
        phi_bar = sine * phi_bar
        step = phi / rho
        location = [location[q] + step * search[q] for q in range(4)]
        if turn == 0:
            unit_square = square / (beta * beta)
            adjoint = [(normal_model[q] - alpha * adjoint[q]) / beta for q in range(4)]
            vector = [adjoint[q] - beta * model[q] for q in range(4)]
            alpha = jnp.sqrt(inner(vector, vector) + eps_small)
            model = [value / alpha for value in vector]
            theta = sine * alpha
            rho_bar = -cosine * alpha
            search = [model[q] - theta / rho * search[q] for q in range(4)]

    lanes = lax.broadcasted_iota(jnp.int32, (ROWS, LANES), 1)
    mine = (lanes == device_index()).astype(jnp.float32)
    own = dot_exact(mine, jnp.concatenate(location, axis=0), NT)
    for q in range(4):
        out_ref[q : q + 1, :] = own[0:1, q * EV_DEV : (q + 1) * EV_DEV]


def swapped(block, partner):
    count = lax.axis_size("g") * lax.axis_size("c")
    route = [(i, partner(i)) for i in range(count) if 0 <= partner(i) < count]
    return lax.ppermute(block, ("g", "c"), route)


def in_other_core(index):
    return index + 1 - 2 * (index % 2)


def in_other_chip(index):
    return index - 1 + 2 * (index % 2)


VMEM = pl.BlockSpec(memory_space=pltpu.VMEM)
SMEM = pl.BlockSpec(memory_space=pltpu.SMEM)
HBM = pl.BlockSpec(memory_space=pltpu.HBM)
PARAMS = pltpu.CompilerParams(vmem_limit_bytes=VMEM_BYTES)
WHOLE_VMEM = pltpu.CompilerParams(vmem_limit_bytes=WHOLE_BYTES)


def pack(traces, ray_slowness, travel_time, pair_first, pair_second, pair_lag, pair_live):
    return pl.pallas_call(
        pack_kernel,
        out_shape=jax.ShapeDtypeStruct((TRACES_DEV + 1, ROWS, LENGTH), jnp.float32),
        in_specs=[HBM] * 7,
        out_specs=HBM,
        scratch_shapes=[
            pltpu.VMEM((TRACES_DEV, EV_DEV, LENGTH), jnp.float32),
            pltpu.SMEM((1,), jnp.int32),
            pltpu.VMEM((3, STATIONS_DEV, EV_DEV), jnp.float32),
            pltpu.VMEM((STATIONS_DEV, EV_DEV), jnp.float32),
            pltpu.VMEM((1, PAIR_DEV), jnp.int32),
            pltpu.VMEM((1, PAIR_DEV), jnp.int32),
            pltpu.VMEM((STATIONS_DEV, PAIR_DEV), jnp.int32),
            pltpu.VMEM((ROWS, LENGTH), jnp.float32),
            pltpu.SemaphoreType.DMA((13,)),
        ],
        compiler_params=WHOLE_VMEM,
        name="pack",
    )(
        pair_live,
        traces.reshape(TRACES_DEV, EV_DEV, LENGTH),
        ray_slowness,
        travel_time,
        pair_first.reshape(1, PAIR_DEV),
        pair_second.reshape(1, PAIR_DEV),
        pair_lag,
    )


def firsts(message):
    toeplitz = jax.ShapeDtypeStruct((TRACES_DEV, EV_DEV * LAGS, SPAN), jnp.bfloat16)
    return pl.pallas_call(
        first_kernel,
        out_shape=(
            toeplitz,
            toeplitz,
            jax.ShapeDtypeStruct((ROWS, PAIR_DEV), jnp.int32),
            jax.ShapeDtypeStruct((PAIR_DEV, EV_DEV * LAGS), jnp.float32),
            jax.ShapeDtypeStruct((1, PAYLOAD), jnp.float32),
        ),
        in_specs=[VMEM],
        out_specs=(VMEM,) * 5,
        compiler_params=PARAMS,
        name="firsts",
    )(message)


MOVED = jax.ShapeDtypeStruct((TRACES_DEV * PAIR_DEV * ROWS, LANES), jnp.float32)


def early(places, message, from_mate):
    return pl.pallas_call(
        early_kernel,
        out_shape=MOVED,
        in_specs=[SMEM, VMEM, VMEM],
        out_specs=VMEM,
        scratch_shapes=[pltpu.VMEM((3 * PART_ROWS + 2 * ROWS, LANES), jnp.float32)],
        compiler_params=PARAMS,
        name="early",
    )(places, message, from_mate)


def late(places, moved, message, from_mate, from_cross, high, low, pick, rates):
    refined_shift, block, _ = pl.pallas_call(
        late_kernel,
        out_shape=(
            jax.ShapeDtypeStruct((STATIONS_DEV, PAIR_DEV), jnp.float32),
            jax.ShapeDtypeStruct((1, PAYLOAD), jnp.float32),
            MOVED,
        ),
        in_specs=[VMEM] * 9,
        out_specs=(VMEM, VMEM, VMEM),
        scratch_shapes=[
            pltpu.VMEM((PART_ROWS + 2 * ROWS, LANES), jnp.float32),
            pltpu.SMEM((ROWS, PAIR_DEV), jnp.int32),
            pltpu.SemaphoreType.DMA,
        ],
        input_output_aliases={1: 2},
        compiler_params=PARAMS,
        name="late",
    )(places, moved, message, from_mate, from_cross, high, low, pick, rates)
    return refined_shift, block


def solve(gathered, shift):
    return pl.pallas_call(
        solve_kernel,
        out_shape=(
            jax.ShapeDtypeStruct((4, EV_DEV), jnp.float32),
            jax.ShapeDtypeStruct((STATIONS_DEV, PAIR_DEV), jnp.float32),
        ),
        in_specs=[VMEM, VMEM],
        out_specs=(VMEM, VMEM),
        scratch_shapes=[pltpu.VMEM((PAYLOAD, LANES), jnp.float32)],
        compiler_params=PARAMS,
        name="solve",
    )(gathered, shift)


def body(traces, ray_slowness, travel_time, pair_first, pair_second, pair_lag, pair_live):
    message = pack(
        traces, ray_slowness, travel_time, pair_first, pair_second, pair_lag, pair_live
    )
    from_cross = swapped(message, in_other_chip)
    from_mate = swapped(message, in_other_core)
    high, low, places, pick, rates = firsts(message)
    moved = early(places, message, from_mate)
    shift, block = late(
        places, moved, message, from_mate, from_cross, high, low, pick, rates
    )
    block = lax.psum(block, "x")
    chips = lax.axis_size("g")
    copies = jnp.broadcast_to(block, (chips, PAYLOAD))
    gathered = lax.all_to_all(copies, "g", 0, 0, tiled=True)
    gathered = lax.all_gather(gathered, "c", axis=0)
    location, refined_shift = solve(gathered.reshape(2 * chips, PAYLOAD), shift)
    return refined_shift, location


def solution(mesh):
    ev, st = mesh.devices.shape
    fine = Mesh(mesh.devices.reshape(ev // 2, 2, st), ("g", "c", "x"))
    event_axes = ("g", "c")
    in_specs = (
        P("x", None, event_axes, None),
        P(None, "x", event_axes),
        P("x", event_axes),
        P(event_axes),
        P(event_axes),
        P("x", event_axes),
        P(event_axes),
    )
    out_specs = (P("x", event_axes), P(None, event_axes))
    return jax.shard_map(body, mesh=fine, in_specs=in_specs, out_specs=out_specs, check_vma=False)
```

time: 69 us -> 63.8 us (0.925)
  local copies, waits for them, and re-layouts: 5.95 us -> 1.08 us
  blocking collectives: 40 us -> 37.3 us
  starting transfers between devices: 9.47 us -> 10.7 us
  waiting for transfers between devices: 0.01 us -> 1.07 us
    unnamed x14 -> x4, local copies, waits for them, and re-layouts: 5.93 us -> 0.98 us
    all_to_all x1, blocking collectives: 27.2 us -> 25.4 us  [body(): gathered = lax.all_to_all(copies, 'g', 0, 0, tiled=True)]
    ppermute x2, starting transfers between devices: 9.47 us -> 10.7 us  [swapped(): return lax.ppermute(block, ('g', 'c'), route)]
    ppermute x2, waiting for transfers between devices: 0.01 us -> 1.07 us  [swapped(): return lax.ppermute(block, ('g', 'c'), route)]
    all_gather x1, blocking collectives: 6.77 us -> 5.93 us  [body(): gathered = lax.all_gather(gathered, 'c', axis=0)]
    pallas_call x4 -> x5, Pallas kernels: 11.9 us -> 12 us  [the longest x1 3.96 us: late(): pl.pallas_call(late_kernel, out_shape=(jax.ShapeDtypeStruct((STATIONS_DEV...]
  transfers between devices with their start and end apart: 2 -> 2, of which waited for: 0 -> 1; matrix products, arithmetic and copies ran while one was open for 0% -> 0% of each run, Pallas kernels for 3% -> 7%
where the time goes in v3:
time: 63.8 us; the launch traced here: 63.6 us
  blocking collectives  37.3 us (58%)
  Pallas kernels  12 us (19%)
  starting transfers between devices  10.7 us (17%)
  between operations  1.35 us (2%)
  local copies, waits for them, and re-layouts  1.08 us (2%)
  waiting for transfers between devices  1.07 us (2%)
    all_to_all x1, blocking collectives, body(): gathered = lax.all_to_all(copies, 'g', 0, 0, tiled=True)  25.4 us
    ppermute x2, starting transfers between devices, swapped(): return lax.ppermute(block, ('g', 'c'), route)  10.7 us
    psum x1, blocking collectives, body(): block = lax.psum(block, 'x')  6.01 us
    all_gather x1, blocking collectives, body(): gathered = lax.all_gather(gathered, 'c', axis=0)  5.93 us
    pallas_call x1, Pallas kernels, late(): pl.pallas_call(late_kernel, out_shape=(jax.ShapeDtypeStruct((STATIONS_DEV...  3.96 us
    pallas_call x1, Pallas kernels, firsts(): pl.pallas_call(first_kernel, out_shape=(toeplitz, toeplitz, jax.ShapeDtyp...  2.32 us
    pallas_call x1, Pallas kernels, early(): pl.pallas_call(early_kernel, out_shape=MOVED, in_specs=[SMEM, VMEM, VMEM]...  2.28 us
    pallas_call x1, Pallas kernels, solve(): pl.pallas_call(solve_kernel, out_shape=(jax.ShapeDtypeStruct((4, EV_DEV),...  1.74 us
  transfers between devices with their start and end apart: 2, of which 1 were waited for; matrix products, arithmetic and copies ran while one was open for 0% of the time, Pallas kernels for 7%

profile of v3, /device:TPU:1, one launch (start us, length us, event | category | flops | bytes accessed | tf_op | source)
XLA Modules:
  0.0 63.6 jit_solution(10153347087899433652)
XLA Ops:
  1.3 1.7 %pack.1.own_ref = f32[10,8,1024]{2,1,0:T(8,128)} custom-call(s32[1]{0:T(128)S(6)} %copy.12.live_ref, f32[9,8,1024]{2,1,0:T(8,128)} %bitcast.5, f32[3,3,8]{2,1,0:T(4,128)} %slowness_ref.1, f32[3,8]{1,0:T(4,128)} %time_ref.1, s32[1,128]{1,0:T(1,128)} %bitcast.6, s32[1,128]{1,0:T(1,128)} %bitcast.7, s32[3,128]{1,0:T(4,128)} %lag_ref.1), custom_call_target="tpu_custom_call" | custom-call | tf_op jit(solution)/shard_map/pack/pallas_call | solution.py:456
  3.0 8.8 %collective-permute-start = (f32[10,8,1024]{2,1,0:T(8,128)}, f32[10,8,1024]{2,1,0:T(8,128)S(1)}, u32[]{:S(2)}, u32[]{:S(2)}) collective-permute-start(f32[10,8,1024]{2,1,0:T(8,128)} %pack.1.own_ref), channel_id=1, source_target_pairs={{0,4},{4,0},{8,12},{12,8},{16,20},{20,16},{24,28},{28,24},{32,36},... | collective-permute-start | bytes 983048 | tf_op jit(solution)/shard_map/ppermute | solution.py:437
  11.8 1.9 %collective-permute-start.1 = (f32[10,8,1024]{2,1,0:T(8,128)}, f32[10,8,1024]{2,1,0:T(8,128)S(1)}, u32[]{:S(2)}, u32[]{:S(2)}) collective-permute-start(f32[10,8,1024]{2,1,0:T(8,128)} %pack.1.own_ref), channel_id=1, source_target_pairs={{4,8},{8,4},{12,16},{16,12},{20,24},{24,20},{28,32},{32,28},{36,40... | collective-permute-start | bytes 983048 | tf_op jit(solution)/shard_map/ppermute | solution.py:437
  13.7 0.0 copy-start
  13.7 1.0 %copy-done = f32[10,8,1024]{2,1,0:T(8,128)S(1)} copy-done((f32[10,8,1024]{2,1,0:T(8,128)S(1)}, f32[10,8,1024]{2,1,0:T(8,128)}, u32[]{:S(2)}) %copy-start) | copy-done | bytes 327704
  14.7 0.0 copy-start.1
  14.7 2.3 %firsts.1 = (bf16[9,256,640]{2,1,0:T(8,128)(2,1)S(1)}, bf16[9,256,640]{2,1,0:T(8,128)(2,1)S(1)}, s32[8,128]{1,0:T(8,128)S(1)}, f32[128,256]{1,0:T(8,128)S(1)}, f32[1,640]{1,0:T(1,128)S(1)}) custom-call(f32[10,8,1024]{2,1,0:T(8,128)S(1)} %copy-done), custom_call_target="tpu_custom_call" | custom-call | tf_op jit(solution)/shard_map/firsts/pallas_call | solution.py:487
  17.1 0.0 collective-permute-done.mate_ref
  17.1 2.3 %early.1.moved_in_ref = f32[9216,128]{1,0:T(8,128)S(1)} custom-call(s32[8,128]{1,0:T(8,128)S(1)} %get-tuple-element.11.places_ref.places_in_ref, f32[10,8,1024]{2,1,0:T(8,128)S(1)} %copy-done, f32[10,8,1024]{2,1,0:T(8,128)S(1)} %collective-permute-done.mate_ref), custom_call_target="tpu_custom_call" | custom-call | tf_op jit(solution)/shard_map/early/pallas_call | solution.py:507
  19.3 1.1 %collective-permute-done.1.cross_ref = f32[10,8,1024]{2,1,0:T(8,128)S(1)} collective-permute-done((f32[10,8,1024]{2,1,0:T(8,128)}, f32[10,8,1024]{2,1,0:T(8,128)S(1)}, u32[]{:S(2)}, u32[]{:S(2)}) %collective-permute-start.1) | collective-permute-done | bytes 327712 | tf_op jit(solution)/shard_map/ppermute | solution.py:437
  20.4 0.0 copy-done.1
  20.4 4.0 %late.1 = (f32[3,128]{1,0:T(4,128)S(1)}, f32[1,640]{1,0:T(1,128)S(1)}, f32[9216,128]{1,0:T(8,128)S(1)}) custom-call(s32[8,128]{1,0:T(8,128)S(1)} %get-tuple-element.11.places_ref.places_in_ref, f32[9216,128]{1,0:T(8,128)S(1)} %early.1.moved_in_ref, f32[10,8,1024]{2,1,0:T(8,128)S(1)} %copy-done.1, ...), custom_call_target="tpu_custom_call", output_to_operand_aliasing={{2}: (1, {})} | custom-call | tf_op jit(solution)/shard_map/late/pallas_call | solution.py:519
  24.4 6.0 %psum.10 = f32[640]{0:T(1024)S(1)} all-reduce(f32[640]{0:T(1024)S(1)} %reduce), channel_id=1, replica_groups=mesh['g'=64,'c'=2,'x'=4] {'x'}, use_global_device_ids=true, to_apply=%region_0.0 | all-reduce | flops 640 | bytes 5120 | tf_op jit(solution)/shard_map/psum | solution.py:566
  30.4 0.1 broadcast_in_dim.2
  30.5 25.4 %all_to_all.6 = f32[64,1,640]{2,1,0:T(1,128)S(1)} all-to-all(f32[64,1,640]{2,1,0:T(1,128)S(1)} %broadcast_in_dim.2), channel_id=1, replica_groups=mesh['g'=64,'c'=2,'x'=4] {'g'}, dimensions={0} | all-to-all | bytes 327680 | tf_op jit(solution)/shard_map/all_to_all | solution.py:569
  55.9 5.9 %all-gather = f32[128,1,640]{2,0,1:T(8,128)S(1)} all-gather(f32[64,1,640]{2,0,1:T(8,128)S(1)} %copy.10), channel_id=2, replica_groups=mesh['g'=64,'c'=2,'x'=4] {'c'}, dimensions={0}, use_global_device_ids=true | all-gather | bytes 491520 | tf_op jit(solution)/shard_map/all_gather | solution.py:570
  61.8 1.7 %solve.1 = (f32[4,8]{1,0:T(4,128)}, f32[3,128]{1,0:T(4,128)}) custom-call(f32[128,640]{1,0:T(8,128)S(1)} %bitcast.4, f32[3,128]{1,0:T(4,128)S(1)} %get-tuple-element.17.shift_ref), custom_call_target="tpu_custom_call" | custom-call | tf_op jit(solution)/shard_map/solve/pallas_call | solution.py:541
  (2 shorter events, 0.0 us)
Async XLA Ops:
  3.0 14.0 %collective-permute-start = (f32[10,8,1024]{2,1,0:T(8,128)}, f32[10,8,1024]{2,1,0:T(8,128)S(1)}, u32[]{:S(2)}, u32[]{:S(2)}) collective-permute-start(f32[10,8,1024]{2,1,0:T(8,128)} %pack.1.own_ref), channel_id=1, source_target_pairs={{0,4},{4,0},{8,12},{12,8},{16,20},{20,16},{24,28},{28,24},{32,36},... | collective-permute-start | bytes 983048 | tf_op jit(solution)/shard_map/ppermute | solution.py:437
  11.8 8.6 %collective-permute-start.1 = (f32[10,8,1024]{2,1,0:T(8,128)}, f32[10,8,1024]{2,1,0:T(8,128)S(1)}, u32[]{:S(2)}, u32[]{:S(2)}) collective-permute-start(f32[10,8,1024]{2,1,0:T(8,128)} %pack.1.own_ref), channel_id=1, source_target_pairs={{4,8},{8,4},{12,16},{16,12},{20,24},{24,20},{28,32},{32,28},{36,40... | collective-permute-start | bytes 983048 | tf_op jit(solution)/shard_map/ppermute | solution.py:437
  13.7 1.0 %copy-start = (f32[10,8,1024]{2,1,0:T(8,128)S(1)}, f32[10,8,1024]{2,1,0:T(8,128)}, u32[]{:S(2)}) copy-start(f32[10,8,1024]{2,1,0:T(8,128)} %pack.1.own_ref) | copy-start | bytes 983044
  14.7 5.7 %copy-start.1 = (f32[10,8,1024]{2,1,0:T(8,128)S(1)}, f32[10,8,1024]{2,1,0:T(8,128)}, u32[]{:S(2)}) copy-start(f32[10,8,1024]{2,1,0:T(8,128)} %pack.1.own_ref) | copy-start | bytes 983044

commit v4 on v3

--- a/solution.py
+++ b/solution.py
@@ -22,7 +22,6 @@
 PAIR_DEV = 128
 PART_ROWS = TRACES_DEV * EV_DEV * CHUNKS
 VMEM_BYTES = 24 * 1024 * 1024
-WHOLE_BYTES = 60 * 1024 * 1024
 DEAD = -1000.0
 PAYLOAD = 5 * LANES
 SQUARE_AT = 4 * NEAR
@@ -82,19 +81,15 @@
     second_ref,
     lag_ref,
     out_ref,
-    traces,
-    live,
     slowness,
     time,
     first,
     second,
     lag,
-    aux,
     sems,
 ):
-    pairs = [(traces_ref.at[pl.ds(3 * part, 3)], traces.at[pl.ds(3 * part, 3)]) for part in range(3)]
-    pairs += [
-        (live_ref, live),
+    pairs = [
+        (traces_ref, out_ref.at[pl.ds(0, TRACES_DEV)]),
         (slowness_ref, slowness),
         (time_ref, time),
         (first_ref, first),
@@ -105,18 +100,15 @@
         pltpu.make_async_copy(source, target, sems.at[at])
         for at, (source, target) in enumerate(pairs)
     ]
-    moves = [
-        pltpu.make_async_copy(traces.at[part], out_ref.at[part], sems.at[len(copies) + at])
-        for at, part in enumerate([pl.ds(3 * third, 3) for third in range(3)])
-    ]
     for copy in copies:
         copy.start()
+    aux = out_ref.at[TRACES_DEV]
     aux[...] = jnp.zeros((ROWS, LENGTH), jnp.float32)
-    for copy in copies[3:]:
+    for copy in copies[1:]:
         copy.wait()
     base = device_index() * EV_DEV - EV_DEV
     slots = lax.broadcasted_iota(jnp.int32, (1, PAIR_DEV), 1)
-    alive = slots < live[0]
+    alive = slots < live_ref[0]
     for row, ids in enumerate((first, second)):
         near = (ids[...] - base).astype(jnp.float32)
         aux[row : row + 1, 0:LANES] = jnp.where(alive, near, DEAD)
@@ -126,13 +118,7 @@
         lane = (2 + q) * LANES
         aux[0:STATIONS_DEV, lane : lane + EV_DEV] = slowness[q]
     aux[0:STATIONS_DEV, 5 * LANES : 6 * LANES] = lag[...].astype(jnp.float32)
-    moves.append(pltpu.make_async_copy(aux, out_ref.at[TRACES_DEV], sems.at[len(copies) + 3]))
-    moves[3].start()
-    for third in range(3):
-        copies[third].wait()
-        moves[third].start()
-    for move in moves:
-        move.wait()
+    copies[0].wait()
 
 
 def first_kernel(own_ref, high_ref, low_ref, places_ref, pick_ref, rates_ref):
@@ -153,8 +139,10 @@
     begin = aux[0:STATIONS_DEV, 5 * LANES : 6 * LANES].astype(jnp.int32) + (QUARTER - LAGS // 2)
     side = lax.shift_right_arithmetic(second, 3)
     mate_side = 2 - 2 * lax.axis_index("c")
-    far = jnp.logical_and(side != 1, side != mate_side)
-    part = jnp.where(side == 1, 0, jnp.where(far, 2, 1))
+    away = jnp.logical_and(side != 1, side != mate_side)
+    part = jnp.where(side == 1, 0, jnp.where(away, 2, 1))
+    alive = aux[0:1, 0:LANES] >= 0.0
+    far = jnp.logical_and(away, alive)
     event = jnp.bitwise_and(second, EV_DEV - 1)
     rows = part * PART_ROWS + event * CHUNKS + lax.shift_right_arithmetic(begin, 7)
     upper = lax.broadcasted_iota(jnp.int32, (PAIR_DEV, PAIR_DEV), 0)
@@ -172,7 +160,10 @@
     places_ref[0:3, :] = rows
     places_ref[3:6, :] = jnp.bitwise_and(begin, LANES - 1)
     places_ref[6:7, :] = listed
-    places_ref[7:8, :] = jnp.broadcast_to(count, (1, PAIR_DEV))
+    live_count = jnp.sum(alive.astype(jnp.float32), axis=1, keepdims=True).astype(jnp.int32)
+    places_ref[7:8, :] = jnp.where(
+        lax.broadcasted_iota(jnp.int32, (1, PAIR_DEV), 1) == 0, count, live_count
+    )
     ends = jnp.bitwise_and(first, EV_DEV - 1).astype(jnp.float32)
     column = jnp.transpose(jnp.broadcast_to(ends, (LANES, PAIR_DEV)))
     groups = lax.broadcasted_iota(jnp.int32, (PAIR_DEV, LANES), 1) // LAGS
@@ -220,18 +211,20 @@
             moved_ref[pl.ds(to, ROWS), :] = moved
 
 
-def early_kernel(places_ref, own_ref, mate_ref, moved_ref, table_ref):
+def early_kernel(places_ref, chip_ref, moved_ref, table_ref):
     table_ref[pl.ds(2 * PART_ROWS, PART_ROWS + 2 * ROWS), :] = jnp.zeros(
         (PART_ROWS + 2 * ROWS, LANES), jnp.float32
     )
-    fill_table(own_ref, table_ref, 0)
-    fill_table(mate_ref, table_ref, 1)
-
-    def step(slot, carry):
-        align(places_ref, table_ref, moved_ref, slot, 0)
+    core = lax.axis_index("c")
+    fill_table(chip_ref.at[core], table_ref, 0)
+    fill_table(chip_ref.at[1 - core], table_ref, 1)
+
+    def step(index, carry):
+        for turn in range(16):
+            align(places_ref, table_ref, moved_ref, index * 16 + turn, 0)
         return carry
 
-    lax.fori_loop(0, PAIR_DEV, step, 0, unroll=32)
+    lax.fori_loop(0, lax.shift_right_arithmetic(places_ref[7, 1] + 15, 4), step, 0)
 
 
 def incidence(aux, offset):
@@ -251,8 +244,7 @@
 def late_kernel(
     places_in_ref,
     moved_in_ref,
-    own_ref,
-    mate_ref,
+    chip_ref,
     cross_ref,
     high_ref,
     low_ref,
@@ -280,10 +272,10 @@
 
     lax.fori_loop(0, lax.shift_right_arithmetic(places_ref[7, 0] + 7, 3), step, 0)
 
-    aux_own = own_ref[TRACES_DEV]
-    even = lax.axis_index("c") == 0
-    aux_left = jnp.where(even, cross_ref[TRACES_DEV], mate_ref[TRACES_DEV])
-    aux_right = jnp.where(even, mate_ref[TRACES_DEV], cross_ref[TRACES_DEV])
+    core = lax.axis_index("c")
+    aux_own = chip_ref[core, TRACES_DEV]
+    aux_left = jnp.where(core == 0, cross_ref[TRACES_DEV], chip_ref[0, TRACES_DEV])
+    aux_right = jnp.where(core == 0, chip_ref[1, TRACES_DEV], cross_ref[TRACES_DEV])
 
     lane_ids = lax.broadcasted_iota(jnp.int32, (1, LANES), 1)
     centred = (lane_ids - LAGS // 2).astype(jnp.float32)
@@ -314,14 +306,14 @@
         above = jnp.sum(rows[0:LAGS], axis=0, keepdims=True)
         below = jnp.sum(rows[LAGS:], axis=0, keepdims=True)
         station_shift.append(above / (below + eps_small))
-    slots_alive = (aux_own[0:1, 0:LANES] >= 0.0).astype(jnp.float32)
-    shift = jnp.concatenate(station_shift, axis=0) * slots_alive
+    alive = aux_own[0:1, 0:LANES] >= 0.0
+    shift = jnp.where(alive, jnp.concatenate(station_shift, axis=0), 0.0)
     shift_ref[...] = shift
 
     signs = incidence(aux_own, 0.0).astype(jnp.bfloat16)
     times = dot_signs(near_block(aux_left, aux_own, aux_right, 1), signs, NN)
     lags = aux_own[0:STATIONS_DEV, 5 * LANES : 6 * LANES]
-    rhs = slots_alive * (sample_step * (lags + shift)) - times
+    rhs = jnp.where(alive, sample_step * (lags + shift), 0.0) - times
     per_event = dot_signs(rhs, signs, NT)
     counts = dot_bf16(signs[EV_DEV : 2 * EV_DEV], signs, NT)
     for aux, offset in ((aux_left, -float(EV_DEV)), (aux_right, float(EV_DEV))):
@@ -431,48 +423,21 @@
         out_ref[q : q + 1, :] = own[0:1, q * EV_DEV : (q + 1) * EV_DEV]
 
 
-def swapped(block, partner):
+def from_other_chip(block):
     count = lax.axis_size("g") * lax.axis_size("c")
-    route = [(i, partner(i)) for i in range(count) if 0 <= partner(i) < count]
+    partners = [(i, i - 1 + 2 * (i % 2)) for i in range(count)]
+    route = [(i, other) for i, other in partners if 0 <= other < count]
     return lax.ppermute(block, ("g", "c"), route)
-
-
-def in_other_core(index):
-    return index + 1 - 2 * (index % 2)
-
-
-def in_other_chip(index):
-    return index - 1 + 2 * (index % 2)
 
 
 VMEM = pl.BlockSpec(memory_space=pltpu.VMEM)
 SMEM = pl.BlockSpec(memory_space=pltpu.SMEM)
 HBM = pl.BlockSpec(memory_space=pltpu.HBM)
 PARAMS = pltpu.CompilerParams(vmem_limit_bytes=VMEM_BYTES)
-WHOLE_VMEM = pltpu.CompilerParams(vmem_limit_bytes=WHOLE_BYTES)
 
 
 def pack(traces, ray_slowness, travel_time, pair_first, pair_second, pair_lag, pair_live):
-    return pl.pallas_call(
-        pack_kernel,
-        out_shape=jax.ShapeDtypeStruct((TRACES_DEV + 1, ROWS, LENGTH), jnp.float32),
-        in_specs=[HBM] * 7,
-        out_specs=HBM,
-        scratch_shapes=[
-            pltpu.VMEM((TRACES_DEV, EV_DEV, LENGTH), jnp.float32),
-            pltpu.SMEM((1,), jnp.int32),
-            pltpu.VMEM((3, STATIONS_DEV, EV_DEV), jnp.float32),
-            pltpu.VMEM((STATIONS_DEV, EV_DEV), jnp.float32),
-            pltpu.VMEM((1, PAIR_DEV), jnp.int32),
-            pltpu.VMEM((1, PAIR_DEV), jnp.int32),
-            pltpu.VMEM((STATIONS_DEV, PAIR_DEV), jnp.int32),
-            pltpu.VMEM((ROWS, LENGTH), jnp.float32),
-            pltpu.SemaphoreType.DMA((13,)),
-        ],
-        compiler_params=WHOLE_VMEM,
-        name="pack",
-    )(
-        pair_live,
+    arguments = (
         traces.reshape(TRACES_DEV, EV_DEV, LENGTH),
         ray_slowness,
         travel_time,
@@ -480,6 +445,22 @@
         pair_second.reshape(1, PAIR_DEV),
         pair_lag,
     )
+    return pl.pallas_call(
+        pack_kernel,
+        out_shape=pltpu.VMEM((TRACES_DEV + 1, ROWS, LENGTH), jnp.float32),
+        in_specs=[SMEM] + [HBM] * 6,
+        out_specs=VMEM,
+        scratch_shapes=[
+            pltpu.VMEM((3, STATIONS_DEV, EV_DEV), jnp.float32),
+            pltpu.VMEM((STATIONS_DEV, EV_DEV), jnp.float32),
+            pltpu.VMEM((1, PAIR_DEV), jnp.int32),
+            pltpu.VMEM((1, PAIR_DEV), jnp.int32),
+            pltpu.VMEM((STATIONS_DEV, PAIR_DEV), jnp.int32),
+            pltpu.SemaphoreType.DMA((6,)),
+        ],
+        compiler_params=PARAMS,
+        name="pack",
+    )(pair_live, *[pltpu.with_memory_space_constraint(value, pltpu.HBM) for value in arguments])
 
 
 def firsts(message):
@@ -503,19 +484,19 @@
 MOVED = jax.ShapeDtypeStruct((TRACES_DEV * PAIR_DEV * ROWS, LANES), jnp.float32)
 
 
-def early(places, message, from_mate):
+def early(places, chip):
     return pl.pallas_call(
         early_kernel,
         out_shape=MOVED,
-        in_specs=[SMEM, VMEM, VMEM],
+        in_specs=[SMEM, VMEM],
         out_specs=VMEM,
         scratch_shapes=[pltpu.VMEM((3 * PART_ROWS + 2 * ROWS, LANES), jnp.float32)],
         compiler_params=PARAMS,
         name="early",
-    )(places, message, from_mate)
-
-
-def late(places, moved, message, from_mate, from_cross, high, low, pick, rates):
+    )(places, chip)
+
+
+def late(places, moved, chip, from_cross, high, low, pick, rates):
     refined_shift, block, _ = pl.pallas_call(
         late_kernel,
         out_shape=(
@@ -523,7 +504,7 @@
             jax.ShapeDtypeStruct((1, PAYLOAD), jnp.float32),
             MOVED,
         ),
-        in_specs=[VMEM] * 9,
+        in_specs=[VMEM] * 8,
         out_specs=(VMEM, VMEM, VMEM),
         scratch_shapes=[
             pltpu.VMEM((PART_ROWS + 2 * ROWS, LANES), jnp.float32),
@@ -533,7 +514,7 @@
         input_output_aliases={1: 2},
         compiler_params=PARAMS,
         name="late",
-    )(places, moved, message, from_mate, from_cross, high, low, pick, rates)
+    )(places, moved, chip, from_cross, high, low, pick, rates)
     return refined_shift, block
 
 
@@ -556,13 +537,11 @@
     message = pack(
         traces, ray_slowness, travel_time, pair_first, pair_second, pair_lag, pair_live
     )
-    from_cross = swapped(message, in_other_chip)
-    from_mate = swapped(message, in_other_core)
+    from_cross = from_other_chip(message)
     high, low, places, pick, rates = firsts(message)
-    moved = early(places, message, from_mate)
-    shift, block = late(
-        places, moved, message, from_mate, from_cross, high, low, pick, rates
-    )
+    chip = lax.all_gather(message, "c", axis=0)
+    moved = early(places, chip)
+    shift, block = late(places, moved, chip, from_cross, high, low, pick, rates)
     block = lax.psum(block, "x")
     chips = lax.axis_size("g")
     copies = jnp.broadcast_to(block, (chips, PAYLOAD))

time: 63.8 us -> 61 us (0.956)
  blocking collectives: 37.3 us -> 43.5 us
  starting transfers between devices: 10.7 us -> 4.59 us
  waiting for transfers between devices: 1.07 us -> 0.01 us
  local copies, waits for them, and re-layouts: 1.08 us -> 0.1 us
  Pallas kernels: 12 us -> 11.2 us
    ppermute x2 -> x1, starting transfers between devices: 10.7 us -> 4.59 us  [from_other_chip(): return lax.ppermute(block, ('g', 'c'), route)]
    all_gather x0 -> x1, blocking collectives: none -> 4.87 us  [body(): chip = lax.all_gather(message, 'c', axis=0)]
    all_to_all x1, blocking collectives: 25.4 us -> 26.9 us  [body(): gathered = lax.all_to_all(copies, 'g', 0, 0, tiled=True)]
    ppermute x2 -> x1, waiting for transfers between devices: 1.07 us -> 0.01 us  [from_other_chip(): return lax.ppermute(block, ('g', 'c'), route)]
    unnamed x4 -> x0, local copies, waits for them, and re-layouts: 0.98 us -> none
    pallas_call x2, Pallas kernels: 4 us -> 3.36 us  [the longest x1 2.34 us: early(): pl.pallas_call(early_kernel, out_shape=MOVED, in_specs=[SMEM, VMEM], out_...]
  transfers between devices with their start and end apart: 2 -> 1, of which waited for: 1 -> 0; matrix products, arithmetic and copies ran while one was open for 0% -> 0% of each run, Pallas kernels for 7% -> 8%
where the time goes in v4:
time: 61 us; the launch traced here: 60.8 us
  blocking collectives  43.5 us (71%)
  Pallas kernels  11.2 us (18%)
  starting transfers between devices  4.59 us (8%)
  between operations  1.33 us (2%)
    all_to_all x1, blocking collectives, body(): gathered = lax.all_to_all(copies, 'g', 0, 0, tiled=True)  26.9 us
    psum x1, blocking collectives, body(): block = lax.psum(block, 'x')  6.33 us
    all_gather x1, blocking collectives, body(): gathered = lax.all_gather(gathered, 'c', axis=0)  5.42 us
    all_gather x1, blocking collectives, body(): chip = lax.all_gather(message, 'c', axis=0)  4.87 us
    ppermute x1, starting transfers between devices, from_other_chip(): return lax.ppermute(block, ('g', 'c'), route)  4.59 us
    pallas_call x1, Pallas kernels, late(): pl.pallas_call(late_kernel, out_shape=(jax.ShapeDtypeStruct((STATIONS_DEV...  3.79 us
    pallas_call x1, Pallas kernels, early(): pl.pallas_call(early_kernel, out_shape=MOVED, in_specs=[SMEM, VMEM], out_...  2.34 us
    pallas_call x1, Pallas kernels, firsts(): pl.pallas_call(first_kernel, out_shape=(toeplitz, toeplitz, jax.ShapeDtyp...  2.31 us
  transfers between devices with their start and end apart: 1, of which 0 were waited for; matrix products, arithmetic and copies ran while one was open for 0% of the time, Pallas kernels for 8%

profile of v4, /device:TPU:1, one launch (start us, length us, event | category | flops | bytes accessed | tf_op | source)
XLA Modules:
  0.0 60.8 jit_solution(17780053714405824269)
XLA Ops:
  1.3 1.0 %pack.1.own_ref = f32[10,8,1024]{2,1,0:T(8,128)S(1)} custom-call(s32[1]{0:T(128)S(6)} %copy.12.live_ref, f32[9,8,1024]{2,1,0:T(8,128)} %bitcast.8, f32[3,3,8]{2,1,0:T(4,128)} %slowness_ref.1, f32[3,8]{1,0:T(4,128)} %time_ref.1, s32[1,128]{1,0:T(1,128)} %bitcast.9, s32[1,128]{1,0:T(1,128)} %bitcast.10, s32[3,128]{1,0:T(4,128)} %lag_ref.1), custom_call_target="tpu_custom_call" | custom-call | tf_op jit(solution)/shard_map/pack/pallas_call | solution.py:448
  2.3 4.6 %collective-permute-start = (f32[10,8,1024]{2,1,0:T(8,128)S(1)}, f32[10,8,1024]{2,1,0:T(8,128)S(1)}, u32[]{:S(2)}, u32[]{:S(2)}) collective-permute-start(f32[10,8,1024]{2,1,0:T(8,128)S(1)} %pack.1.own_ref), channel_id=1, source_target_pairs={{4,8},{8,4},{12,16},{16,12},{20,24},{24,20},{28,32},{32,28},{36,40... | collective-permute-start | bytes 983048 | tf_op jit(solution)/shard_map/ppermute | solution.py:430
  6.9 2.3 %firsts.1 = (bf16[9,256,640]{2,1,0:T(8,128)(2,1)S(1)}, bf16[9,256,640]{2,1,0:T(8,128)(2,1)S(1)}, s32[8,128]{1,0:T(8,128)S(1)}, f32[128,256]{1,0:T(8,128)S(1)}, f32[1,640]{1,0:T(1,128)S(1)}) custom-call(f32[10,8,1024]{2,1,0:T(8,128)S(1)} %pack.1.own_ref), custom_call_target="tpu_custom_call" | custom-call | tf_op jit(solution)/shard_map/firsts/pallas_call | solution.py:468
  9.2 4.9 %all-gather = f32[20,8,1024]{2,1,0:T(8,128)S(1)} all-gather(f32[10,8,1024]{2,1,0:T(8,128)S(1)} %pack.1.own_ref), channel_id=2, replica_groups=mesh['g'=64,'c'=2,'x'=4] {'c'}, dimensions={0}, use_global_device_ids=true | all-gather | bytes 983040 | tf_op jit(solution)/shard_map/all_gather | solution.py:542
  14.1 2.3 %early.1.moved_in_ref = f32[9216,128]{1,0:T(8,128)S(1)} custom-call(s32[8,128]{1,0:T(8,128)S(1)} %get-tuple-element.11.places_ref.places_in_ref, f32[2,10,8,1024]{3,2,1,0:T(8,128)S(1)} %bitcast.5), custom_call_target="tpu_custom_call" | custom-call | tf_op jit(solution)/shard_map/early/pallas_call | solution.py:488
  16.4 0.0 collective-permute-done.cross_ref
  16.4 3.8 %late.1 = (f32[3,128]{1,0:T(4,128)S(1)}, f32[1,640]{1,0:T(1,128)S(1)}, f32[9216,128]{1,0:T(8,128)S(1)}) custom-call(s32[8,128]{1,0:T(8,128)S(1)} %get-tuple-element.11.places_ref.places_in_ref, f32[9216,128]{1,0:T(8,128)S(1)} %early.1.moved_in_ref, f32[2,10,8,1024]{3,2,1,0:T(8,128)S(1)} %bitcast.6, ...), custom_call_target="tpu_custom_call", output_to_operand_aliasing={{2}: (1, {})} | custom-call | tf_op jit(solution)/shard_map/late/pallas_call | solution.py:500
  20.3 6.3 %psum.10 = f32[640]{0:T(1024)S(1)} all-reduce(f32[640]{0:T(1024)S(1)} %reduce), channel_id=1, replica_groups=mesh['g'=64,'c'=2,'x'=4] {'x'}, use_global_device_ids=true, to_apply=%region_0.0 | all-reduce | flops 640 | bytes 5120 | tf_op jit(solution)/shard_map/psum | solution.py:545
  26.6 0.1 broadcast_in_dim.2
  26.7 26.9 %all_to_all.6 = f32[64,1,640]{2,1,0:T(1,128)S(1)} all-to-all(f32[64,1,640]{2,1,0:T(1,128)S(1)} %broadcast_in_dim.2), channel_id=1, replica_groups=mesh['g'=64,'c'=2,'x'=4] {'g'}, dimensions={0} | all-to-all | bytes 327680 | tf_op jit(solution)/shard_map/all_to_all | solution.py:548
  53.6 5.4 %all-gather.1 = f32[128,1,640]{2,0,1:T(8,128)S(1)} all-gather(f32[64,1,640]{2,0,1:T(8,128)S(1)} %copy.10), channel_id=3, replica_groups=mesh['g'=64,'c'=2,'x'=4] {'c'}, dimensions={0}, use_global_device_ids=true | all-gather | bytes 491520 | tf_op jit(solution)/shard_map/all_gather | solution.py:549
  59.0 1.7 %solve.1 = (f32[4,8]{1,0:T(4,128)}, f32[3,128]{1,0:T(4,128)}) custom-call(f32[128,640]{1,0:T(8,128)S(1)} %bitcast.7, f32[3,128]{1,0:T(4,128)S(1)} %get-tuple-element.17.shift_ref), custom_call_target="tpu_custom_call" | custom-call | tf_op jit(solution)/shard_map/solve/pallas_call | solution.py:522
  (2 shorter events, 0.0 us)
Async XLA Ops:
  2.3 14.1 %collective-permute-start = (f32[10,8,1024]{2,1,0:T(8,128)S(1)}, f32[10,8,1024]{2,1,0:T(8,128)S(1)}, u32[]{:S(2)}, u32[]{:S(2)}) collective-permute-start(f32[10,8,1024]{2,1,0:T(8,128)S(1)} %pack.1.own_ref), channel_id=1, source_target_pairs={{4,8},{8,4},{12,16},{16,12},{20,24},{24,20},{28,32},{32,28},{36,40... | collective-permute-start | bytes 983048 | tf_op jit(solution)/shard_map/ppermute | solution.py:430

commit v5 on v4

--- a/solution.py
+++ b/solution.py
@@ -430,6 +430,11 @@
     return lax.ppermute(block, ("g", "c"), route)
 
 
+def spread(row, axis):
+    copies = jnp.broadcast_to(row, (lax.axis_size(axis), row.shape[1]))
+    return lax.all_to_all(copies, axis, 0, 0, tiled=True)
+
+
 VMEM = pl.BlockSpec(memory_space=pltpu.VMEM)
 SMEM = pl.BlockSpec(memory_space=pltpu.SMEM)
 HBM = pl.BlockSpec(memory_space=pltpu.HBM)
@@ -542,11 +547,9 @@
     chip = lax.all_gather(message, "c", axis=0)
     moved = early(places, chip)
     shift, block = late(places, moved, chip, from_cross, high, low, pick, rates)
-    block = lax.psum(block, "x")
+    block = jnp.sum(spread(block, "x"), axis=0, keepdims=True)
     chips = lax.axis_size("g")
-    copies = jnp.broadcast_to(block, (chips, PAYLOAD))
-    gathered = lax.all_to_all(copies, "g", 0, 0, tiled=True)
-    gathered = lax.all_gather(gathered, "c", axis=0)
+    gathered = lax.all_gather(spread(block, "g"), "c", axis=0)
     location, refined_shift = solve(gathered.reshape(2 * chips, PAYLOAD), shift)
     return refined_shift, location
 

time: 61 us -> 59.9 us (0.982)
  blocking collectives: 43.5 us -> 42.8 us
    all_to_all x1 -> x2, blocking collectives: 26.9 us -> 33.3 us  [spread(): return lax.all_to_all(copies, axis, 0, 0, tiled=True)]
    psum x1 -> x0, blocking collectives: 6.33 us -> none  [body(): block = lax.psum(block, 'x')]
    all_gather x1, blocking collectives: 5.42 us -> 4.63 us  [body(): gathered = lax.all_gather(spread(block, 'g'), 'c', axis=0)]
  transfers between devices with their start and end apart: 1 -> 1, of which waited for: 0 -> 0; matrix products, arithmetic and copies ran while one was open for 0% -> 0% of each run, Pallas kernels for 8% -> 7%
where the time goes in v5:
time: 59.9 us; the launch traced here: 59.7 us
  blocking collectives  42.8 us (71%)
  Pallas kernels  10.8 us (18%)
  starting transfers between devices  4.59 us (8%)
  between operations  1.34 us (2%)
    all_to_all x2, blocking collectives, spread(): return lax.all_to_all(copies, axis, 0, 0, tiled=True)  33.3 us
    all_gather x1, blocking collectives, body(): chip = lax.all_gather(message, 'c', axis=0)  4.87 us
    all_gather x1, blocking collectives, body(): gathered = lax.all_gather(spread(block, 'g'), 'c', axis=0)  4.63 us
    ppermute x1, starting transfers between devices, from_other_chip(): return lax.ppermute(block, ('g', 'c'), route)  4.59 us
    pallas_call x1, Pallas kernels, late(): pl.pallas_call(late_kernel, out_shape=(jax.ShapeDtypeStruct((STATIONS_DEV...  3.63 us
    pallas_call x1, Pallas kernels, firsts(): pl.pallas_call(first_kernel, out_shape=(toeplitz, toeplitz, jax.ShapeDtyp...  2.31 us
    pallas_call x1, Pallas kernels, early(): pl.pallas_call(early_kernel, out_shape=MOVED, in_specs=[SMEM, VMEM], out_...  2.12 us
    pallas_call x1, Pallas kernels, solve(): pl.pallas_call(solve_kernel, out_shape=(jax.ShapeDtypeStruct((4, EV_DEV),...  1.74 us
  transfers between devices with their start and end apart: 1, of which 0 were waited for; matrix products, arithmetic and copies ran while one was open for 0% of the time, Pallas kernels for 7%

profile of v5, /device:TPU:1, one launch (start us, length us, event | category | flops | bytes accessed | tf_op | source)
XLA Modules:
  0.0 59.7 jit_solution(3484173367296271960)
XLA Ops:
  1.3 1.0 %pack.1.own_ref = f32[10,8,1024]{2,1,0:T(8,128)S(1)} custom-call(s32[1]{0:T(128)S(6)} %copy.16.live_ref, f32[9,8,1024]{2,1,0:T(8,128)} %bitcast.8, f32[3,3,8]{2,1,0:T(4,128)} %slowness_ref.1, f32[3,8]{1,0:T(4,128)} %time_ref.1, s32[1,128]{1,0:T(1,128)} %bitcast.9, s32[1,128]{1,0:T(1,128)} %bitcast.10, s32[3,128]{1,0:T(4,128)} %lag_ref.1), custom_call_target="tpu_custom_call" | custom-call | tf_op jit(solution)/shard_map/pack/pallas_call | solution.py:453
  2.3 4.6 %collective-permute-start = (f32[10,8,1024]{2,1,0:T(8,128)S(1)}, f32[10,8,1024]{2,1,0:T(8,128)S(1)}, u32[]{:S(2)}, u32[]{:S(2)}) collective-permute-start(f32[10,8,1024]{2,1,0:T(8,128)S(1)} %pack.1.own_ref), channel_id=1, source_target_pairs={{4,8},{8,4},{12,16},{16,12},{20,24},{24,20},{28,32},{32,28},{36,40... | collective-permute-start | bytes 983048 | tf_op jit(solution)/shard_map/ppermute | solution.py:430
  6.9 2.3 %firsts.1 = (bf16[9,256,640]{2,1,0:T(8,128)(2,1)S(1)}, bf16[9,256,640]{2,1,0:T(8,128)(2,1)S(1)}, s32[8,128]{1,0:T(8,128)S(1)}, f32[128,256]{1,0:T(8,128)S(1)}, f32[1,640]{1,0:T(1,128)S(1)}) custom-call(f32[10,8,1024]{2,1,0:T(8,128)S(1)} %pack.1.own_ref), custom_call_target="tpu_custom_call" | custom-call | tf_op jit(solution)/shard_map/firsts/pallas_call | solution.py:473
  9.2 4.9 %all-gather = f32[20,8,1024]{2,1,0:T(8,128)S(1)} all-gather(f32[10,8,1024]{2,1,0:T(8,128)S(1)} %pack.1.own_ref), channel_id=2, replica_groups=mesh['g'=64,'c'=2,'x'=4] {'c'}, dimensions={0}, use_global_device_ids=true | all-gather | bytes 983040 | tf_op jit(solution)/shard_map/all_gather | solution.py:547
  14.1 2.1 %early.1.moved_in_ref = f32[9216,128]{1,0:T(8,128)S(1)} custom-call(s32[8,128]{1,0:T(8,128)S(1)} %get-tuple-element.11.places_ref.places_in_ref, f32[2,10,8,1024]{3,2,1,0:T(8,128)S(1)} %bitcast.5), custom_call_target="tpu_custom_call" | custom-call | tf_op jit(solution)/shard_map/early/pallas_call | solution.py:493
  16.2 0.0 collective-permute-done.cross_ref
  16.2 3.6 %late.1 = (f32[3,128]{1,0:T(4,128)S(1)}, f32[1,640]{1,0:T(1,128)S(1)}, f32[9216,128]{1,0:T(8,128)S(1)}) custom-call(s32[8,128]{1,0:T(8,128)S(1)} %get-tuple-element.11.places_ref.places_in_ref, f32[9216,128]{1,0:T(8,128)S(1)} %early.1.moved_in_ref, f32[2,10,8,1024]{3,2,1,0:T(8,128)S(1)} %bitcast.6, ...), custom_call_target="tpu_custom_call", output_to_operand_aliasing={{2}: (1, {})} | custom-call | tf_op jit(solution)/shard_map/late/pallas_call | solution.py:505
  19.9 6.6 %all_to_all.12 = f32[4,1,640]{2,1,0:T(1,128)S(1)} all-to-all(f32[4,1,640]{2,1,0:T(1,128)S(1)} %broadcast_in_dim.4), channel_id=1, replica_groups=mesh['g'=64,'c'=2,'x'=4] {'x'}, dimensions={0} | all-to-all | bytes 20480 | tf_op jit(solution)/shard_map/all_to_all | solution.py:435
  26.5 0.1 broadcast_in_dim.5
  26.6 26.7 %all_to_all.13 = f32[64,1,640]{2,1,0:T(1,128)S(1)} all-to-all(f32[64,1,640]{2,1,0:T(1,128)S(1)} %broadcast_in_dim.5), channel_id=1, replica_groups=mesh['g'=64,'c'=2,'x'=4] {'g'}, dimensions={0} | all-to-all | bytes 327680 | tf_op jit(solution)/shard_map/all_to_all | solution.py:435
  53.3 4.6 %all-gather.1 = f32[128,1,640]{2,0,1:T(8,128)S(1)} all-gather(f32[64,1,640]{2,0,1:T(8,128)S(1)} %copy.13), channel_id=3, replica_groups=mesh['g'=64,'c'=2,'x'=4] {'c'}, dimensions={0}, use_global_device_ids=true | all-gather | bytes 491520 | tf_op jit(solution)/shard_map/all_gather | solution.py:552
  57.9 1.7 %solve.1 = (f32[4,8]{1,0:T(4,128)}, f32[3,128]{1,0:T(4,128)}) custom-call(f32[128,640]{1,0:T(8,128)S(1)} %bitcast.7, f32[3,128]{1,0:T(4,128)S(1)} %get-tuple-element.17.shift_ref), custom_call_target="tpu_custom_call" | custom-call | tf_op jit(solution)/shard_map/solve/pallas_call | solution.py:527
  (4 shorter events, 0.1 us)
Async XLA Ops:
  2.3 13.9 %collective-permute-start = (f32[10,8,1024]{2,1,0:T(8,128)S(1)}, f32[10,8,1024]{2,1,0:T(8,128)S(1)}, u32[]{:S(2)}, u32[]{:S(2)}) collective-permute-start(f32[10,8,1024]{2,1,0:T(8,128)S(1)} %pack.1.own_ref), channel_id=1, source_target_pairs={{4,8},{8,4},{12,16},{16,12},{20,24},{24,20},{28,32},{32,28},{36,40... | collective-permute-start | bytes 983048 | tf_op jit(solution)/shard_map/ppermute | solution.py:430

commit v6 on v5

--- a/solution.py
+++ b/solution.py
@@ -23,6 +23,8 @@
 PART_ROWS = TRACES_DEV * EV_DEV * CHUNKS
 VMEM_BYTES = 24 * 1024 * 1024
 DEAD = -1000.0
+PLACE_ROWS = 16
+GROUP = 16
 PAYLOAD = 5 * LANES
 SQUARE_AT = 4 * NEAR
 
@@ -121,8 +123,8 @@
     copies[0].wait()
 
 
-def first_kernel(own_ref, high_ref, low_ref, places_ref, pick_ref, rates_ref):
-    for item in range(TRACES_DEV):
+def first_windows(own_ref, high_ref, low_ref, items):
+    for item in items:
         window = own_ref[item, :, QUARTER : QUARTER + WINDOW]
         power = jnp.sum(window * window, axis=1, keepdims=True)
         window = window * lax.rsqrt(power + eps_small)
@@ -133,6 +135,11 @@
             high, low = split_bf16(wide)
             high_ref[item, pl.ds(event * LAGS, LAGS), :] = high
             low_ref[item, pl.ds(event * LAGS, LAGS), :] = low
+
+
+def first_kernel(
+    own_ref, high_ref, low_ref, places_ref, pick_ref, rates_ref, places, sem
+):
     aux = own_ref[TRACES_DEV]
     first = aux[0:1, 6 * LANES : 7 * LANES].astype(jnp.int32)
     second = aux[1:2, 6 * LANES : 7 * LANES].astype(jnp.int32)
@@ -145,25 +152,33 @@
     far = jnp.logical_and(away, alive)
     event = jnp.bitwise_and(second, EV_DEV - 1)
     rows = part * PART_ROWS + event * CHUNKS + lax.shift_right_arithmetic(begin, 7)
+    near = jnp.logical_and(jnp.logical_not(away), alive)
     upper = lax.broadcasted_iota(jnp.int32, (PAIR_DEV, PAIR_DEV), 0)
     lower = lax.broadcasted_iota(jnp.int32, (PAIR_DEV, PAIR_DEV), 1)
+    lane_ids = lower[0:1]
     ahead = (upper <= lower).astype(jnp.bfloat16)
-    marked = jnp.broadcast_to(far.astype(jnp.float32), (ROWS, PAIR_DEV)).astype(jnp.bfloat16)
-    place = dot_bf16(marked, ahead, NN)[0:1]
-    place = jnp.where(far, place - 1.0, -1.0)
-    hot = (upper.astype(jnp.float32) == place).astype(jnp.bfloat16)
     slots = lax.broadcasted_iota(jnp.int32, (ROWS, PAIR_DEV), 1).astype(jnp.bfloat16)
-    listed = dot_bf16(slots, hot, NT)[0:1].astype(jnp.int32)
-    count = jnp.sum(far.astype(jnp.float32), axis=1, keepdims=True).astype(jnp.int32)
-    spare = lax.broadcasted_iota(jnp.int32, (1, PAIR_DEV), 1) >= count
-    listed = jnp.where(spare, listed[:, 0:1], listed)
-    places_ref[0:3, :] = rows
-    places_ref[3:6, :] = jnp.bitwise_and(begin, LANES - 1)
-    places_ref[6:7, :] = listed
-    live_count = jnp.sum(alive.astype(jnp.float32), axis=1, keepdims=True).astype(jnp.int32)
-    places_ref[7:8, :] = jnp.where(
-        lax.broadcasted_iota(jnp.int32, (1, PAIR_DEV), 1) == 0, count, live_count
-    )
+    hots, counts, listed = [], [], []
+    for marked in (far, near):
+        ones = marked.astype(jnp.float32)
+        wide = jnp.broadcast_to(ones, (ROWS, PAIR_DEV)).astype(jnp.bfloat16)
+        place = jnp.where(marked, dot_bf16(wide, ahead, NN)[0:1] - 1.0, -1.0)
+        hots.append((upper.astype(jnp.float32) == place).astype(jnp.bfloat16))
+        counts.append(jnp.sum(ones, axis=1, keepdims=True).astype(jnp.int32))
+    first_windows(own_ref, high_ref, low_ref, range(2))
+    for hot in hots:
+        listed.append(dot_bf16(slots, hot, NT)[0:1])
+    first_windows(own_ref, high_ref, low_ref, range(2, 4))
+    places[...] = jnp.zeros((PLACE_ROWS, PAIR_DEV), jnp.int32)
+    places[0:3, :] = rows
+    places[3:6, :] = jnp.bitwise_and(begin, LANES - 1)
+    for at in range(2):
+        filled = jnp.where(lane_ids < counts[at], listed[at], listed[at][:, 0:1])
+        places[6 + at : 7 + at, :] = filled.astype(jnp.int32)
+        places[8 + at : 9 + at, :] = jnp.broadcast_to(counts[at], (1, PAIR_DEV))
+    move = pltpu.make_async_copy(places, places_ref, sem)
+    move.start()
+    first_windows(own_ref, high_ref, low_ref, range(4, TRACES_DEV))
     ends = jnp.bitwise_and(first, EV_DEV - 1).astype(jnp.float32)
     column = jnp.transpose(jnp.broadcast_to(ends, (LANES, PAIR_DEV)))
     groups = lax.broadcasted_iota(jnp.int32, (PAIR_DEV, LANES), 1) // LAGS
@@ -180,6 +195,7 @@
                 rates_ref[:, at : at + EV_DEV] = jnp.where(
                     lax.axis_index("x") == group, own, 0.0
                 )
+    move.wait()
 
 
 def fill_table(ref, table_ref, part):
@@ -211,20 +227,22 @@
             moved_ref[pl.ds(to, ROWS), :] = moved
 
 
+def groups_of(count):
+    return lax.div(count + (GROUP - 1), GROUP)
+
+
 def early_kernel(places_ref, chip_ref, moved_ref, table_ref):
-    table_ref[pl.ds(2 * PART_ROWS, PART_ROWS + 2 * ROWS), :] = jnp.zeros(
-        (PART_ROWS + 2 * ROWS, LANES), jnp.float32
-    )
+    table_ref[pl.ds(2 * PART_ROWS, 2 * ROWS), :] = jnp.zeros((2 * ROWS, LANES), jnp.float32)
     core = lax.axis_index("c")
     fill_table(chip_ref.at[core], table_ref, 0)
     fill_table(chip_ref.at[1 - core], table_ref, 1)
 
     def step(index, carry):
-        for turn in range(16):
-            align(places_ref, table_ref, moved_ref, index * 16 + turn, 0)
+        for turn in range(GROUP):
+            align(places_ref, table_ref, moved_ref, places_ref[7, index * GROUP + turn], 0)
         return carry
 
-    lax.fori_loop(0, lax.shift_right_arithmetic(places_ref[7, 1] + 15, 4), step, 0)
+    lax.fori_loop(0, groups_of(places_ref[9, 0]), step, 0)
 
 
 def incidence(aux, offset):
@@ -242,7 +260,7 @@
 
 
 def late_kernel(
-    places_in_ref,
+    places_ref,
     moved_in_ref,
     chip_ref,
     cross_ref,
@@ -254,23 +272,18 @@
     block_ref,
     moved_ref,
     table_ref,
-    places_ref,
-    sem,
 ):
     del moved_in_ref
-    fetch = pltpu.make_async_copy(places_in_ref, places_ref, sem)
-    fetch.start()
     table_ref[pl.ds(PART_ROWS, 2 * ROWS), :] = jnp.zeros((2 * ROWS, LANES), jnp.float32)
     fill_table(cross_ref, table_ref, 0)
-    fetch.wait()
 
     def step(index, carry):
-        for turn in range(8):
-            slot = places_ref[6, index * 8 + turn]
+        for turn in range(GROUP):
+            slot = places_ref[6, index * GROUP + turn]
             align(places_ref, table_ref, moved_ref, slot, 2 * PART_ROWS)
         return carry
 
-    lax.fori_loop(0, lax.shift_right_arithmetic(places_ref[7, 0] + 7, 3), step, 0)
+    lax.fori_loop(0, groups_of(places_ref[8, 0]), step, 0)
 
     core = lax.axis_index("c")
     aux_own = chip_ref[core, TRACES_DEV]
@@ -475,12 +488,16 @@
         out_shape=(
             toeplitz,
             toeplitz,
-            jax.ShapeDtypeStruct((ROWS, PAIR_DEV), jnp.int32),
+            pltpu.SMEM((PLACE_ROWS, PAIR_DEV), jnp.int32),
             jax.ShapeDtypeStruct((PAIR_DEV, EV_DEV * LAGS), jnp.float32),
             jax.ShapeDtypeStruct((1, PAYLOAD), jnp.float32),
         ),
         in_specs=[VMEM],
-        out_specs=(VMEM,) * 5,
+        out_specs=(VMEM, VMEM, SMEM, VMEM, VMEM),
+        scratch_shapes=[
+            pltpu.VMEM((PLACE_ROWS, PAIR_DEV), jnp.int32),
+            pltpu.SemaphoreType.DMA,
+        ],
         compiler_params=PARAMS,
         name="firsts",
     )(message)
@@ -495,7 +512,7 @@
         out_shape=MOVED,
         in_specs=[SMEM, VMEM],
         out_specs=VMEM,
-        scratch_shapes=[pltpu.VMEM((3 * PART_ROWS + 2 * ROWS, LANES), jnp.float32)],
+        scratch_shapes=[pltpu.VMEM((2 * PART_ROWS + 2 * ROWS, LANES), jnp.float32)],
         compiler_params=PARAMS,
         name="early",
     )(places, chip)
@@ -509,13 +526,9 @@
             jax.ShapeDtypeStruct((1, PAYLOAD), jnp.float32),
             MOVED,
         ),
-        in_specs=[VMEM] * 8,
+        in_specs=[SMEM] + [VMEM] * 7,
         out_specs=(VMEM, VMEM, VMEM),
-        scratch_shapes=[
-            pltpu.VMEM((PART_ROWS + 2 * ROWS, LANES), jnp.float32),
-            pltpu.SMEM((ROWS, PAIR_DEV), jnp.int32),
-            pltpu.SemaphoreType.DMA,
-        ],
+        scratch_shapes=[pltpu.VMEM((PART_ROWS + 2 * ROWS, LANES), jnp.float32)],
         input_output_aliases={1: 2},
         compiler_params=PARAMS,
         name="late",
@@ -544,6 +557,7 @@
     )
     from_cross = from_other_chip(message)
     high, low, places, pick, rates = firsts(message)
+    places = pltpu.with_memory_space_constraint(places, pltpu.SMEM)
     chip = lax.all_gather(message, "c", axis=0)
     moved = early(places, chip)
     shift, block = late(places, moved, chip, from_cross, high, low, pick, rates)

time: 59.9 us -> 59.3 us (0.990)
  Pallas kernels: 10.8 us -> 9.27 us
  blocking collectives: 42.8 us -> 43.7 us
    pallas_call x1, Pallas kernels: 2.12 us -> 0.86 us  [early(): pl.pallas_call(early_kernel, out_shape=MOVED, in_specs=[SMEM, VMEM], out_...]
    pallas_call x1, Pallas kernels: 3.63 us -> 2.79 us  [late(): pl.pallas_call(late_kernel, out_shape=(jax.ShapeDtypeStruct((STATIONS_DEV...]
  transfers between devices with their start and end apart: 1 -> 1, of which waited for: 0 -> 0; matrix products, arithmetic and copies ran while one was open for 0% -> 0% of each run, Pallas kernels for 7% -> 6%
where the time goes in v6:
time: 59.3 us; the launch traced here: 59.1 us
  blocking collectives  43.7 us (74%)
  Pallas kernels  9.27 us (16%)
  starting transfers between devices  4.59 us (8%)
  between operations  1.35 us (2%)
    all_to_all x2, blocking collectives, spread(): return lax.all_to_all(copies, axis, 0, 0, tiled=True)  33.6 us
    all_gather x1, blocking collectives, body(): gathered = lax.all_gather(spread(block, 'g'), 'c', axis=0)  5.22 us
    all_gather x1, blocking collectives, body(): chip = lax.all_gather(message, 'c', axis=0)  4.87 us
    ppermute x1, starting transfers between devices, from_other_chip(): return lax.ppermute(block, ('g', 'c'), route)  4.59 us
    pallas_call x1, Pallas kernels, firsts(): pl.pallas_call(first_kernel, out_shape=(toeplitz, toeplitz, pltpu.SMEM((P...  2.86 us
    pallas_call x1, Pallas kernels, late(): pl.pallas_call(late_kernel, out_shape=(jax.ShapeDtypeStruct((STATIONS_DEV...  2.79 us
    pallas_call x1, Pallas kernels, solve(): pl.pallas_call(solve_kernel, out_shape=(jax.ShapeDtypeStruct((4, EV_DEV),...  1.74 us
  transfers between devices with their start and end apart: 1, of which 0 were waited for; matrix products, arithmetic and copies ran while one was open for 0% of the time, Pallas kernels for 6%

profile of v6, /device:TPU:1, one launch (start us, length us, event | category | flops | bytes accessed | tf_op | source)
XLA Modules:
  0.0 59.1 jit_solution(9297880922602145142)
XLA Ops:
  1.3 1.0 %pack.1.own_ref = f32[10,8,1024]{2,1,0:T(8,128)S(1)} custom-call(s32[1]{0:T(128)S(6)} %copy.16.live_ref, f32[9,8,1024]{2,1,0:T(8,128)} %bitcast.8, f32[3,3,8]{2,1,0:T(4,128)} %slowness_ref.1, f32[3,8]{1,0:T(4,128)} %time_ref.1, s32[1,128]{1,0:T(1,128)} %bitcast.9, s32[1,128]{1,0:T(1,128)} %bitcast.10, s32[3,128]{1,0:T(4,128)} %lag_ref.1), custom_call_target="tpu_custom_call" | custom-call | tf_op jit(solution)/shard_map/pack/pallas_call | solution.py:466
  2.3 4.6 %collective-permute-start = (f32[10,8,1024]{2,1,0:T(8,128)S(1)}, f32[10,8,1024]{2,1,0:T(8,128)S(1)}, u32[]{:S(2)}, u32[]{:S(2)}) collective-permute-start(f32[10,8,1024]{2,1,0:T(8,128)S(1)} %pack.1.own_ref), channel_id=1, source_target_pairs={{4,8},{8,4},{12,16},{16,12},{20,24},{24,20},{28,32},{32,28},{36,40... | collective-permute-start | bytes 983048 | tf_op jit(solution)/shard_map/ppermute | solution.py:443
  6.9 2.9 %firsts.1 = (bf16[9,256,640]{2,1,0:T(8,128)(2,1)S(1)}, bf16[9,256,640]{2,1,0:T(8,128)(2,1)S(1)}, s32[16,128]{1,0:T(8,128)S(4)}, f32[128,256]{1,0:T(8,128)S(1)}, f32[1,640]{1,0:T(1,128)S(1)}) custom-call(f32[10,8,1024]{2,1,0:T(8,128)S(1)} %pack.1.own_ref), custom_call_target="tpu_custom_call" | custom-call | tf_op jit(solution)/shard_map/firsts/pallas_call | solution.py:486
  9.8 4.9 %all-gather = f32[20,8,1024]{2,1,0:T(8,128)S(1)} all-gather(f32[10,8,1024]{2,1,0:T(8,128)S(1)} %pack.1.own_ref), channel_id=2, replica_groups=mesh['g'=64,'c'=2,'x'=4] {'c'}, dimensions={0}, use_global_device_ids=true | all-gather | bytes 983040 | tf_op jit(solution)/shard_map/all_gather | solution.py:561
  14.6 0.9 %early.1.moved_in_ref = f32[9216,128]{1,0:T(8,128)S(1)} custom-call(s32[16,128]{1,0:T(8,128)S(4)} %get-tuple-element.11.places_ref, f32[2,10,8,1024]{3,2,1,0:T(8,128)S(1)} %bitcast.5), custom_call_target="tpu_custom_call" | custom-call | tf_op jit(solution)/shard_map/early/pallas_call | solution.py:510
  15.5 0.0 collective-permute-done.cross_ref
  15.5 2.8 %late.1 = (f32[3,128]{1,0:T(4,128)S(1)}, f32[1,640]{1,0:T(1,128)S(1)}, f32[9216,128]{1,0:T(8,128)S(1)}) custom-call(s32[16,128]{1,0:T(8,128)S(4)} %get-tuple-element.11.places_ref, f32[9216,128]{1,0:T(8,128)S(1)} %early.1.moved_in_ref, f32[2,10,8,1024]{3,2,1,0:T(8,128)S(1)} %bitcast.6, ...), custom_call_target="tpu_custom_call", output_to_operand_aliasing={{2}: (1, {})} | custom-call | tf_op jit(solution)/shard_map/late/pallas_call | solution.py:522
  18.4 6.5 %all_to_all.12 = f32[4,1,640]{2,1,0:T(1,128)S(1)} all-to-all(f32[4,1,640]{2,1,0:T(1,128)S(1)} %broadcast_in_dim.4), channel_id=1, replica_groups=mesh['g'=64,'c'=2,'x'=4] {'x'}, dimensions={0} | all-to-all | bytes 20480 | tf_op jit(solution)/shard_map/all_to_all | solution.py:448
  24.9 0.1 broadcast_in_dim.5
  25.0 27.1 %all_to_all.13 = f32[64,1,640]{2,1,0:T(1,128)S(1)} all-to-all(f32[64,1,640]{2,1,0:T(1,128)S(1)} %broadcast_in_dim.5), channel_id=1, replica_groups=mesh['g'=64,'c'=2,'x'=4] {'g'}, dimensions={0} | all-to-all | bytes 327680 | tf_op jit(solution)/shard_map/all_to_all | solution.py:448
  52.1 5.2 %all-gather.1 = f32[128,1,640]{2,0,1:T(8,128)S(1)} all-gather(f32[64,1,640]{2,0,1:T(8,128)S(1)} %copy.13), channel_id=3, replica_groups=mesh['g'=64,'c'=2,'x'=4] {'c'}, dimensions={0}, use_global_device_ids=true | all-gather | bytes 491520 | tf_op jit(solution)/shard_map/all_gather | solution.py:566
  57.3 1.7 %solve.1 = (f32[4,8]{1,0:T(4,128)}, f32[3,128]{1,0:T(4,128)}) custom-call(f32[128,640]{1,0:T(8,128)S(1)} %bitcast.7, f32[3,128]{1,0:T(4,128)S(1)} %get-tuple-element.17.shift_ref), custom_call_target="tpu_custom_call" | custom-call | tf_op jit(solution)/shard_map/solve/pallas_call | solution.py:540
  (4 shorter events, 0.1 us)
Async XLA Ops:
  2.3 13.2 %collective-permute-start = (f32[10,8,1024]{2,1,0:T(8,128)S(1)}, f32[10,8,1024]{2,1,0:T(8,128)S(1)}, u32[]{:S(2)}, u32[]{:S(2)}) collective-permute-start(f32[10,8,1024]{2,1,0:T(8,128)S(1)} %pack.1.own_ref), channel_id=1, source_target_pairs={{4,8},{8,4},{12,16},{16,12},{20,24},{24,20},{28,32},{32,28},{36,40... | collective-permute-start | bytes 983048 | tf_op jit(solution)/shard_map/ppermute | solution.py:443

commit v7 on v6

--- a/solution.py
+++ b/solution.py
@@ -22,7 +22,6 @@
 PAIR_DEV = 128
 PART_ROWS = TRACES_DEV * EV_DEV * CHUNKS
 VMEM_BYTES = 24 * 1024 * 1024
-DEAD = -1000.0
 PLACE_ROWS = 16
 GROUP = 16
 PAYLOAD = 5 * LANES
@@ -30,19 +29,12 @@
 
 eps_small = 1e-06
 sample_step = 0.01
-exact_mode = lax.Precision.HIGHEST
 NT = (((1,), (1,)), ((), ()))
 NN = (((1,), (0,)), ((), ()))
 
 
 def device_index():
     return lax.axis_index("g") * 2 + lax.axis_index("c")
-
-
-def dot_exact(left, right, dims):
-    return lax.dot_general(
-        left, right, dims, precision=exact_mode, preferred_element_type=jnp.float32
-    )
 
 
 def dot_bf16(left, right, dims):
@@ -58,13 +50,17 @@
     return 3 * LANES + 8 * index if index < 32 else 2 * LANES + 96 + 8 * (index - 32)
 
 
-def dot_signs(left, signs, dims):
-    high = left.astype(jnp.bfloat16)
-    rest = left - high.astype(jnp.float32)
+def thirds(values):
+    high = values.astype(jnp.bfloat16)
+    rest = values - high.astype(jnp.float32)
     middle = rest.astype(jnp.bfloat16)
     low = (rest - middle.astype(jnp.float32)).astype(jnp.bfloat16)
+    return jnp.concatenate([high, middle, low], axis=0)
+
+
+def dot_signs(left, signs, dims):
     rows = left.shape[0]
-    parts = dot_bf16(jnp.concatenate([high, middle, low], axis=0), signs, dims)
+    parts = dot_bf16(thirds(left), signs, dims)
     return parts[0:rows] + parts[rows : 2 * rows] + parts[2 * rows :]
 
 
@@ -75,7 +71,6 @@
 
 
 def pack_kernel(
-    live_ref,
     traces_ref,
     slowness_ref,
     time_ref,
@@ -109,12 +104,8 @@
     for copy in copies[1:]:
         copy.wait()
     base = device_index() * EV_DEV - EV_DEV
-    slots = lax.broadcasted_iota(jnp.int32, (1, PAIR_DEV), 1)
-    alive = slots < live_ref[0]
     for row, ids in enumerate((first, second)):
-        near = (ids[...] - base).astype(jnp.float32)
-        aux[row : row + 1, 0:LANES] = jnp.where(alive, near, DEAD)
-        aux[row : row + 1, 6 * LANES : 7 * LANES] = near
+        aux[row : row + 1, 0:LANES] = (ids[...] - base).astype(jnp.float32)
     aux[0:STATIONS_DEV, LANES : LANES + EV_DEV] = time[...]
     for q in range(3):
         lane = (2 + q) * LANES
@@ -138,17 +129,17 @@
 
 
 def first_kernel(
-    own_ref, high_ref, low_ref, places_ref, pick_ref, rates_ref, places, sem
+    live_ref, own_ref, high_ref, low_ref, places_ref, pick_ref, rates_ref, places, sem
 ):
     aux = own_ref[TRACES_DEV]
-    first = aux[0:1, 6 * LANES : 7 * LANES].astype(jnp.int32)
-    second = aux[1:2, 6 * LANES : 7 * LANES].astype(jnp.int32)
+    first = aux[0:1, 0:LANES].astype(jnp.int32)
+    second = aux[1:2, 0:LANES].astype(jnp.int32)
     begin = aux[0:STATIONS_DEV, 5 * LANES : 6 * LANES].astype(jnp.int32) + (QUARTER - LAGS // 2)
     side = lax.shift_right_arithmetic(second, 3)
     mate_side = 2 - 2 * lax.axis_index("c")
     away = jnp.logical_and(side != 1, side != mate_side)
     part = jnp.where(side == 1, 0, jnp.where(away, 2, 1))
-    alive = aux[0:1, 0:LANES] >= 0.0
+    alive = lax.broadcasted_iota(jnp.int32, (1, PAIR_DEV), 1) < live_ref[0]
     far = jnp.logical_and(away, alive)
     event = jnp.bitwise_and(second, EV_DEV - 1)
     rows = part * PART_ROWS + event * CHUNKS + lax.shift_right_arithmetic(begin, 7)
@@ -176,6 +167,7 @@
         filled = jnp.where(lane_ids < counts[at], listed[at], listed[at][:, 0:1])
         places[6 + at : 7 + at, :] = filled.astype(jnp.int32)
         places[8 + at : 9 + at, :] = jnp.broadcast_to(counts[at], (1, PAIR_DEV))
+    places[10:11, :] = jnp.broadcast_to(live_ref[0], (1, PAIR_DEV))
     move = pltpu.make_async_copy(places, places_ref, sem)
     move.start()
     first_windows(own_ref, high_ref, low_ref, range(4, TRACES_DEV))
@@ -245,11 +237,10 @@
     lax.fori_loop(0, groups_of(places_ref[9, 0]), step, 0)
 
 
-def incidence(aux, offset):
+def incidence(aux):
     events = lax.broadcasted_iota(jnp.int32, (NEAR, PAIR_DEV), 0).astype(jnp.float32)
-    starts = aux[0:1, 0:LANES] + offset
-    ends = aux[1:2, 0:LANES] + offset
-    return (events == starts).astype(jnp.float32) - (events == ends).astype(jnp.float32)
+    starts = (events == aux[0:1, 0:LANES]).astype(jnp.float32)
+    return starts - (events == aux[1:2, 0:LANES]).astype(jnp.float32)
 
 
 def near_block(left, own, right, part):
@@ -319,19 +310,16 @@
         above = jnp.sum(rows[0:LAGS], axis=0, keepdims=True)
         below = jnp.sum(rows[LAGS:], axis=0, keepdims=True)
         station_shift.append(above / (below + eps_small))
-    alive = aux_own[0:1, 0:LANES] >= 0.0
+    alive = lax.broadcasted_iota(jnp.int32, (1, PAIR_DEV), 1) < places_ref[10, 0]
     shift = jnp.where(alive, jnp.concatenate(station_shift, axis=0), 0.0)
     shift_ref[...] = shift
 
-    signs = incidence(aux_own, 0.0).astype(jnp.bfloat16)
+    signs = jnp.where(alive, incidence(aux_own), 0.0).astype(jnp.bfloat16)
     times = dot_signs(near_block(aux_left, aux_own, aux_right, 1), signs, NN)
     lags = aux_own[0:STATIONS_DEV, 5 * LANES : 6 * LANES]
     rhs = jnp.where(alive, sample_step * (lags + shift), 0.0) - times
     per_event = dot_signs(rhs, signs, NT)
     counts = dot_bf16(signs[EV_DEV : 2 * EV_DEV], signs, NT)
-    for aux, offset in ((aux_left, -float(EV_DEV)), (aux_right, float(EV_DEV))):
-        other = incidence(aux, offset).astype(jnp.bfloat16)
-        counts = counts + dot_bf16(other[EV_DEV : 2 * EV_DEV], other, NT)
     counts = jnp.where(lax.axis_index("x") == 0, counts, 0.0)
     block_ref[...] = rates_ref[...]
     for event in range(EV_DEV):
@@ -346,7 +334,30 @@
     block_ref[:, SQUARE_AT : SQUARE_AT + 1] = total
 
 
-def solve_kernel(gathered_ref, shift_ref, out_ref, shift_out_ref, rows_ref):
+def symmetric(counts, turned_ref):
+    for side, block in ((0, 0), (2, 1)):
+        for a in range(EV_DEV):
+            at = block * EV_DEV * EV_DEV + a
+            turned_ref[pl.ds(at, EV_DEV, stride=EV_DEV), :] = counts[a][side]
+    lower = sum(counts[a][0] for a in range(1, EV_DEV)) + counts[0][0]
+    upper = sum(counts[a][2] for a in range(1, EV_DEV)) + counts[0][2]
+    ends = pltpu.roll(upper, 1, 1) + pltpu.roll(lower, LANES - 1, 1)
+    rows = lax.broadcasted_iota(jnp.int32, (EV_DEV, LANES), 0)
+    result = []
+    for a in range(EV_DEV):
+        to_lower = turned_ref[pl.ds(a * EV_DEV, EV_DEV), :]
+        to_upper = turned_ref[pl.ds((EV_DEV + a) * EV_DEV, EV_DEV), :]
+        result.append(
+            [
+                counts[a][0] + pltpu.roll(to_upper, 1, 1),
+                counts[a][1] - jnp.where(rows == a, ends, 0.0),
+                counts[a][2] + pltpu.roll(to_lower, LANES - 1, 1),
+            ]
+        )
+    return result
+
+
+def solve_kernel(gathered_ref, shift_ref, out_ref, shift_out_ref, rows_ref, turned_ref):
     shift_out_ref[...] = shift_ref[...]
     half = LANES // 2
     tables = []
@@ -363,7 +374,9 @@
         return own + pltpu.roll(upper, 1, 1) + pltpu.roll(lower, LANES - 1, 1)
 
     back = [along(*[read(q * NEAR + 8 * side) for side in range(3)]) for q in range(4)]
-    counts = [[read(count_place(a) + 8 * side) for side in range(3)] for a in range(EV_DEV)]
+    counts = symmetric(
+        [[read(count_place(a) + 8 * side) for side in range(3)] for a in range(EV_DEV)], turned_ref
+    )
     deriv = [
         [read(rate_place(group, station, q)) for q in range(3)]
         for group in range(4)
@@ -431,7 +444,9 @@
 
     lanes = lax.broadcasted_iota(jnp.int32, (ROWS, LANES), 1)
     mine = (lanes == device_index()).astype(jnp.float32)
-    own = dot_exact(mine, jnp.concatenate(location, axis=0), NT)
+    parts = dot_bf16(mine.astype(jnp.bfloat16), thirds(jnp.concatenate(location, axis=0)), NT)
+    rows = 4 * EV_DEV
+    own = parts[:, 0:rows] + parts[:, rows : 2 * rows] + parts[:, 2 * rows :]
     for q in range(4):
         out_ref[q : q + 1, :] = own[0:1, q * EV_DEV : (q + 1) * EV_DEV]
 
@@ -454,7 +469,7 @@
 PARAMS = pltpu.CompilerParams(vmem_limit_bytes=VMEM_BYTES)
 
 
-def pack(traces, ray_slowness, travel_time, pair_first, pair_second, pair_lag, pair_live):
+def pack(traces, ray_slowness, travel_time, pair_first, pair_second, pair_lag):
     arguments = (
         traces.reshape(TRACES_DEV, EV_DEV, LENGTH),
         ray_slowness,
@@ -466,7 +481,7 @@
     return pl.pallas_call(
         pack_kernel,
         out_shape=pltpu.VMEM((TRACES_DEV + 1, ROWS, LENGTH), jnp.float32),
-        in_specs=[SMEM] + [HBM] * 6,
+        in_specs=[HBM] * 6,
         out_specs=VMEM,
         scratch_shapes=[
             pltpu.VMEM((3, STATIONS_DEV, EV_DEV), jnp.float32),
@@ -478,10 +493,10 @@
         ],
         compiler_params=PARAMS,
         name="pack",
-    )(pair_live, *[pltpu.with_memory_space_constraint(value, pltpu.HBM) for value in arguments])
-
-
-def firsts(message):
+    )(*[pltpu.with_memory_space_constraint(value, pltpu.HBM) for value in arguments])
+
+
+def firsts(pair_live, message):
     toeplitz = jax.ShapeDtypeStruct((TRACES_DEV, EV_DEV * LAGS, SPAN), jnp.bfloat16)
     return pl.pallas_call(
         first_kernel,
@@ -492,7 +507,7 @@
             jax.ShapeDtypeStruct((PAIR_DEV, EV_DEV * LAGS), jnp.float32),
             jax.ShapeDtypeStruct((1, PAYLOAD), jnp.float32),
         ),
-        in_specs=[VMEM],
+        in_specs=[SMEM, VMEM],
         out_specs=(VMEM, VMEM, SMEM, VMEM, VMEM),
         scratch_shapes=[
             pltpu.VMEM((PLACE_ROWS, PAIR_DEV), jnp.int32),
@@ -500,7 +515,7 @@
         ],
         compiler_params=PARAMS,
         name="firsts",
-    )(message)
+    )(pair_live, message)
 
 
 MOVED = jax.ShapeDtypeStruct((TRACES_DEV * PAIR_DEV * ROWS, LANES), jnp.float32)
@@ -545,18 +560,20 @@
         ),
         in_specs=[VMEM, VMEM],
         out_specs=(VMEM, VMEM),
-        scratch_shapes=[pltpu.VMEM((PAYLOAD, LANES), jnp.float32)],
+        scratch_shapes=[
+            pltpu.VMEM((PAYLOAD, LANES), jnp.float32),
+            pltpu.VMEM((2 * EV_DEV * EV_DEV, LANES), jnp.float32),
+        ],
         compiler_params=PARAMS,
         name="solve",
     )(gathered, shift)
 
 
 def body(traces, ray_slowness, travel_time, pair_first, pair_second, pair_lag, pair_live):
-    message = pack(
-        traces, ray_slowness, travel_time, pair_first, pair_second, pair_lag, pair_live
-    )
+    message = pack(traces, ray_slowness, travel_time, pair_first, pair_second, pair_lag)
     from_cross = from_other_chip(message)
-    high, low, places, pick, rates = firsts(message)
+    pair_live = lax.optimization_barrier((message, pair_live))[1]
+    high, low, places, pick, rates = firsts(pair_live, message)
     places = pltpu.with_memory_space_constraint(places, pltpu.SMEM)
     chip = lax.all_gather(message, "c", axis=0)
     moved = early(places, chip)

time: 59.3 us -> 58.8 us (level)
  blocking collectives: 43.7 us -> 43.1 us
where the time goes in v7:
time: 58.8 us; the launch traced here: 58.6 us
  blocking collectives  43.1 us (73%)
  Pallas kernels  9.4 us (16%)
  starting transfers between devices  4.59 us (8%)
  between operations  1.35 us (2%)
    all_to_all x2, blocking collectives, spread(): return lax.all_to_all(copies, axis, 0, 0, tiled=True)  33.5 us
    all_gather x1, blocking collectives, body(): chip = lax.all_gather(message, 'c', axis=0)  4.87 us
    all_gather x1, blocking collectives, body(): gathered = lax.all_gather(spread(block, 'g'), 'c', axis=0)  4.74 us
    ppermute x1, starting transfers between devices, from_other_chip(): return lax.ppermute(block, ('g', 'c'), route)  4.59 us
    pallas_call x1, Pallas kernels, firsts(): pl.pallas_call(first_kernel, out_shape=(toeplitz, toeplitz, pltpu.SMEM((P...  2.86 us
    pallas_call x1, Pallas kernels, late(): pl.pallas_call(late_kernel, out_shape=(jax.ShapeDtypeStruct((STATIONS_DEV...  2.78 us
    pallas_call x1, Pallas kernels, solve(): pl.pallas_call(solve_kernel, out_shape=(jax.ShapeDtypeStruct((4, EV_DEV),...  1.87 us
  transfers between devices with their start and end apart: 1, of which 0 were waited for; matrix products, arithmetic and copies ran while one was open for 0% of the time, Pallas kernels for 6%

profile of v7, /device:TPU:1, one launch (start us, length us, event | category | flops | bytes accessed | tf_op | source)
XLA Modules:
  0.0 58.6 jit_solution(1115053803841703246)
XLA Ops:
  0.6 1.0 %pack.1.own_ref = f32[10,8,1024]{2,1,0:T(8,128)S(1)} custom-call(f32[9,8,1024]{2,1,0:T(8,128)} %bitcast.8, f32[3,3,8]{2,1,0:T(4,128)} %slowness_ref.1, f32[3,8]{1,0:T(4,128)} %time_ref.1, s32[1,128]{1,0:T(1,128)} %bitcast.9, s32[1,128]{1,0:T(1,128)} %bitcast.10, s32[3,128]{1,0:T(4,128)} %lag_ref.1), custom_call_target="tpu_custom_call" | custom-call | tf_op jit(solution)/shard_map/pack/pallas_call | solution.py:481
  1.7 4.6 %collective-permute-start = (f32[10,8,1024]{2,1,0:T(8,128)S(1)}, f32[10,8,1024]{2,1,0:T(8,128)S(1)}, u32[]{:S(2)}, u32[]{:S(2)}) collective-permute-start(f32[10,8,1024]{2,1,0:T(8,128)S(1)} %pack.1.own_ref), channel_id=1, source_target_pairs={{4,8},{8,4},{12,16},{16,12},{20,24},{24,20},{28,32},{32,28},{36,40... | collective-permute-start | bytes 983048 | tf_op jit(solution)/shard_map/ppermute | solution.py:458
  6.9 2.9 %firsts.1 = (bf16[9,256,640]{2,1,0:T(8,128)(2,1)S(1)}, bf16[9,256,640]{2,1,0:T(8,128)(2,1)S(1)}, s32[16,128]{1,0:T(8,128)S(4)}, f32[128,256]{1,0:T(8,128)S(1)}, f32[1,640]{1,0:T(1,128)S(1)}) custom-call(s32[1]{0:T(128)S(6)} %copy.16.live_ref, f32[10,8,1024]{2,1,0:T(8,128)S(1)} %pack.1.own_ref), custom_call_target="tpu_custom_call" | custom-call | tf_op jit(solution)/shard_map/firsts/pallas_call | solution.py:501
  9.8 4.9 %all-gather = f32[20,8,1024]{2,1,0:T(8,128)S(1)} all-gather(f32[10,8,1024]{2,1,0:T(8,128)S(1)} %pack.1.own_ref), channel_id=2, replica_groups=mesh['g'=64,'c'=2,'x'=4] {'c'}, dimensions={0}, use_global_device_ids=true | all-gather | bytes 983040 | tf_op jit(solution)/shard_map/all_gather | solution.py:578
  14.6 0.9 %early.1.moved_in_ref = f32[9216,128]{1,0:T(8,128)S(1)} custom-call(s32[16,128]{1,0:T(8,128)S(4)} %get-tuple-element.13.places_ref, f32[2,10,8,1024]{3,2,1,0:T(8,128)S(1)} %bitcast.5), custom_call_target="tpu_custom_call" | custom-call | tf_op jit(solution)/shard_map/early/pallas_call | solution.py:525
  15.5 0.0 collective-permute-done.cross_ref
  15.5 2.8 %late.1 = (f32[3,128]{1,0:T(4,128)S(1)}, f32[1,640]{1,0:T(1,128)S(1)}, f32[9216,128]{1,0:T(8,128)S(1)}) custom-call(s32[16,128]{1,0:T(8,128)S(4)} %get-tuple-element.13.places_ref, f32[9216,128]{1,0:T(8,128)S(1)} %early.1.moved_in_ref, f32[2,10,8,1024]{3,2,1,0:T(8,128)S(1)} %bitcast.6, ...), custom_call_target="tpu_custom_call", output_to_operand_aliasing={{2}: (1, {})} | custom-call | tf_op jit(solution)/shard_map/late/pallas_call | solution.py:537
  18.3 6.5 %all_to_all.12 = f32[4,1,640]{2,1,0:T(1,128)S(1)} all-to-all(f32[4,1,640]{2,1,0:T(1,128)S(1)} %broadcast_in_dim.4), channel_id=1, replica_groups=mesh['g'=64,'c'=2,'x'=4] {'x'}, dimensions={0} | all-to-all | bytes 20480 | tf_op jit(solution)/shard_map/all_to_all | solution.py:463
  24.9 0.1 broadcast_in_dim.5
  25.0 27.0 %all_to_all.13 = f32[64,1,640]{2,1,0:T(1,128)S(1)} all-to-all(f32[64,1,640]{2,1,0:T(1,128)S(1)} %broadcast_in_dim.5), channel_id=1, replica_groups=mesh['g'=64,'c'=2,'x'=4] {'g'}, dimensions={0} | all-to-all | bytes 327680 | tf_op jit(solution)/shard_map/all_to_all | solution.py:463
  52.0 4.7 %all-gather.1 = f32[128,1,640]{2,0,1:T(8,128)S(1)} all-gather(f32[64,1,640]{2,0,1:T(8,128)S(1)} %copy.13), channel_id=3, replica_groups=mesh['g'=64,'c'=2,'x'=4] {'c'}, dimensions={0}, use_global_device_ids=true | all-gather | bytes 491520 | tf_op jit(solution)/shard_map/all_gather | solution.py:583
  56.7 1.9 %solve.1 = (f32[4,8]{1,0:T(4,128)}, f32[3,128]{1,0:T(4,128)}) custom-call(f32[128,640]{1,0:T(8,128)S(1)} %bitcast.7, f32[3,128]{1,0:T(4,128)S(1)} %get-tuple-element.19.shift_ref), custom_call_target="tpu_custom_call" | custom-call | tf_op jit(solution)/shard_map/solve/pallas_call | solution.py:555
  (4 shorter events, 0.1 us)
Async XLA Ops:
  1.7 13.9 %collective-permute-start = (f32[10,8,1024]{2,1,0:T(8,128)S(1)}, f32[10,8,1024]{2,1,0:T(8,128)S(1)}, u32[]{:S(2)}, u32[]{:S(2)}) collective-permute-start(f32[10,8,1024]{2,1,0:T(8,128)S(1)} %pack.1.own_ref), channel_id=1, source_target_pairs={{4,8},{8,4},{12,16},{16,12},{20,24},{24,20},{28,32},{32,28},{36,40... | collective-permute-start | bytes 983048 | tf_op jit(solution)/shard_map/ppermute | solution.py:458

commit v8 on v7

--- a/solution.py
+++ b/solution.py
@@ -129,7 +129,7 @@
 
 
 def first_kernel(
-    live_ref, own_ref, high_ref, low_ref, places_ref, pick_ref, rates_ref, places, sem
+    live_ref, own_ref, high_ref, low_ref, places_ref, pick_ref, rates_ref
 ):
     aux = own_ref[TRACES_DEV]
     first = aux[0:1, 0:LANES].astype(jnp.int32)
@@ -160,16 +160,14 @@
     for hot in hots:
         listed.append(dot_bf16(slots, hot, NT)[0:1])
     first_windows(own_ref, high_ref, low_ref, range(2, 4))
-    places[...] = jnp.zeros((PLACE_ROWS, PAIR_DEV), jnp.int32)
-    places[0:3, :] = rows
-    places[3:6, :] = jnp.bitwise_and(begin, LANES - 1)
+    places_ref[...] = jnp.zeros((PLACE_ROWS, PAIR_DEV), jnp.int32)
+    places_ref[0:3, :] = rows
+    places_ref[3:6, :] = jnp.bitwise_and(begin, LANES - 1)
     for at in range(2):
         filled = jnp.where(lane_ids < counts[at], listed[at], listed[at][:, 0:1])
-        places[6 + at : 7 + at, :] = filled.astype(jnp.int32)
-        places[8 + at : 9 + at, :] = jnp.broadcast_to(counts[at], (1, PAIR_DEV))
-    places[10:11, :] = jnp.broadcast_to(live_ref[0], (1, PAIR_DEV))
-    move = pltpu.make_async_copy(places, places_ref, sem)
-    move.start()
+        places_ref[6 + at : 7 + at, :] = filled.astype(jnp.int32)
+        places_ref[8 + at : 9 + at, :] = jnp.broadcast_to(counts[at], (1, PAIR_DEV))
+    places_ref[10:11, :] = jnp.broadcast_to(live_ref[0], (1, PAIR_DEV))
     first_windows(own_ref, high_ref, low_ref, range(4, TRACES_DEV))
     ends = jnp.bitwise_and(first, EV_DEV - 1).astype(jnp.float32)
     column = jnp.transpose(jnp.broadcast_to(ends, (LANES, PAIR_DEV)))
@@ -187,7 +185,6 @@
                 rates_ref[:, at : at + EV_DEV] = jnp.where(
                     lax.axis_index("x") == group, own, 0.0
                 )
-    move.wait()
 
 
 def fill_table(ref, table_ref, part):
@@ -223,11 +220,14 @@
     return lax.div(count + (GROUP - 1), GROUP)
 
 
-def early_kernel(places_ref, chip_ref, moved_ref, table_ref):
+def early_kernel(listed_ref, chip_ref, moved_ref, places_ref, table_ref, sem):
+    fetch = pltpu.make_async_copy(listed_ref, places_ref, sem)
+    fetch.start()
     table_ref[pl.ds(2 * PART_ROWS, 2 * ROWS), :] = jnp.zeros((2 * ROWS, LANES), jnp.float32)
     core = lax.axis_index("c")
     fill_table(chip_ref.at[core], table_ref, 0)
     fill_table(chip_ref.at[1 - core], table_ref, 1)
+    fetch.wait()
 
     def step(index, carry):
         for turn in range(GROUP):
@@ -503,31 +503,30 @@
         out_shape=(
             toeplitz,
             toeplitz,
-            pltpu.SMEM((PLACE_ROWS, PAIR_DEV), jnp.int32),
+            jax.ShapeDtypeStruct((PLACE_ROWS, PAIR_DEV), jnp.int32),
             jax.ShapeDtypeStruct((PAIR_DEV, EV_DEV * LAGS), jnp.float32),
             jax.ShapeDtypeStruct((1, PAYLOAD), jnp.float32),
         ),
         in_specs=[SMEM, VMEM],
-        out_specs=(VMEM, VMEM, SMEM, VMEM, VMEM),
-        scratch_shapes=[
-            pltpu.VMEM((PLACE_ROWS, PAIR_DEV), jnp.int32),
-            pltpu.SemaphoreType.DMA,
-        ],
+        out_specs=(VMEM,) * 5,
         compiler_params=PARAMS,
         name="firsts",
     )(pair_live, message)
 
 
-MOVED = jax.ShapeDtypeStruct((TRACES_DEV * PAIR_DEV * ROWS, LANES), jnp.float32)
+MOVED = jax.ShapeDtypeStruct((TRACES_DEV * PAIR_DEV * ROWS + ROWS, LANES), jnp.float32)
 
 
 def early(places, chip):
     return pl.pallas_call(
         early_kernel,
-        out_shape=MOVED,
-        in_specs=[SMEM, VMEM],
-        out_specs=VMEM,
-        scratch_shapes=[pltpu.VMEM((2 * PART_ROWS + 2 * ROWS, LANES), jnp.float32)],
+        out_shape=(MOVED, pltpu.SMEM((PLACE_ROWS, PAIR_DEV), jnp.int32)),
+        in_specs=[VMEM, VMEM],
+        out_specs=(VMEM, SMEM),
+        scratch_shapes=[
+            pltpu.VMEM((2 * PART_ROWS + 2 * ROWS, LANES), jnp.float32),
+            pltpu.SemaphoreType.DMA,
+        ],
         compiler_params=PARAMS,
         name="early",
     )(places, chip)
@@ -561,8 +560,8 @@
         in_specs=[VMEM, VMEM],
         out_specs=(VMEM, VMEM),
         scratch_shapes=[
-            pltpu.VMEM((PAYLOAD, LANES), jnp.float32),
-            pltpu.VMEM((2 * EV_DEV * EV_DEV, LANES), jnp.float32),
+            pltpu.VMEM((PAYLOAD + ROWS, LANES), jnp.float32),
+            pltpu.VMEM((2 * EV_DEV * EV_DEV + ROWS, LANES), jnp.float32),
         ],
         compiler_params=PARAMS,
         name="solve",
@@ -574,9 +573,9 @@
     from_cross = from_other_chip(message)
     pair_live = lax.optimization_barrier((message, pair_live))[1]
     high, low, places, pick, rates = firsts(pair_live, message)
+    chip = lax.all_gather(message, "c", axis=0)
+    moved, places = early(places, chip)
     places = pltpu.with_memory_space_constraint(places, pltpu.SMEM)
-    chip = lax.all_gather(message, "c", axis=0)
-    moved = early(places, chip)
     shift, block = late(places, moved, chip, from_cross, high, low, pick, rates)
     block = jnp.sum(spread(block, "x"), axis=0, keepdims=True)
     chips = lax.axis_size("g")

time: 58.8 us -> 58.7 us (level)
  blocking collectives: 43.1 us -> 42.2 us
  Pallas kernels: 9.4 us -> 10.2 us
    all_to_all x2, blocking collectives: 33.5 us -> 32.6 us  [spread(): return lax.all_to_all(copies, axis, 0, 0, tiled=True)]
    pallas_call x2, Pallas kernels: 3.72 us -> 4.32 us  [the longest x1 2.28 us: firsts(): pl.pallas_call(first_kernel, out_shape=(toeplitz, toeplitz, jax.ShapeDtyp...]
  transfers between devices with their start and end apart: 1 -> 1, of which waited for: 0 -> 0; matrix products, arithmetic and copies ran while one was open for 0% -> 0% of each run, Pallas kernels for 6% -> 7%
where the time goes in v8:
time: 58.7 us; the launch traced here: 58.5 us
  blocking collectives  42.2 us (72%)
  Pallas kernels  10.2 us (17%)
  starting transfers between devices  4.59 us (8%)
  between operations  1.35 us (2%)
    all_to_all x2, blocking collectives, spread(): return lax.all_to_all(copies, axis, 0, 0, tiled=True)  32.6 us
    all_gather x1, blocking collectives, body(): chip = lax.all_gather(message, 'c', axis=0)  4.86 us
    all_gather x1, blocking collectives, body(): gathered = lax.all_gather(spread(block, 'g'), 'c', axis=0)  4.69 us
    ppermute x1, starting transfers between devices, from_other_chip(): return lax.ppermute(block, ('g', 'c'), route)  4.59 us
    pallas_call x1, Pallas kernels, late(): pl.pallas_call(late_kernel, out_shape=(jax.ShapeDtypeStruct((STATIONS_DEV...  2.98 us
    pallas_call x1, Pallas kernels, firsts(): pl.pallas_call(first_kernel, out_shape=(toeplitz, toeplitz, jax.ShapeDtyp...  2.28 us
    pallas_call x1, Pallas kernels, early(): pl.pallas_call(early_kernel, out_shape=(MOVED, pltpu.SMEM((PLACE_ROWS, PA...  2.04 us
    pallas_call x1, Pallas kernels, solve(): pl.pallas_call(solve_kernel, out_shape=(jax.ShapeDtypeStruct((4, EV_DEV),...  1.87 us
  transfers between devices with their start and end apart: 1, of which 0 were waited for; matrix products, arithmetic and copies ran while one was open for 0% of the time, Pallas kernels for 7%

profile of v8, /device:TPU:1, one launch (start us, length us, event | category | flops | bytes accessed | tf_op | source)
XLA Modules:
  0.0 58.5 jit_solution(7411506808817582100)
XLA Ops:
  0.6 1.0 %pack.1.own_ref = f32[10,8,1024]{2,1,0:T(8,128)S(1)} custom-call(f32[9,8,1024]{2,1,0:T(8,128)} %bitcast.8, f32[3,3,8]{2,1,0:T(4,128)} %slowness_ref.1, f32[3,8]{1,0:T(4,128)} %time_ref.1, s32[1,128]{1,0:T(1,128)} %bitcast.9, s32[1,128]{1,0:T(1,128)} %bitcast.10, s32[3,128]{1,0:T(4,128)} %lag_ref.1), custom_call_target="tpu_custom_call" | custom-call | tf_op jit(solution)/shard_map/pack/pallas_call | solution.py:481
  1.7 4.6 %collective-permute-start = (f32[10,8,1024]{2,1,0:T(8,128)S(1)}, f32[10,8,1024]{2,1,0:T(8,128)S(1)}, u32[]{:S(2)}, u32[]{:S(2)}) collective-permute-start(f32[10,8,1024]{2,1,0:T(8,128)S(1)} %pack.1.own_ref), channel_id=1, source_target_pairs={{4,8},{8,4},{12,16},{16,12},{20,24},{24,20},{28,32},{32,28},{36,40... | collective-permute-start | bytes 983048 | tf_op jit(solution)/shard_map/ppermute | solution.py:458
  6.9 2.3 %firsts.1 = (bf16[9,256,640]{2,1,0:T(8,128)(2,1)S(1)}, bf16[9,256,640]{2,1,0:T(8,128)(2,1)S(1)}, s32[16,128]{1,0:T(8,128)S(1)}, f32[128,256]{1,0:T(8,128)S(1)}, f32[1,640]{1,0:T(1,128)S(1)}) custom-call(s32[1]{0:T(128)S(6)} %copy.16.live_ref, f32[10,8,1024]{2,1,0:T(8,128)S(1)} %pack.1.own_ref), custom_call_target="tpu_custom_call" | custom-call | tf_op jit(solution)/shard_map/firsts/pallas_call | solution.py:501
  9.2 4.9 %all-gather = f32[20,8,1024]{2,1,0:T(8,128)S(1)} all-gather(f32[10,8,1024]{2,1,0:T(8,128)S(1)} %pack.1.own_ref), channel_id=2, replica_groups=mesh['g'=64,'c'=2,'x'=4] {'c'}, dimensions={0}, use_global_device_ids=true | all-gather | bytes 983040 | tf_op jit(solution)/shard_map/all_gather | solution.py:576
  14.0 2.0 %early.1 = (f32[9224,128]{1,0:T(8,128)S(1)}, s32[16,128]{1,0:T(8,128)S(4)}) custom-call(s32[16,128]{1,0:T(8,128)S(1)} %get-tuple-element.15.listed_ref, f32[2,10,8,1024]{3,2,1,0:T(8,128)S(1)} %bitcast.5), custom_call_target="tpu_custom_call" | custom-call | tf_op jit(solution)/shard_map/early/pallas_call | solution.py:521
  16.1 0.0 collective-permute-done.cross_ref
  16.1 3.0 %late.1 = (f32[3,128]{1,0:T(4,128)S(1)}, f32[1,640]{1,0:T(1,128)S(1)}, f32[9224,128]{1,0:T(8,128)S(1)}) custom-call(s32[16,128]{1,0:T(8,128)S(4)} %get-tuple-element.16.places_ref, f32[9224,128]{1,0:T(8,128)S(1)} %get-tuple-element.17.moved_in_ref, f32[2,10,8,1024]{3,2,1,0:T(8,128)S(1)} %bitcast.6, ...), custom_call_target="tpu_custom_call", output_to_operand_aliasing={{2}: (1, {})} | custom-call | tf_op jit(solution)/shard_map/late/pallas_call | solution.py:536
  19.1 6.5 %all_to_all.12 = f32[4,1,640]{2,1,0:T(1,128)S(1)} all-to-all(f32[4,1,640]{2,1,0:T(1,128)S(1)} %broadcast_in_dim.4), channel_id=1, replica_groups=mesh['g'=64,'c'=2,'x'=4] {'x'}, dimensions={0} | all-to-all | bytes 20480 | tf_op jit(solution)/shard_map/all_to_all | solution.py:463
  25.7 0.1 broadcast_in_dim.5
  25.8 26.1 %all_to_all.13 = f32[64,1,640]{2,1,0:T(1,128)S(1)} all-to-all(f32[64,1,640]{2,1,0:T(1,128)S(1)} %broadcast_in_dim.5), channel_id=1, replica_groups=mesh['g'=64,'c'=2,'x'=4] {'g'}, dimensions={0} | all-to-all | bytes 327680 | tf_op jit(solution)/shard_map/all_to_all | solution.py:463
  51.9 4.7 %all-gather.1 = f32[128,1,640]{2,0,1:T(8,128)S(1)} all-gather(f32[64,1,640]{2,0,1:T(8,128)S(1)} %copy.13), channel_id=3, replica_groups=mesh['g'=64,'c'=2,'x'=4] {'c'}, dimensions={0}, use_global_device_ids=true | all-gather | bytes 491520 | tf_op jit(solution)/shard_map/all_gather | solution.py:582
  56.6 1.9 %solve.1 = (f32[4,8]{1,0:T(4,128)}, f32[3,128]{1,0:T(4,128)}) custom-call(f32[128,640]{1,0:T(8,128)S(1)} %bitcast.7, f32[3,128]{1,0:T(4,128)S(1)} %get-tuple-element.23.shift_ref), custom_call_target="tpu_custom_call" | custom-call | tf_op jit(solution)/shard_map/solve/pallas_call | solution.py:554
  (4 shorter events, 0.1 us)
Async XLA Ops:
  1.7 14.4 %collective-permute-start = (f32[10,8,1024]{2,1,0:T(8,128)S(1)}, f32[10,8,1024]{2,1,0:T(8,128)S(1)}, u32[]{:S(2)}, u32[]{:S(2)}) collective-permute-start(f32[10,8,1024]{2,1,0:T(8,128)S(1)} %pack.1.own_ref), channel_id=1, source_target_pairs={{4,8},{8,4},{12,16},{16,12},{20,24},{24,20},{28,32},{32,28},{36,40... | collective-permute-start | bytes 983048 | tf_op jit(solution)/shard_map/ppermute | solution.py:458

commit v9 on v8

--- a/solution.py
+++ b/solution.py
@@ -23,6 +23,7 @@
 PART_ROWS = TRACES_DEV * EV_DEV * CHUNKS
 VMEM_BYTES = 24 * 1024 * 1024
 PLACE_ROWS = 16
+FIRST_ITEMS = 3
 GROUP = 16
 PAYLOAD = 5 * LANES
 SQUARE_AT = 4 * NEAR
@@ -120,12 +121,13 @@
         power = jnp.sum(window * window, axis=1, keepdims=True)
         window = window * lax.rsqrt(power + eps_small)
         padded = jnp.concatenate([window, jnp.zeros((EV_DEV, LANES), jnp.float32)], axis=1)
+        at = item - items[0]
         for event in range(EV_DEV):
             wide = jnp.broadcast_to(padded[event : event + 1], (LAGS, SPAN))
             wide = pltpu.roll(wide, 0, 1, stride=1, stride_axis=0)
             high, low = split_bf16(wide)
-            high_ref[item, pl.ds(event * LAGS, LAGS), :] = high
-            low_ref[item, pl.ds(event * LAGS, LAGS), :] = low
+            high_ref[at, pl.ds(event * LAGS, LAGS), :] = high
+            low_ref[at, pl.ds(event * LAGS, LAGS), :] = low
 
 
 def first_kernel(
@@ -156,10 +158,8 @@
         place = jnp.where(marked, dot_bf16(wide, ahead, NN)[0:1] - 1.0, -1.0)
         hots.append((upper.astype(jnp.float32) == place).astype(jnp.bfloat16))
         counts.append(jnp.sum(ones, axis=1, keepdims=True).astype(jnp.int32))
-    first_windows(own_ref, high_ref, low_ref, range(2))
     for hot in hots:
         listed.append(dot_bf16(slots, hot, NT)[0:1])
-    first_windows(own_ref, high_ref, low_ref, range(2, 4))
     places_ref[...] = jnp.zeros((PLACE_ROWS, PAIR_DEV), jnp.int32)
     places_ref[0:3, :] = rows
     places_ref[3:6, :] = jnp.bitwise_and(begin, LANES - 1)
@@ -168,7 +168,7 @@
         places_ref[6 + at : 7 + at, :] = filled.astype(jnp.int32)
         places_ref[8 + at : 9 + at, :] = jnp.broadcast_to(counts[at], (1, PAIR_DEV))
     places_ref[10:11, :] = jnp.broadcast_to(live_ref[0], (1, PAIR_DEV))
-    first_windows(own_ref, high_ref, low_ref, range(4, TRACES_DEV))
+    first_windows(own_ref, high_ref, low_ref, range(FIRST_ITEMS))
     ends = jnp.bitwise_and(first, EV_DEV - 1).astype(jnp.float32)
     column = jnp.transpose(jnp.broadcast_to(ends, (LANES, PAIR_DEV)))
     groups = lax.broadcasted_iota(jnp.int32, (PAIR_DEV, LANES), 1) // LAGS
@@ -220,11 +220,14 @@
     return lax.div(count + (GROUP - 1), GROUP)
 
 
-def early_kernel(listed_ref, chip_ref, moved_ref, places_ref, table_ref, sem):
+def early_kernel(
+    listed_ref, chip_ref, moved_ref, places_ref, high_ref, low_ref, table_ref, sem
+):
     fetch = pltpu.make_async_copy(listed_ref, places_ref, sem)
     fetch.start()
     table_ref[pl.ds(2 * PART_ROWS, 2 * ROWS), :] = jnp.zeros((2 * ROWS, LANES), jnp.float32)
     core = lax.axis_index("c")
+    first_windows(chip_ref.at[core], high_ref, low_ref, range(FIRST_ITEMS, TRACES_DEV))
     fill_table(chip_ref.at[core], table_ref, 0)
     fill_table(chip_ref.at[1 - core], table_ref, 1)
     fetch.wait()
@@ -257,6 +260,8 @@
     cross_ref,
     high_ref,
     low_ref,
+    last_high_ref,
+    last_low_ref,
     pick_ref,
     rates_ref,
     shift_ref,
@@ -294,8 +299,13 @@
                 for chunk in range(SPAN_CHUNKS)
             ]
             high, low = split_bf16(jnp.concatenate(pieces, axis=1))
-            both = dot_bf16(jnp.concatenate([high, low], axis=0), high_ref[item], NT)
-            xcorr = both[0:PAIR_DEV] + both[PAIR_DEV:] + dot_bf16(high, low_ref[item], NT)
+            if item < FIRST_ITEMS:
+                first_high, first_low = high_ref[item], low_ref[item]
+            else:
+                first_high = last_high_ref[item - FIRST_ITEMS]
+                first_low = last_low_ref[item - FIRST_ITEMS]
+            both = dot_bf16(jnp.concatenate([high, low], axis=0), first_high, NT)
+            xcorr = both[0:PAIR_DEV] + both[PAIR_DEV:] + dot_bf16(high, first_low, NT)
             energy = energy + xcorr * xcorr
         energy = energy * pick_ref[...]
         energy = energy[:, 0:LANES] + energy[:, LANES:]
@@ -497,7 +507,7 @@
 
 
 def firsts(pair_live, message):
-    toeplitz = jax.ShapeDtypeStruct((TRACES_DEV, EV_DEV * LAGS, SPAN), jnp.bfloat16)
+    toeplitz = jax.ShapeDtypeStruct((FIRST_ITEMS, EV_DEV * LAGS, SPAN), jnp.bfloat16)
     return pl.pallas_call(
         first_kernel,
         out_shape=(
@@ -518,11 +528,14 @@
 
 
 def early(places, chip):
+    toeplitz = jax.ShapeDtypeStruct(
+        (TRACES_DEV - FIRST_ITEMS, EV_DEV * LAGS, SPAN), jnp.bfloat16
+    )
     return pl.pallas_call(
         early_kernel,
-        out_shape=(MOVED, pltpu.SMEM((PLACE_ROWS, PAIR_DEV), jnp.int32)),
+        out_shape=(MOVED, pltpu.SMEM((PLACE_ROWS, PAIR_DEV), jnp.int32), toeplitz, toeplitz),
         in_specs=[VMEM, VMEM],
-        out_specs=(VMEM, SMEM),
+        out_specs=(VMEM, SMEM, VMEM, VMEM),
         scratch_shapes=[
             pltpu.VMEM((2 * PART_ROWS + 2 * ROWS, LANES), jnp.float32),
             pltpu.SemaphoreType.DMA,
@@ -532,7 +545,7 @@
     )(places, chip)
 
 
-def late(places, moved, chip, from_cross, high, low, pick, rates):
+def late(places, moved, chip, from_cross, toeplitz, pick, rates):
     refined_shift, block, _ = pl.pallas_call(
         late_kernel,
         out_shape=(
@@ -540,13 +553,13 @@
             jax.ShapeDtypeStruct((1, PAYLOAD), jnp.float32),
             MOVED,
         ),
-        in_specs=[SMEM] + [VMEM] * 7,
+        in_specs=[SMEM] + [VMEM] * 9,
         out_specs=(VMEM, VMEM, VMEM),
         scratch_shapes=[pltpu.VMEM((PART_ROWS + 2 * ROWS, LANES), jnp.float32)],
         input_output_aliases={1: 2},
         compiler_params=PARAMS,
         name="late",
-    )(places, moved, chip, from_cross, high, low, pick, rates)
+    )(places, moved, chip, from_cross, *toeplitz, pick, rates)
     return refined_shift, block
 
 
@@ -574,9 +587,10 @@
     pair_live = lax.optimization_barrier((message, pair_live))[1]
     high, low, places, pick, rates = firsts(pair_live, message)
     chip = lax.all_gather(message, "c", axis=0)
-    moved, places = early(places, chip)
+    moved, places, last_high, last_low = early(places, chip)
     places = pltpu.with_memory_space_constraint(places, pltpu.SMEM)
-    shift, block = late(places, moved, chip, from_cross, high, low, pick, rates)
+    toeplitz = (high, low, last_high, last_low)
+    shift, block = late(places, moved, chip, from_cross, toeplitz, pick, rates)
     block = jnp.sum(spread(block, "x"), axis=0, keepdims=True)
     chips = lax.axis_size("g")
     gathered = lax.all_gather(spread(block, "g"), "c", axis=0)

time: 58.7 us -> 58.7 us (level)
    pallas_call x1, Pallas kernels: 2.28 us -> 0.85 us  [firsts(): pl.pallas_call(first_kernel, out_shape=(toeplitz, toeplitz, jax.ShapeDtyp...]
    pallas_call x1, Pallas kernels: 2.04 us -> 2.98 us  [early(): pl.pallas_call(early_kernel, out_shape=(MOVED, pltpu.SMEM((PLACE_ROWS, PA...]
where the time goes in v9:
time: 58.7 us; the launch traced here: 58.5 us
  blocking collectives  42.4 us (72%)
  Pallas kernels  9.98 us (17%)
  starting transfers between devices  4.59 us (8%)
  between operations  1.35 us (2%)
    all_to_all x2, blocking collectives, spread(): return lax.all_to_all(copies, axis, 0, 0, tiled=True)  32.4 us
    all_gather x1, blocking collectives, body(): gathered = lax.all_gather(spread(block, 'g'), 'c', axis=0)  5.12 us
    all_gather x1, blocking collectives, body(): chip = lax.all_gather(message, 'c', axis=0)  4.87 us
    ppermute x1, starting transfers between devices, from_other_chip(): return lax.ppermute(block, ('g', 'c'), route)  4.59 us
    pallas_call x1, Pallas kernels, late(): pl.pallas_call(late_kernel, out_shape=(jax.ShapeDtypeStruct((STATIONS_DEV...  3.25 us
    pallas_call x1, Pallas kernels, early(): pl.pallas_call(early_kernel, out_shape=(MOVED, pltpu.SMEM((PLACE_ROWS, PA...  2.98 us
    pallas_call x1, Pallas kernels, solve(): pl.pallas_call(solve_kernel, out_shape=(jax.ShapeDtypeStruct((4, EV_DEV),...  1.87 us
  transfers between devices with their start and end apart: 1, of which 0 were waited for; matrix products, arithmetic and copies ran while one was open for 0% of the time, Pallas kernels for 7%

profile of v9, /device:TPU:1, one launch (start us, length us, event | category | flops | bytes accessed | tf_op | source)
XLA Modules:
  0.0 58.5 jit_solution(4631570902893122655)
XLA Ops:
  0.6 1.0 %pack.1.own_ref = f32[10,8,1024]{2,1,0:T(8,128)S(1)} custom-call(f32[9,8,1024]{2,1,0:T(8,128)} %bitcast.8, f32[3,3,8]{2,1,0:T(4,128)} %slowness_ref.1, f32[3,8]{1,0:T(4,128)} %time_ref.1, s32[1,128]{1,0:T(1,128)} %bitcast.9, s32[1,128]{1,0:T(1,128)} %bitcast.10, s32[3,128]{1,0:T(4,128)} %lag_ref.1), custom_call_target="tpu_custom_call" | custom-call | tf_op jit(solution)/shard_map/pack/pallas_call | solution.py:491
  1.7 4.6 %collective-permute-start = (f32[10,8,1024]{2,1,0:T(8,128)S(1)}, f32[10,8,1024]{2,1,0:T(8,128)S(1)}, u32[]{:S(2)}, u32[]{:S(2)}) collective-permute-start(f32[10,8,1024]{2,1,0:T(8,128)S(1)} %pack.1.own_ref), channel_id=1, source_target_pairs={{4,8},{8,4},{12,16},{16,12},{20,24},{24,20},{28,32},{32,28},{36,40... | collective-permute-start | bytes 983048 | tf_op jit(solution)/shard_map/ppermute | solution.py:468
  6.9 0.9 %firsts.1 = (bf16[3,256,640]{2,1,0:T(8,128)(2,1)S(1)}, bf16[3,256,640]{2,1,0:T(8,128)(2,1)S(1)}, s32[16,128]{1,0:T(8,128)S(1)}, f32[128,256]{1,0:T(8,128)S(1)}, f32[1,640]{1,0:T(1,128)S(1)}) custom-call(s32[1]{0:T(128)S(6)} %copy.16.live_ref, f32[10,8,1024]{2,1,0:T(8,128)S(1)} %pack.1.own_ref), custom_call_target="tpu_custom_call" | custom-call | tf_op jit(solution)/shard_map/firsts/pallas_call | solution.py:511
  7.8 4.9 %all-gather = f32[20,8,1024]{2,1,0:T(8,128)S(1)} all-gather(f32[10,8,1024]{2,1,0:T(8,128)S(1)} %pack.1.own_ref), channel_id=2, replica_groups=mesh['g'=64,'c'=2,'x'=4] {'c'}, dimensions={0}, use_global_device_ids=true | all-gather | bytes 983040 | tf_op jit(solution)/shard_map/all_gather | solution.py:589
  12.6 3.0 %early.1 = (f32[9224,128]{1,0:T(8,128)S(1)}, s32[16,128]{1,0:T(8,128)S(4)}, bf16[6,256,640]{2,1,0:T(8,128)(2,1)S(1)}, bf16[6,256,640]{2,1,0:T(8,128)(2,1)S(1)}) custom-call(s32[16,128]{1,0:T(8,128)S(1)} %get-tuple-element.17.listed_ref, f32[2,10,8,1024]{3,2,1,0:T(8,128)S(1)} %bitcast.5), custom_call_target="tpu_custom_call" | custom-call | tf_op jit(solution)/shard_map/early/pallas_call | solution.py:534
  15.6 0.0 collective-permute-done.cross_ref
  15.6 3.3 %late.1 = (f32[3,128]{1,0:T(4,128)S(1)}, f32[1,640]{1,0:T(1,128)S(1)}, f32[9224,128]{1,0:T(8,128)S(1)}) custom-call(s32[16,128]{1,0:T(8,128)S(4)} %get-tuple-element.18.places_ref, f32[9224,128]{1,0:T(8,128)S(1)} %get-tuple-element.19.moved_in_ref, f32[2,10,8,1024]{3,2,1,0:T(8,128)S(1)} %bitcast.6, ...), custom_call_target="tpu_custom_call", output_to_operand_aliasing={{2}: (1, {})} | custom-call | tf_op jit(solution)/shard_map/late/pallas_call | solution.py:549
  18.9 6.5 %all_to_all.12 = f32[4,1,640]{2,1,0:T(1,128)S(1)} all-to-all(f32[4,1,640]{2,1,0:T(1,128)S(1)} %broadcast_in_dim.4), channel_id=1, replica_groups=mesh['g'=64,'c'=2,'x'=4] {'x'}, dimensions={0} | all-to-all | bytes 20480 | tf_op jit(solution)/shard_map/all_to_all | solution.py:473
  25.5 0.1 broadcast_in_dim.5
  25.6 25.9 %all_to_all.13 = f32[64,1,640]{2,1,0:T(1,128)S(1)} all-to-all(f32[64,1,640]{2,1,0:T(1,128)S(1)} %broadcast_in_dim.5), channel_id=1, replica_groups=mesh['g'=64,'c'=2,'x'=4] {'g'}, dimensions={0} | all-to-all | bytes 327680 | tf_op jit(solution)/shard_map/all_to_all | solution.py:473
  51.5 5.1 %all-gather.1 = f32[128,1,640]{2,0,1:T(8,128)S(1)} all-gather(f32[64,1,640]{2,0,1:T(8,128)S(1)} %copy.13), channel_id=3, replica_groups=mesh['g'=64,'c'=2,'x'=4] {'c'}, dimensions={0}, use_global_device_ids=true | all-gather | bytes 491520 | tf_op jit(solution)/shard_map/all_gather | solution.py:596
  56.6 1.9 %solve.1 = (f32[4,8]{1,0:T(4,128)}, f32[3,128]{1,0:T(4,128)}) custom-call(f32[128,640]{1,0:T(8,128)S(1)} %bitcast.7, f32[3,128]{1,0:T(4,128)S(1)} %get-tuple-element.27.shift_ref), custom_call_target="tpu_custom_call" | custom-call | tf_op jit(solution)/shard_map/solve/pallas_call | solution.py:567
  (4 shorter events, 0.1 us)
Async XLA Ops:
  1.7 14.0 %collective-permute-start = (f32[10,8,1024]{2,1,0:T(8,128)S(1)}, f32[10,8,1024]{2,1,0:T(8,128)S(1)}, u32[]{:S(2)}, u32[]{:S(2)}) collective-permute-start(f32[10,8,1024]{2,1,0:T(8,128)S(1)} %pack.1.own_ref), channel_id=1, source_target_pairs={{4,8},{8,4},{12,16},{16,12},{20,24},{24,20},{28,32},{32,28},{36,40... | collective-permute-start | bytes 983048 | tf_op jit(solution)/shard_map/ppermute | solution.py:468

commit v10 on v9

--- a/solution.py
+++ b/solution.py
@@ -24,6 +24,8 @@
 VMEM_BYTES = 24 * 1024 * 1024
 PLACE_ROWS = 16
 FIRST_ITEMS = 3
+TILES = TRACES_DEV * CHUNKS + 1
+AUX = TILES - 1
 GROUP = 16
 PAYLOAD = 5 * LANES
 SQUARE_AT = 4 * NEAR
@@ -51,12 +53,15 @@
     return 3 * LANES + 8 * index if index < 32 else 2 * LANES + 96 + 8 * (index - 32)
 
 
+def rounded(values):
+    return values.astype(jnp.bfloat16).astype(jnp.float32)
+
+
 def thirds(values):
-    high = values.astype(jnp.bfloat16)
-    rest = values - high.astype(jnp.float32)
-    middle = rest.astype(jnp.bfloat16)
-    low = (rest - middle.astype(jnp.float32)).astype(jnp.bfloat16)
-    return jnp.concatenate([high, middle, low], axis=0)
+    high = rounded(values)
+    middle = rounded(values - high)
+    low = values - high - middle
+    return jnp.concatenate([high, middle, low], axis=0).astype(jnp.bfloat16)
 
 
 def dot_signs(left, signs, dims):
@@ -87,7 +92,7 @@
     sems,
 ):
     pairs = [
-        (traces_ref, out_ref.at[pl.ds(0, TRACES_DEV)]),
+        (traces_ref, out_ref.at[pl.ds(0, AUX)]),
         (slowness_ref, slowness),
         (time_ref, time),
         (first_ref, first),
@@ -100,24 +105,25 @@
     ]
     for copy in copies:
         copy.start()
-    aux = out_ref.at[TRACES_DEV]
-    aux[...] = jnp.zeros((ROWS, LENGTH), jnp.float32)
+    aux = out_ref.at[AUX]
+    aux[...] = jnp.zeros((ROWS, LANES), jnp.float32)
     for copy in copies[1:]:
         copy.wait()
     base = device_index() * EV_DEV - EV_DEV
+    aux[0:STATIONS_DEV, 0:EV_DEV] = time[...]
+    for q in range(3):
+        lane = (1 + q) * EV_DEV
+        aux[0:STATIONS_DEV, lane : lane + EV_DEV] = slowness[q]
     for row, ids in enumerate((first, second)):
-        aux[row : row + 1, 0:LANES] = (ids[...] - base).astype(jnp.float32)
-    aux[0:STATIONS_DEV, LANES : LANES + EV_DEV] = time[...]
-    for q in range(3):
-        lane = (2 + q) * LANES
-        aux[0:STATIONS_DEV, lane : lane + EV_DEV] = slowness[q]
-    aux[0:STATIONS_DEV, 5 * LANES : 6 * LANES] = lag[...].astype(jnp.float32)
+        aux[3 + row : 4 + row, :] = (ids[...] - base).astype(jnp.float32)
+    aux[5:8, :] = lag[...].astype(jnp.float32)
     copies[0].wait()
 
 
 def first_windows(own_ref, high_ref, low_ref, items):
     for item in items:
-        window = own_ref[item, :, QUARTER : QUARTER + WINDOW]
+        tiles = [own_ref[item * CHUNKS + chunk] for chunk in range(2, 6)]
+        window = jnp.concatenate(tiles, axis=1)
         power = jnp.sum(window * window, axis=1, keepdims=True)
         window = window * lax.rsqrt(power + eps_small)
         padded = jnp.concatenate([window, jnp.zeros((EV_DEV, LANES), jnp.float32)], axis=1)
@@ -133,10 +139,10 @@
 def first_kernel(
     live_ref, own_ref, high_ref, low_ref, places_ref, pick_ref, rates_ref
 ):
-    aux = own_ref[TRACES_DEV]
-    first = aux[0:1, 0:LANES].astype(jnp.int32)
-    second = aux[1:2, 0:LANES].astype(jnp.int32)
-    begin = aux[0:STATIONS_DEV, 5 * LANES : 6 * LANES].astype(jnp.int32) + (QUARTER - LAGS // 2)
+    aux = own_ref[AUX]
+    first = aux[3:4].astype(jnp.int32)
+    second = aux[4:5].astype(jnp.int32)
+    begin = aux[5:8].astype(jnp.int32) + (QUARTER - LAGS // 2)
     side = lax.shift_right_arithmetic(second, 3)
     mate_side = 2 - 2 * lax.axis_index("c")
     away = jnp.logical_and(side != 1, side != mate_side)
@@ -178,7 +184,7 @@
     rates_ref[...] = jnp.zeros((1, PAYLOAD), jnp.float32)
     for station in range(STATIONS_DEV):
         for q in range(3):
-            lane = (2 + q) * LANES
+            lane = (1 + q) * EV_DEV
             own = aux[station : station + 1, lane : lane + EV_DEV]
             for group in range(4):
                 at = rate_place(group, station, q)
@@ -189,14 +195,14 @@
 
 def fill_table(ref, table_ref, part):
     for item in range(TRACES_DEV):
-        values = ref[item]
-        power = jnp.sum(values * values, axis=1, keepdims=True)
-        values = values * lax.rsqrt(power + eps_small)
+        tiles = [ref[item * CHUNKS + chunk] for chunk in range(CHUNKS)]
+        squares = tiles[0] * tiles[0]
+        for tile in tiles[1:]:
+            squares = squares + tile * tile
+        scale = lax.rsqrt(jnp.sum(squares, axis=1, keepdims=True) + eps_small)
         for chunk in range(CHUNKS):
             start = part * PART_ROWS + item * EV_DEV * CHUNKS + chunk
-            table_ref[pl.ds(start, EV_DEV, stride=CHUNKS), :] = values[
-                :, chunk * LANES : (chunk + 1) * LANES
-            ]
+            table_ref[pl.ds(start, EV_DEV, stride=CHUNKS), :] = tiles[chunk] * scale
 
 
 def align(places_ref, table_ref, moved_ref, slot, offset):
@@ -242,12 +248,12 @@
 
 def incidence(aux):
     events = lax.broadcasted_iota(jnp.int32, (NEAR, PAIR_DEV), 0).astype(jnp.float32)
-    starts = (events == aux[0:1, 0:LANES]).astype(jnp.float32)
-    return starts - (events == aux[1:2, 0:LANES]).astype(jnp.float32)
+    starts = (events == aux[3:4]).astype(jnp.float32)
+    return starts - (events == aux[4:5]).astype(jnp.float32)
 
 
 def near_block(left, own, right, part):
-    lane = part * LANES
+    lane = part * EV_DEV
     return jnp.concatenate(
         [aux[0:STATIONS_DEV, lane : lane + EV_DEV] for aux in (left, own, right)], axis=1
     )
@@ -282,9 +288,9 @@
     lax.fori_loop(0, groups_of(places_ref[8, 0]), step, 0)
 
     core = lax.axis_index("c")
-    aux_own = chip_ref[core, TRACES_DEV]
-    aux_left = jnp.where(core == 0, cross_ref[TRACES_DEV], chip_ref[0, TRACES_DEV])
-    aux_right = jnp.where(core == 0, chip_ref[1, TRACES_DEV], cross_ref[TRACES_DEV])
+    aux_own = chip_ref[core, AUX]
+    aux_left = jnp.where(core == 0, cross_ref[AUX], chip_ref[0, AUX])
+    aux_right = jnp.where(core == 0, chip_ref[1, AUX], cross_ref[AUX])
 
     lane_ids = lax.broadcasted_iota(jnp.int32, (1, LANES), 1)
     centred = (lane_ids - LAGS // 2).astype(jnp.float32)
@@ -324,12 +330,14 @@
     shift = jnp.where(alive, jnp.concatenate(station_shift, axis=0), 0.0)
     shift_ref[...] = shift
 
-    signs = jnp.where(alive, incidence(aux_own), 0.0).astype(jnp.bfloat16)
-    times = dot_signs(near_block(aux_left, aux_own, aux_right, 1), signs, NN)
-    lags = aux_own[0:STATIONS_DEV, 5 * LANES : 6 * LANES]
+    signs = jnp.where(alive, incidence(aux_own), 0.0)
+    own_signs = signs[EV_DEV : 2 * EV_DEV].astype(jnp.bfloat16)
+    signs = signs.astype(jnp.bfloat16)
+    times = dot_signs(near_block(aux_left, aux_own, aux_right, 0), signs, NN)
+    lags = aux_own[5:8]
     rhs = jnp.where(alive, sample_step * (lags + shift), 0.0) - times
     per_event = dot_signs(rhs, signs, NT)
-    counts = dot_bf16(signs[EV_DEV : 2 * EV_DEV], signs, NT)
+    counts = dot_bf16(own_signs, signs, NT)
     counts = jnp.where(lax.axis_index("x") == 0, counts, 0.0)
     block_ref[...] = rates_ref[...]
     for event in range(EV_DEV):
@@ -338,7 +346,7 @@
     for q in range(4):
         terms = per_event
         if q < 3:
-            terms = terms * near_block(aux_left, aux_own, aux_right, 2 + q)
+            terms = terms * near_block(aux_left, aux_own, aux_right, 1 + q)
         block_ref[:, q * NEAR : (q + 1) * NEAR] = jnp.sum(terms, axis=0, keepdims=True)
     total = jnp.sum(jnp.sum(rhs * rhs, axis=1, keepdims=True), axis=0, keepdims=True)
     block_ref[:, SQUARE_AT : SQUARE_AT + 1] = total
@@ -480,8 +488,9 @@
 
 
 def pack(traces, ray_slowness, travel_time, pair_first, pair_second, pair_lag):
+    tiles = traces.reshape(TRACES_DEV, EV_DEV, CHUNKS, LANES).transpose(0, 2, 1, 3)
     arguments = (
-        traces.reshape(TRACES_DEV, EV_DEV, LENGTH),
+        tiles.reshape(AUX, EV_DEV, LANES),
         ray_slowness,
         travel_time,
         pair_first.reshape(1, PAIR_DEV),
@@ -490,7 +499,7 @@
     )
     return pl.pallas_call(
         pack_kernel,
-        out_shape=pltpu.VMEM((TRACES_DEV + 1, ROWS, LENGTH), jnp.float32),
+        out_shape=pltpu.VMEM((TILES, ROWS, LANES), jnp.float32),
         in_specs=[HBM] * 6,
         out_specs=VMEM,
         scratch_shapes=[

time: 58.7 us -> 58.4 us (level)
  Pallas kernels: 9.98 us -> 8.8 us
  blocking collectives: 42.4 us -> 43.3 us
    all_to_all x2, blocking collectives: 32.4 us -> 33.4 us  [spread(): return lax.all_to_all(copies, axis, 0, 0, tiled=True)]
    pallas_call x1, Pallas kernels: 2.98 us -> 2.32 us  [early(): pl.pallas_call(early_kernel, out_shape=(MOVED, pltpu.SMEM((PLACE_ROWS, PA...]
  transfers between devices with their start and end apart: 1 -> 1, of which waited for: 0 -> 0; matrix products, arithmetic and copies ran while one was open for 0% -> 0% of each run, Pallas kernels for 7% -> 5%
where the time goes in v10:
time: 58.4 us; the launch traced here: 58.2 us
  blocking collectives  43.3 us (74%)
  Pallas kernels  8.8 us (15%)
  starting transfers between devices  4.59 us (8%)
  between operations  1.35 us (2%)
    all_to_all x2, blocking collectives, spread(): return lax.all_to_all(copies, axis, 0, 0, tiled=True)  33.4 us
    all_gather x1, blocking collectives, body(): gathered = lax.all_gather(spread(block, 'g'), 'c', axis=0)  5.11 us
    all_gather x1, blocking collectives, body(): chip = lax.all_gather(message, 'c', axis=0)  4.82 us
    ppermute x1, starting transfers between devices, from_other_chip(): return lax.ppermute(block, ('g', 'c'), route)  4.59 us
    pallas_call x1, Pallas kernels, late(): pl.pallas_call(late_kernel, out_shape=(jax.ShapeDtypeStruct((STATIONS_DEV...  2.79 us
    pallas_call x1, Pallas kernels, early(): pl.pallas_call(early_kernel, out_shape=(MOVED, pltpu.SMEM((PLACE_ROWS, PA...  2.32 us
    pallas_call x1, Pallas kernels, solve(): pl.pallas_call(solve_kernel, out_shape=(jax.ShapeDtypeStruct((4, EV_DEV),...  1.87 us
  transfers between devices with their start and end apart: 1, of which 0 were waited for; matrix products, arithmetic and copies ran while one was open for 0% of the time, Pallas kernels for 5%

profile of v10, /device:TPU:1, one launch (start us, length us, event | category | flops | bytes accessed | tf_op | source)
XLA Modules:
  0.0 58.2 jit_solution(7698583612415684065)
XLA Ops:
  0.6 1.0 %pack.1.own_ref = f32[73,8,128]{2,1,0:T(8,128)S(1)} custom-call(f32[72,8,128]{2,1,0:T(8,128)} %bitcast.12, f32[3,3,8]{2,1,0:T(4,128)} %slowness_ref.1, f32[3,8]{1,0:T(4,128)} %time_ref.1, s32[1,128]{1,0:T(1,128)} %bitcast.13, s32[1,128]{1,0:T(1,128)} %bitcast.14, s32[3,128]{1,0:T(4,128)} %lag_ref.1), custom_call_target="tpu_custom_call" | custom-call | tf_op jit(solution)/shard_map/pack/pallas_call | solution.py:500
  1.7 4.6 %collective-permute-start = (f32[73,8,128]{2,1,0:T(8,128)S(1)}, f32[73,8,128]{2,1,0:T(8,128)S(1)}, u32[]{:S(2)}, u32[]{:S(2)}) collective-permute-start(f32[73,8,128]{2,1,0:T(8,128)S(1)} %pack.1.own_ref), channel_id=1, source_target_pairs={{4,8},{8,4},{12,16},{16,12},{20,24},{24,20},{28,32},{32,28},{36,40... | collective-permute-start | bytes 897032 | tf_op jit(solution)/shard_map/ppermute | solution.py:476
  6.9 0.8 %firsts.1 = (bf16[3,256,640]{2,1,0:T(8,128)(2,1)S(1)}, bf16[3,256,640]{2,1,0:T(8,128)(2,1)S(1)}, s32[16,128]{1,0:T(8,128)S(1)}, f32[128,256]{1,0:T(8,128)S(1)}, f32[1,640]{1,0:T(1,128)S(1)}) custom-call(s32[1]{0:T(128)S(6)} %copy.16.live_ref, f32[73,8,128]{2,1,0:T(8,128)S(1)} %pack.1.own_ref), custom_call_target="tpu_custom_call" | custom-call | tf_op jit(solution)/shard_map/firsts/pallas_call | solution.py:520
  7.7 4.8 %all-gather = f32[146,8,128]{2,1,0:T(8,128)S(1)} all-gather(f32[73,8,128]{2,1,0:T(8,128)S(1)} %pack.1.own_ref), channel_id=2, replica_groups=mesh['g'=64,'c'=2,'x'=4] {'c'}, dimensions={0}, use_global_device_ids=true | all-gather | bytes 897024 | tf_op jit(solution)/shard_map/all_gather | solution.py:598
  12.5 2.3 %early.1 = (f32[9224,128]{1,0:T(8,128)S(1)}, s32[16,128]{1,0:T(8,128)S(4)}, bf16[6,256,640]{2,1,0:T(8,128)(2,1)S(1)}, bf16[6,256,640]{2,1,0:T(8,128)(2,1)S(1)}) custom-call(s32[16,128]{1,0:T(8,128)S(1)} %get-tuple-element.17.listed_ref, f32[2,73,8,128]{3,2,1,0:T(8,128)S(1)} %bitcast.9), custom_call_target="tpu_custom_call" | custom-call | tf_op jit(solution)/shard_map/early/pallas_call | solution.py:543
  14.9 0.0 collective-permute-done.cross_ref
  14.9 2.8 %late.1 = (f32[3,128]{1,0:T(4,128)S(1)}, f32[1,640]{1,0:T(1,128)S(1)}, f32[9224,128]{1,0:T(8,128)S(1)}) custom-call(s32[16,128]{1,0:T(8,128)S(4)} %get-tuple-element.18.places_ref, f32[9224,128]{1,0:T(8,128)S(1)} %get-tuple-element.19.moved_in_ref, f32[2,73,8,128]{3,2,1,0:T(8,128)S(1)} %bitcast.10, ...), custom_call_target="tpu_custom_call", output_to_operand_aliasing={{2}: (1, {})} | custom-call | tf_op jit(solution)/shard_map/late/pallas_call | solution.py:558
  17.7 6.5 %all_to_all.12 = f32[4,1,640]{2,1,0:T(1,128)S(1)} all-to-all(f32[4,1,640]{2,1,0:T(1,128)S(1)} %broadcast_in_dim.4), channel_id=1, replica_groups=mesh['g'=64,'c'=2,'x'=4] {'x'}, dimensions={0} | all-to-all | bytes 20480 | tf_op jit(solution)/shard_map/all_to_all | solution.py:481
  24.3 0.1 broadcast_in_dim.5
  24.4 26.8 %all_to_all.13 = f32[64,1,640]{2,1,0:T(1,128)S(1)} all-to-all(f32[64,1,640]{2,1,0:T(1,128)S(1)} %broadcast_in_dim.5), channel_id=1, replica_groups=mesh['g'=64,'c'=2,'x'=4] {'g'}, dimensions={0} | all-to-all | bytes 327680 | tf_op jit(solution)/shard_map/all_to_all | solution.py:481
  51.2 5.1 %all-gather.1 = f32[128,1,640]{2,0,1:T(8,128)S(1)} all-gather(f32[64,1,640]{2,0,1:T(8,128)S(1)} %copy.13), channel_id=3, replica_groups=mesh['g'=64,'c'=2,'x'=4] {'c'}, dimensions={0}, use_global_device_ids=true | all-gather | bytes 491520 | tf_op jit(solution)/shard_map/all_gather | solution.py:605
  56.3 1.9 %solve.1 = (f32[4,8]{1,0:T(4,128)}, f32[3,128]{1,0:T(4,128)}) custom-call(f32[128,640]{1,0:T(8,128)S(1)} %bitcast.11, f32[3,128]{1,0:T(4,128)S(1)} %get-tuple-element.27.shift_ref), custom_call_target="tpu_custom_call" | custom-call | tf_op jit(solution)/shard_map/solve/pallas_call | solution.py:576
  (4 shorter events, 0.1 us)
Async XLA Ops:
  1.7 13.2 %collective-permute-start = (f32[73,8,128]{2,1,0:T(8,128)S(1)}, f32[73,8,128]{2,1,0:T(8,128)S(1)}, u32[]{:S(2)}, u32[]{:S(2)}) collective-permute-start(f32[73,8,128]{2,1,0:T(8,128)S(1)} %pack.1.own_ref), channel_id=1, source_target_pairs={{4,8},{8,4},{12,16},{16,12},{20,24},{24,20},{28,32},{32,28},{36,40... | collective-permute-start | bytes 897032 | tf_op jit(solution)/shard_map/ppermute | solution.py:476

commit v11 on v10

--- a/solution.py
+++ b/solution.py
@@ -422,43 +422,59 @@
                 for side in range(3):
                     term = counts[a][side] * row
                     sides[side] = term if a == 0 else sides[side] + term
-            mixed = along(*sides)
+            joined = along(*sides)
             for q in range(3):
-                result[q] = result[q] + rates[q] * mixed
-            result[3] = result[3] + mixed
+                result[q] = result[q] + rates[q] * joined
+            result[3] = result[3] + joined
         return result
 
+    def mixed(left, left_scale, right, right_scale):
+        return [left[q] * left_scale + right[q] * right_scale for q in range(4)]
+
+    def residual(square):
+        square = jnp.maximum(square, 0.0)
+        return square, jnp.sqrt(square + eps_small)
+
     rhs_square = total(tables[0][SQUARE_AT : SQUARE_AT + 1])
-    beta = jnp.sqrt(rhs_square + eps_small)
-    unit_square = rhs_square / (beta * beta)
-    adjoint = [value / beta for value in back]
-    alpha = jnp.sqrt(inner(adjoint, adjoint) + eps_small)
-    model = [value / alpha for value in adjoint]
-    search = model
-    location = [jnp.zeros((EV_DEV, LANES), jnp.float32) for _ in range(4)]
-    phi_bar = beta
-    rho_bar = alpha
-    for turn in range(2):
-        normal_model = normal(model)
-        square = inner(model, normal_model) - 2.0 * alpha * inner(model, adjoint)
-        square = jnp.maximum(square + alpha * alpha * unit_square, 0.0)
-        beta = jnp.sqrt(square + eps_small)
-        rho = jnp.sqrt(rho_bar * rho_bar + beta * beta)
-        cosine = rho_bar / rho
-        sine = beta / rho
-        phi = cosine * phi_bar
-        phi_bar = sine * phi_bar
-        step = phi / rho
-        location = [location[q] + step * search[q] for q in range(4)]
-        if turn == 0:
-            unit_square = square / (beta * beta)
-            adjoint = [(normal_model[q] - alpha * adjoint[q]) / beta for q in range(4)]
-            vector = [adjoint[q] - beta * model[q] for q in range(4)]
-            alpha = jnp.sqrt(inner(vector, vector) + eps_small)
-            model = [value / alpha for value in vector]
-            theta = sine * alpha
-            rho_bar = -cosine * alpha
-            search = [model[q] - theta / rho * search[q] for q in range(4)]
+    back_normal = normal(back)
+    back_square = inner(back, back)
+    back_bend = inner(back, back_normal)
+    first_beta = jnp.sqrt(rhs_square + eps_small)
+    from_beta = 1.0 / first_beta
+    adjoint_square = back_square * from_beta * from_beta
+    alpha = jnp.sqrt(adjoint_square + eps_small)
+    scale = from_beta / alpha
+    unit_square = rhs_square * from_beta * from_beta
+    square, beta = residual(
+        back_bend * scale * scale - 2.0 * adjoint_square + alpha * alpha * unit_square
+    )
+    rho = jnp.sqrt(alpha * alpha + beta * beta)
+    cosine = alpha / rho
+    sine = beta / rho
+    step = cosine * first_beta / rho
+    phi_bar = sine * first_beta
+    to_beta = 1.0 / beta
+    adjoint = mixed(back_normal, scale * to_beta, back, -(alpha * from_beta * to_beta))
+    vector = mixed(adjoint, 1.0, back, -(beta * scale))
+    vector_normal = normal(vector)
+    vector_square = inner(vector, vector)
+    vector_bend = inner(vector, vector_normal)
+    vector_adjoint = inner(vector, adjoint)
+    unit_square = square * to_beta * to_beta
+    next_alpha = jnp.sqrt(vector_square + eps_small)
+    to_alpha = 1.0 / next_alpha
+    _, beta = residual(
+        vector_bend * to_alpha * to_alpha
+        - 2.0 * vector_adjoint
+        + next_alpha * next_alpha * unit_square
+    )
+    theta = sine * next_alpha
+    rho_bar = -cosine * next_alpha
+    last_rho = jnp.sqrt(rho_bar * rho_bar + beta * beta)
+    last_step = rho_bar / last_rho * phi_bar / last_rho
+    location = mixed(
+        back, (step - last_step * theta / rho) * scale, vector, last_step * to_alpha
+    )
 
     lanes = lax.broadcasted_iota(jnp.int32, (ROWS, LANES), 1)
     mine = (lanes == device_index()).astype(jnp.float32)

time: 58.4 us -> 58 us (level)
  no operation moved by 1% of the time
where the time goes in v11:
time: 58 us; the launch traced here: 57.7 us
  blocking collectives  43.3 us (75%)
  Pallas kernels  8.32 us (14%)
  starting transfers between devices  4.59 us (8%)
  between operations  1.35 us (2%)
    all_to_all x2, blocking collectives, spread(): return lax.all_to_all(copies, axis, 0, 0, tiled=True)  33.7 us
    all_gather x1, blocking collectives, body(): chip = lax.all_gather(message, 'c', axis=0)  4.82 us
    all_gather x1, blocking collectives, body(): gathered = lax.all_gather(spread(block, 'g'), 'c', axis=0)  4.7 us
    ppermute x1, starting transfers between devices, from_other_chip(): return lax.ppermute(block, ('g', 'c'), route)  4.59 us
    pallas_call x1, Pallas kernels, late(): pl.pallas_call(late_kernel, out_shape=(jax.ShapeDtypeStruct((STATIONS_DEV...  2.78 us
    pallas_call x1, Pallas kernels, early(): pl.pallas_call(early_kernel, out_shape=(MOVED, pltpu.SMEM((PLACE_ROWS, PA...  2.1 us
    pallas_call x1, Pallas kernels, solve(): pl.pallas_call(solve_kernel, out_shape=(jax.ShapeDtypeStruct((4, EV_DEV),...  1.62 us
  transfers between devices with their start and end apart: 1, of which 0 were waited for; matrix products, arithmetic and copies ran while one was open for 0% of the time, Pallas kernels for 5%

profile of v11, /device:TPU:1, one launch (start us, length us, event | category | flops | bytes accessed | tf_op | source)
XLA Modules:
  0.0 57.7 jit_solution(4513558256230944481)
XLA Ops:
  0.6 1.0 %pack.1.own_ref = f32[73,8,128]{2,1,0:T(8,128)S(1)} custom-call(f32[72,8,128]{2,1,0:T(8,128)} %bitcast.12, f32[3,3,8]{2,1,0:T(4,128)} %slowness_ref.1, f32[3,8]{1,0:T(4,128)} %time_ref.1, s32[1,128]{1,0:T(1,128)} %bitcast.13, s32[1,128]{1,0:T(1,128)} %bitcast.14, s32[3,128]{1,0:T(4,128)} %lag_ref.1), custom_call_target="tpu_custom_call" | custom-call | tf_op jit(solution)/shard_map/pack/pallas_call | solution.py:516
  1.7 4.6 %collective-permute-start = (f32[73,8,128]{2,1,0:T(8,128)S(1)}, f32[73,8,128]{2,1,0:T(8,128)S(1)}, u32[]{:S(2)}, u32[]{:S(2)}) collective-permute-start(f32[73,8,128]{2,1,0:T(8,128)S(1)} %pack.1.own_ref), channel_id=1, source_target_pairs={{4,8},{8,4},{12,16},{16,12},{20,24},{24,20},{28,32},{32,28},{36,40... | collective-permute-start | bytes 897032 | tf_op jit(solution)/shard_map/ppermute | solution.py:492
  6.9 0.8 %firsts.1 = (bf16[3,256,640]{2,1,0:T(8,128)(2,1)S(1)}, bf16[3,256,640]{2,1,0:T(8,128)(2,1)S(1)}, s32[16,128]{1,0:T(8,128)S(1)}, f32[128,256]{1,0:T(8,128)S(1)}, f32[1,640]{1,0:T(1,128)S(1)}) custom-call(s32[1]{0:T(128)S(6)} %copy.16.live_ref, f32[73,8,128]{2,1,0:T(8,128)S(1)} %pack.1.own_ref), custom_call_target="tpu_custom_call" | custom-call | tf_op jit(solution)/shard_map/firsts/pallas_call | solution.py:536
  7.7 4.8 %all-gather = f32[146,8,128]{2,1,0:T(8,128)S(1)} all-gather(f32[73,8,128]{2,1,0:T(8,128)S(1)} %pack.1.own_ref), channel_id=2, replica_groups=mesh['g'=64,'c'=2,'x'=4] {'c'}, dimensions={0}, use_global_device_ids=true | all-gather | bytes 897024 | tf_op jit(solution)/shard_map/all_gather | solution.py:614
  12.5 2.1 %early.1 = (f32[9224,128]{1,0:T(8,128)S(1)}, s32[16,128]{1,0:T(8,128)S(4)}, bf16[6,256,640]{2,1,0:T(8,128)(2,1)S(1)}, bf16[6,256,640]{2,1,0:T(8,128)(2,1)S(1)}) custom-call(s32[16,128]{1,0:T(8,128)S(1)} %get-tuple-element.17.listed_ref, f32[2,73,8,128]{3,2,1,0:T(8,128)S(1)} %bitcast.9), custom_call_target="tpu_custom_call" | custom-call | tf_op jit(solution)/shard_map/early/pallas_call | solution.py:559
  14.7 0.0 collective-permute-done.cross_ref
  14.7 2.8 %late.1 = (f32[3,128]{1,0:T(4,128)S(1)}, f32[1,640]{1,0:T(1,128)S(1)}, f32[9224,128]{1,0:T(8,128)S(1)}) custom-call(s32[16,128]{1,0:T(8,128)S(4)} %get-tuple-element.18.places_ref, f32[9224,128]{1,0:T(8,128)S(1)} %get-tuple-element.19.moved_in_ref, f32[2,73,8,128]{3,2,1,0:T(8,128)S(1)} %bitcast.10, ...), custom_call_target="tpu_custom_call", output_to_operand_aliasing={{2}: (1, {})} | custom-call | tf_op jit(solution)/shard_map/late/pallas_call | solution.py:574
  17.5 6.5 %all_to_all.12 = f32[4,1,640]{2,1,0:T(1,128)S(1)} all-to-all(f32[4,1,640]{2,1,0:T(1,128)S(1)} %broadcast_in_dim.4), channel_id=1, replica_groups=mesh['g'=64,'c'=2,'x'=4] {'x'}, dimensions={0} | all-to-all | bytes 20480 | tf_op jit(solution)/shard_map/all_to_all | solution.py:497
  24.0 0.1 broadcast_in_dim.5
  24.1 27.2 %all_to_all.13 = f32[64,1,640]{2,1,0:T(1,128)S(1)} all-to-all(f32[64,1,640]{2,1,0:T(1,128)S(1)} %broadcast_in_dim.5), channel_id=1, replica_groups=mesh['g'=64,'c'=2,'x'=4] {'g'}, dimensions={0} | all-to-all | bytes 327680 | tf_op jit(solution)/shard_map/all_to_all | solution.py:497
  51.4 4.7 %all-gather.1 = f32[128,1,640]{2,0,1:T(8,128)S(1)} all-gather(f32[64,1,640]{2,0,1:T(8,128)S(1)} %copy.13), channel_id=3, replica_groups=mesh['g'=64,'c'=2,'x'=4] {'c'}, dimensions={0}, use_global_device_ids=true | all-gather | bytes 491520 | tf_op jit(solution)/shard_map/all_gather | solution.py:621
  56.1 1.6 %solve.1 = (f32[4,8]{1,0:T(4,128)}, f32[3,128]{1,0:T(4,128)}) custom-call(f32[128,640]{1,0:T(8,128)S(1)} %bitcast.11, f32[3,128]{1,0:T(4,128)S(1)} %get-tuple-element.27.shift_ref), custom_call_target="tpu_custom_call" | custom-call | tf_op jit(solution)/shard_map/solve/pallas_call | solution.py:592
  (4 shorter events, 0.1 us)
Async XLA Ops:
  1.7 13.0 %collective-permute-start = (f32[73,8,128]{2,1,0:T(8,128)S(1)}, f32[73,8,128]{2,1,0:T(8,128)S(1)}, u32[]{:S(2)}, u32[]{:S(2)}) collective-permute-start(f32[73,8,128]{2,1,0:T(8,128)S(1)} %pack.1.own_ref), channel_id=1, source_target_pairs={{4,8},{8,4},{12,16},{16,12},{20,24},{24,20},{28,32},{32,28},{36,40... | collective-permute-start | bytes 897032 | tf_op jit(solution)/shard_map/ppermute | solution.py:492

commit v12 on v11

--- a/solution.py
+++ b/solution.py
@@ -182,6 +182,10 @@
         mine = column == (groups + half * (LANES // LAGS)).astype(jnp.float32)
         pick_ref[:, half * LANES : (half + 1) * LANES] = mine.astype(jnp.float32)
     rates_ref[...] = jnp.zeros((1, PAYLOAD), jnp.float32)
+    counts = pair_counts(aux, alive)
+    for event in range(EV_DEV):
+        at = count_place(event)
+        rates_ref[:, at : at + NEAR] = counts[event : event + 1]
     for station in range(STATIONS_DEV):
         for q in range(3):
             lane = (1 + q) * EV_DEV
@@ -191,6 +195,13 @@
                 rates_ref[:, at : at + EV_DEV] = jnp.where(
                     lax.axis_index("x") == group, own, 0.0
                 )
+
+
+def pair_counts(aux, alive):
+    signs = jnp.where(alive, incidence(aux), 0.0)
+    own_signs = signs[EV_DEV : 2 * EV_DEV].astype(jnp.bfloat16)
+    counts = dot_bf16(own_signs, signs.astype(jnp.bfloat16), NT)
+    return jnp.where(lax.axis_index("x") == 0, counts, 0.0)
 
 
 def fill_table(ref, table_ref, part):
@@ -331,18 +342,12 @@
     shift_ref[...] = shift
 
     signs = jnp.where(alive, incidence(aux_own), 0.0)
-    own_signs = signs[EV_DEV : 2 * EV_DEV].astype(jnp.bfloat16)
     signs = signs.astype(jnp.bfloat16)
     times = dot_signs(near_block(aux_left, aux_own, aux_right, 0), signs, NN)
     lags = aux_own[5:8]
     rhs = jnp.where(alive, sample_step * (lags + shift), 0.0) - times
     per_event = dot_signs(rhs, signs, NT)
-    counts = dot_bf16(own_signs, signs, NT)
-    counts = jnp.where(lax.axis_index("x") == 0, counts, 0.0)
     block_ref[...] = rates_ref[...]
-    for event in range(EV_DEV):
-        at = count_place(event)
-        block_ref[:, at : at + NEAR] = counts[event : event + 1]
     for q in range(4):
         terms = per_event
         if q < 3:

time: 58 us -> 58.1 us (level)
    all_gather x1, blocking collectives: 4.7 us -> 5.33 us  [body(): gathered = lax.all_gather(spread(block, 'g'), 'c', axis=0)]
    all_to_all x2, blocking collectives: 33.7 us -> 33.1 us  [spread(): return lax.all_to_all(copies, axis, 0, 0, tiled=True)]
where the time goes in v12:
time: 58.1 us; the launch traced here: 58.2 us
  blocking collectives  43.3 us (75%)
  Pallas kernels  8.8 us (15%)
  starting transfers between devices  4.59 us (8%)
  between operations  1.35 us (2%)
    all_to_all x2, blocking collectives, spread(): return lax.all_to_all(copies, axis, 0, 0, tiled=True)  33.1 us
    all_gather x1, blocking collectives, body(): gathered = lax.all_gather(spread(block, 'g'), 'c', axis=0)  5.33 us
    all_gather x1, blocking collectives, body(): chip = lax.all_gather(message, 'c', axis=0)  4.82 us
    ppermute x1, starting transfers between devices, from_other_chip(): return lax.ppermute(block, ('g', 'c'), route)  4.59 us
    pallas_call x1, Pallas kernels, late(): pl.pallas_call(late_kernel, out_shape=(jax.ShapeDtypeStruct((STATIONS_DEV...  3.03 us
    pallas_call x1, Pallas kernels, early(): pl.pallas_call(early_kernel, out_shape=(MOVED, pltpu.SMEM((PLACE_ROWS, PA...  2.32 us
    pallas_call x1, Pallas kernels, solve(): pl.pallas_call(solve_kernel, out_shape=(jax.ShapeDtypeStruct((4, EV_DEV),...  1.62 us
  transfers between devices with their start and end apart: 1, of which 0 were waited for; matrix products, arithmetic and copies ran while one was open for 0% of the time, Pallas kernels for 5%

profile of v12, /device:TPU:1, one launch (start us, length us, event | category | flops | bytes accessed | tf_op | source)
XLA Modules:
  0.0 58.2 jit_solution(8458383825663684771)
XLA Ops:
  0.6 1.0 %pack.1.own_ref = f32[73,8,128]{2,1,0:T(8,128)S(1)} custom-call(f32[72,8,128]{2,1,0:T(8,128)} %bitcast.12, f32[3,3,8]{2,1,0:T(4,128)} %slowness_ref.1, f32[3,8]{1,0:T(4,128)} %time_ref.1, s32[1,128]{1,0:T(1,128)} %bitcast.13, s32[1,128]{1,0:T(1,128)} %bitcast.14, s32[3,128]{1,0:T(4,128)} %lag_ref.1), custom_call_target="tpu_custom_call" | custom-call | tf_op jit(solution)/shard_map/pack/pallas_call | solution.py:521
  1.7 4.6 %collective-permute-start = (f32[73,8,128]{2,1,0:T(8,128)S(1)}, f32[73,8,128]{2,1,0:T(8,128)S(1)}, u32[]{:S(2)}, u32[]{:S(2)}) collective-permute-start(f32[73,8,128]{2,1,0:T(8,128)S(1)} %pack.1.own_ref), channel_id=1, source_target_pairs={{4,8},{8,4},{12,16},{16,12},{20,24},{24,20},{28,32},{32,28},{36,40... | collective-permute-start | bytes 897032 | tf_op jit(solution)/shard_map/ppermute | solution.py:497
  6.9 0.8 %firsts.1 = (bf16[3,256,640]{2,1,0:T(8,128)(2,1)S(1)}, bf16[3,256,640]{2,1,0:T(8,128)(2,1)S(1)}, s32[16,128]{1,0:T(8,128)S(1)}, f32[128,256]{1,0:T(8,128)S(1)}, f32[1,640]{1,0:T(1,128)S(1)}) custom-call(s32[1]{0:T(128)S(6)} %copy.16.live_ref, f32[73,8,128]{2,1,0:T(8,128)S(1)} %pack.1.own_ref), custom_call_target="tpu_custom_call" | custom-call | tf_op jit(solution)/shard_map/firsts/pallas_call | solution.py:541
  7.7 4.8 %all-gather = f32[146,8,128]{2,1,0:T(8,128)S(1)} all-gather(f32[73,8,128]{2,1,0:T(8,128)S(1)} %pack.1.own_ref), channel_id=2, replica_groups=mesh['g'=64,'c'=2,'x'=4] {'c'}, dimensions={0}, use_global_device_ids=true | all-gather | bytes 897024 | tf_op jit(solution)/shard_map/all_gather | solution.py:619
  12.6 2.3 %early.1 = (f32[9224,128]{1,0:T(8,128)S(1)}, s32[16,128]{1,0:T(8,128)S(4)}, bf16[6,256,640]{2,1,0:T(8,128)(2,1)S(1)}, bf16[6,256,640]{2,1,0:T(8,128)(2,1)S(1)}) custom-call(s32[16,128]{1,0:T(8,128)S(1)} %get-tuple-element.17.listed_ref, f32[2,73,8,128]{3,2,1,0:T(8,128)S(1)} %bitcast.9), custom_call_target="tpu_custom_call" | custom-call | tf_op jit(solution)/shard_map/early/pallas_call | solution.py:564
  14.9 0.0 collective-permute-done.cross_ref
  14.9 3.0 %late.1 = (f32[3,128]{1,0:T(4,128)S(1)}, f32[1,640]{1,0:T(1,128)S(1)}, f32[9224,128]{1,0:T(8,128)S(1)}) custom-call(s32[16,128]{1,0:T(8,128)S(4)} %get-tuple-element.18.places_ref, f32[9224,128]{1,0:T(8,128)S(1)} %get-tuple-element.19.moved_in_ref, f32[2,73,8,128]{3,2,1,0:T(8,128)S(1)} %bitcast.10, ...), custom_call_target="tpu_custom_call", output_to_operand_aliasing={{2}: (1, {})} | custom-call | tf_op jit(solution)/shard_map/late/pallas_call | solution.py:579
  18.0 6.5 %all_to_all.12 = f32[4,1,640]{2,1,0:T(1,128)S(1)} all-to-all(f32[4,1,640]{2,1,0:T(1,128)S(1)} %broadcast_in_dim.4), channel_id=1, replica_groups=mesh['g'=64,'c'=2,'x'=4] {'x'}, dimensions={0} | all-to-all | bytes 20480 | tf_op jit(solution)/shard_map/all_to_all | solution.py:502
  24.5 0.1 broadcast_in_dim.5
  24.6 26.6 %all_to_all.13 = f32[64,1,640]{2,1,0:T(1,128)S(1)} all-to-all(f32[64,1,640]{2,1,0:T(1,128)S(1)} %broadcast_in_dim.5), channel_id=1, replica_groups=mesh['g'=64,'c'=2,'x'=4] {'g'}, dimensions={0} | all-to-all | bytes 327680 | tf_op jit(solution)/shard_map/all_to_all | solution.py:502
  51.2 5.3 %all-gather.1 = f32[128,1,640]{2,0,1:T(8,128)S(1)} all-gather(f32[64,1,640]{2,0,1:T(8,128)S(1)} %copy.13), channel_id=3, replica_groups=mesh['g'=64,'c'=2,'x'=4] {'c'}, dimensions={0}, use_global_device_ids=true | all-gather | bytes 491520 | tf_op jit(solution)/shard_map/all_gather | solution.py:626
  56.6 1.6 %solve.1 = (f32[4,8]{1,0:T(4,128)}, f32[3,128]{1,0:T(4,128)}) custom-call(f32[128,640]{1,0:T(8,128)S(1)} %bitcast.11, f32[3,128]{1,0:T(4,128)S(1)} %get-tuple-element.27.shift_ref), custom_call_target="tpu_custom_call" | custom-call | tf_op jit(solution)/shard_map/solve/pallas_call | solution.py:597
  (4 shorter events, 0.1 us)
Async XLA Ops:
  1.7 13.2 %collective-permute-start = (f32[73,8,128]{2,1,0:T(8,128)S(1)}, f32[73,8,128]{2,1,0:T(8,128)S(1)}, u32[]{:S(2)}, u32[]{:S(2)}) collective-permute-start(f32[73,8,128]{2,1,0:T(8,128)S(1)} %pack.1.own_ref), channel_id=1, source_target_pairs={{4,8},{8,4},{12,16},{16,12},{20,24},{24,20},{28,32},{32,28},{36,40... | collective-permute-start | bytes 897032 | tf_op jit(solution)/shard_map/ppermute | solution.py:497
